TPU v7x, 32 devices: a whole 2x2x4 slice. The times are simulated.
32 devices in a mesh: fsdp: 2 (over x), context: 4 (over z), tensor: 4 (over y, core).
Axes of the slice: x: 2, y: 2, z: 4, core: 2. Of those that a mesh axis runs over, the one named last changes fastest.
Arguments:
- tokens: bfloat16 [8, 2048, 1024], P('fsdp', 'context'), may hold values from -6 to 6
- cotangent: bfloat16 [8, 2048, 1024], P('fsdp', 'context'), may hold values from -6 to 6
- teacher: bfloat16 [8, 2048, 1024], P('fsdp', 'context'), may hold values from -6 to 6
- valid_mask: int32 [8, 2048], P('fsdp', 'context'), may hold values from 0 to 1, as said below
- segment_ids: int32 [8, 2048], P('fsdp'), may hold values from 0 to 3, as said below
- ln1_gain: bfloat16 [1024], P('fsdp'), may hold values from 0.099609375 to 1.8984375
- ln1_bias: bfloat16 [1024], P('fsdp'), may hold values from -2 to 2
- w_qkv: bfloat16 [3, 1024, 1024], P(None, 'fsdp', 'tensor'), may hold values from -0.1875 to 0.1875
- b_qv: bfloat16 [2, 16, 64], P(None, 'tensor', 'fsdp'), may hold values from -2 to 2
- w_out: bfloat16 [1024, 1024], P('tensor', 'fsdp'), may hold values from -0.75 to 0.75
- b_out: bfloat16 [1024], P('fsdp'), may hold values from -2 to 2
- ln2_gain: bfloat16 [1024], P('fsdp'), may hold values from 0.099609375 to 1.8984375
- ln2_bias: bfloat16 [1024], P('fsdp'), may hold values from -2 to 2
- w_fc1: bfloat16 [1024, 4096], P('fsdp', 'tensor'), may hold values from -0.1875 to 0.1875
- b_fc1: bfloat16 [16, 256], P('tensor', 'fsdp'), may hold values from -2 to 2
- w_fc2: bfloat16 [4096, 1024], P('tensor', 'fsdp'), may hold values from -0.09375 to 0.09375
- b_fc2: bfloat16 [1024], P('fsdp'), may hold values from -2 to 2
Outputs:
- output: bfloat16 [8, 2048, 1024], P('fsdp', 'context')
- loss: float32 [], replicated
- input_grad: bfloat16 [8, 2048, 1024], P('fsdp', 'context')
- grad_ln1_gain: float32 [1024], P('fsdp')
- grad_ln1_bias: float32 [1024], P('fsdp')
- grad_w_qkv: float32 [3, 1024, 1024], P(None, 'fsdp', 'tensor')
- grad_b_qv: float32 [2, 16, 64], P(None, 'tensor', 'fsdp')
- grad_w_out: float32 [1024, 1024], P('tensor', 'fsdp')
- grad_b_out: float32 [1024], P('fsdp')
- grad_ln2_gain: float32 [1024], P('fsdp')
- grad_ln2_bias: float32 [1024], P('fsdp')
- grad_w_fc1: float32 [1024, 4096], P('fsdp', 'tensor')
- grad_b_fc1: float32 [16, 256], P('tensor', 'fsdp')
- grad_w_fc2: float32 [4096, 1024], P('tensor', 'fsdp')
- grad_b_fc2: float32 [1024], P('fsdp')
Inputs may be any that keep to these rules, and one draw needn't show every extreme that they name: `valid_mask`: the first token of every sequence is valid. `segment_ids`: never falls along a sequence. Among the 4 sequences of one index of fsdp exactly one is a single document.
All inputs are finite; a program needn't handle non-finite values.
Results may differ from a plain program's by a relative error of at most 0.015.
Values may be sent and summed in bfloat16 or wider, within the bound.
A program may use at most 256 MiB of HBM per device.

v0:
```python
import math

import jax
import jax.numpy as jnp
from jax import lax
from jax.sharding import PartitionSpec as P

D = 1024
HD = 64
WINDOW = 1024


EPSILON = 1e-05
MASKED = -1e30


def passed_along(block, axis, distance):
    devices = range(lax.axis_size(axis))
    route = [(i - distance, i) for i in devices if i - distance in devices]
    return lax.ppermute(block, axis, route)


def norm_rows(values, gain, shift):
    center = values - jnp.mean(values, axis=-1, keepdims=True)
    spread = jnp.mean(center * center, axis=-1, keepdims=True)
    return center * lax.rsqrt(spread + EPSILON) * gain + shift


def gelu_tanh(values):
    return (
        0.5
        * values
        * (1.0 + jnp.tanh(0.7978845608028654 * (values + 0.044715 * values * values * values)))
    )


def masked_scores(query_one, keys_one, allowed_one, scale):
    scores = (
        jnp.einsum("qhe,khe->hqk", query_one, keys_one, preferred_element_type=jnp.float32) * scale
    )
    return jnp.where(allowed_one[None], scores, MASKED)


def row_total(term):
    return lax.psum(term.astype(jnp.bfloat16), "tensor").astype(jnp.float32)


def local(
    tokens,
    cotangent,
    teacher,
    valid_mask,
    segment_ids,
    ln1_gain,
    ln1_bias,
    w_qkv,
    b_qv,
    w_out,
    b_out,
    ln2_gain,
    ln2_bias,
    w_fc1,
    b_fc1,
    w_fc2,
    b_fc2,
):
    (
        gain_one,
        bias_one,
        weight_qkv,
        bias_qv,
        weight_out,
        bias_out,
        gain_two,
        bias_two,
        weight_up,
        bias_up,
        weight_down,
        bias_down,
    ) = (
        lax.all_gather(ln1_gain, "fsdp", axis=0, tiled=True),
        lax.all_gather(ln1_bias, "fsdp", axis=0, tiled=True),
        lax.all_gather(w_qkv, "fsdp", axis=1, tiled=True),
        lax.all_gather(b_qv, "fsdp", axis=2, tiled=True),
        lax.all_gather(w_out, "fsdp", axis=1, tiled=True),
        lax.all_gather(b_out, "fsdp", axis=0, tiled=True),
        lax.all_gather(ln2_gain, "fsdp", axis=0, tiled=True),
        lax.all_gather(ln2_bias, "fsdp", axis=0, tiled=True),
        lax.all_gather(w_fc1, "fsdp", axis=0, tiled=True),
        lax.all_gather(b_fc1, "fsdp", axis=1, tiled=True),
        lax.all_gather(w_fc2, "fsdp", axis=1, tiled=True),
        lax.all_gather(b_fc2, "fsdp", axis=0, tiled=True),
    )
    seqs, group, width = tokens.shape
    rows = seqs * group
    local_width = weight_qkv.shape[2]
    heads_here = local_width // HD
    scale = 1.0 / math.sqrt(HD)
    gain_one = gain_one.astype(jnp.float32)
    bias_one = bias_one.astype(jnp.float32)
    gain_two = gain_two.astype(jnp.float32)
    bias_two = bias_two.astype(jnp.float32)
    bias_out = bias_out.astype(jnp.float32)
    bias_down = bias_down.astype(jnp.float32)
    bias_up = bias_up.astype(jnp.float32).reshape(-1)
    qv_bias = bias_qv.astype(jnp.float32).reshape(2, local_width)
    resid_in = tokens.astype(jnp.float32).reshape(rows, width)
    normed_one = norm_rows(resid_in, gain_one, bias_one).astype(jnp.bfloat16)
    projected = jnp.einsum(
        "rd,tde->tre", normed_one, weight_qkv, preferred_element_type=jnp.float32
    )
    query = (projected[0] + qv_bias[0]).astype(jnp.bfloat16).reshape(seqs, group, heads_here, HD)
    key_proj = projected[1].astype(jnp.bfloat16).reshape(seqs, group, heads_here, HD)
    value_proj = (
        (projected[2] + qv_bias[1]).astype(jnp.bfloat16).reshape(seqs, group, heads_here, HD)
    )
    near_keys, near_values = passed_along((key_proj, value_proj), "context", 1)
    far_keys, far_values = passed_along((key_proj, value_proj), "context", 2)
    keys_all = jnp.concatenate([far_keys, near_keys, key_proj], axis=1)
    values_all = jnp.concatenate([far_values, near_values, value_proj], axis=1)
    place = lax.axis_index("context")
    query_pos = place * group + jnp.arange(group, dtype=jnp.int32)
    key_pos = (place - 2) * group + jnp.arange(3 * group, dtype=jnp.int32)
    padded_seg = jnp.concatenate([jnp.full((seqs, 2 * group), -1, jnp.int32), segment_ids], axis=1)
    key_seg = lax.dynamic_slice_in_dim(padded_seg, place * group, 3 * group, 1)
    query_seg = lax.dynamic_slice_in_dim(segment_ids, place * group, group, 1)
    distance = query_pos[:, None] - key_pos[None, :]
    allowed = ((distance >= 0) & (distance < WINDOW))[None] & (
        query_seg[:, :, None] == key_seg[:, None, :]
    )

    def attend_one(items):
        query_one, keys_one, values_one, allowed_one = items
        scores = masked_scores(query_one, keys_one, allowed_one, scale)
        top = jnp.max(scores, axis=-1, keepdims=True)
        weights = jnp.exp(scores - top)
        total = jnp.sum(weights, axis=-1, keepdims=True)
        probs = (weights / total).astype(jnp.bfloat16)
        mixed = jnp.einsum("hqk,khe->qhe", probs, values_one, preferred_element_type=jnp.float32)
        return (mixed, top + jnp.log(total))

    mixed, log_total = lax.map(attend_one, (query, keys_all, values_all, allowed))
    attended = mixed.reshape(rows, local_width).astype(jnp.bfloat16)
    attn_term = jnp.dot(attended, weight_out, preferred_element_type=jnp.float32)
    mask_rows = valid_mask.reshape(rows).astype(jnp.float32)
    teacher_rows = teacher.astype(jnp.float32).reshape(rows, width)
    cot_rows = cotangent.astype(jnp.float32).reshape(rows, width)
    middle = resid_in + row_total(attn_term) + bias_out
    normed_two = norm_rows(middle, gain_two, bias_two).astype(jnp.bfloat16)
    hidden = jnp.dot(normed_two, weight_up, preferred_element_type=jnp.float32) + bias_up
    activated = gelu_tanh(hidden).astype(jnp.bfloat16)
    down_term = jnp.dot(activated, weight_down, preferred_element_type=jnp.float32)
    block = middle + row_total(down_term) + bias_down
    difference = block - teacher_rows
    count, error_sum = lax.psum(
        (jnp.sum(mask_rows), jnp.sum(mask_rows * jnp.sum(difference * difference, axis=-1))),
        ("fsdp", "context"),
    )
    tokens_all = rows * lax.axis_size("fsdp") * lax.axis_size("context")
    grad_block = cot_rows + tokens_all / count * mask_rows[:, None] * difference
    loss = error_sum / (2.0 * D * count)
    grad_down = grad_block.astype(jnp.bfloat16)
    grad_b_fc2 = jnp.sum(grad_block, axis=0)
    grad_w_fc2 = jnp.einsum("rf,rd->fd", activated, grad_down, preferred_element_type=jnp.float32)
    grad_act = jnp.einsum("rd,fd->rf", grad_down, weight_down, preferred_element_type=jnp.float32)
    _, gelu_pull = jax.vjp(gelu_tanh, hidden)
    grad_hidden = gelu_pull(grad_act)[0].astype(jnp.bfloat16)
    grad_w_fc1 = jnp.einsum(
        "rd,rf->df", normed_two, grad_hidden, preferred_element_type=jnp.float32
    )
    grad_b_fc1 = jnp.sum(grad_hidden, axis=0, dtype=jnp.float32).reshape(b_fc1.shape[0], -1)
    normed_term = jnp.einsum(
        "rf,df->rd", grad_hidden, weight_up, preferred_element_type=jnp.float32
    )
    _, second_pull = jax.vjp(norm_rows, middle, gain_two, bias_two)
    grad_mid_norm, grad_ln2_gain, grad_ln2_bias = second_pull(row_total(normed_term))
    grad_middle = grad_block + grad_mid_norm
    grad_mix = grad_middle.astype(jnp.bfloat16)
    grad_b_out = jnp.sum(grad_middle, axis=0)
    grad_w_out = jnp.einsum("re,rd->ed", attended, grad_mix, preferred_element_type=jnp.float32)
    grad_attended = jnp.einsum(
        "rd,ed->re", grad_mix, weight_out, preferred_element_type=jnp.float32
    )
    grad_attended = grad_attended.astype(jnp.bfloat16).reshape(seqs, group, heads_here, HD)

    def attend_back(items):
        query_one, keys_one, values_one, allowed_one, log_one, grad_one = items
        scores = masked_scores(query_one, keys_one, allowed_one, scale)
        probs = jnp.exp(scores - log_one)
        dprobs = jnp.einsum(
            "qhe,khe->hqk", grad_one, values_one, preferred_element_type=jnp.float32
        )
        weighted = jnp.sum(probs * dprobs, axis=-1, keepdims=True)
        grad_scores = (probs * (dprobs - weighted)).astype(jnp.bfloat16)
        grad_query = (
            jnp.einsum("hqk,khe->qhe", grad_scores, keys_one, preferred_element_type=jnp.float32)
            * scale
        )
        grad_key = (
            jnp.einsum("hqk,qhe->khe", grad_scores, query_one, preferred_element_type=jnp.float32)
            * scale
        )
        grad_value = jnp.einsum(
            "hqk,qhe->khe", probs.astype(jnp.bfloat16), grad_one, preferred_element_type=jnp.float32
        )
        return (grad_query, grad_key, grad_value)

    grad_query, grad_keys_all, grad_values_all = lax.map(
        attend_back, (query, keys_all, values_all, allowed, log_total, grad_attended)
    )
    from_near = (
        passed_along(
            grad_keys_all[:, group : 2 * group].astype(jnp.bfloat16), "context", -1
        ).astype(jnp.float32),
        passed_along(
            grad_values_all[:, group : 2 * group].astype(jnp.bfloat16), "context", -1
        ).astype(jnp.float32),
    )
    from_far = (
        passed_along(grad_keys_all[:, :group].astype(jnp.bfloat16), "context", -2).astype(
            jnp.float32
        ),
        passed_along(grad_values_all[:, :group].astype(jnp.bfloat16), "context", -2).astype(
            jnp.float32
        ),
    )
    grad_key = (grad_keys_all[:, 2 * group :] + from_near[0] + from_far[0]).astype(jnp.bfloat16)
    grad_value = (grad_values_all[:, 2 * group :] + from_near[1] + from_far[1]).astype(jnp.bfloat16)
    grad_query = grad_query.astype(jnp.bfloat16)
    grad_proj = jnp.stack(
        [
            grad_query.reshape(rows, local_width),
            grad_key.reshape(rows, local_width),
            grad_value.reshape(rows, local_width),
        ]
    )
    grad_w_qkv = jnp.einsum(
        "rd,tre->tde", normed_one, grad_proj, preferred_element_type=jnp.float32
    )
    grad_b_qv = jnp.stack(
        [
            jnp.sum(grad_proj[0], axis=0, dtype=jnp.float32),
            jnp.sum(grad_proj[2], axis=0, dtype=jnp.float32),
        ]
    ).reshape(2, heads_here, HD)
    first_term = jnp.einsum(
        "tre,tde->rd", grad_proj, weight_qkv, preferred_element_type=jnp.float32
    )
    _, first_pull = jax.vjp(norm_rows, resid_in, gain_one, bias_one)
    grad_in_norm, grad_ln1_gain, grad_ln1_bias = first_pull(row_total(first_term))
    input_grad = (grad_middle + grad_in_norm).astype(jnp.bfloat16).reshape(seqs, group, width)
    gradients = (
        grad_ln1_gain,
        grad_ln1_bias,
        grad_w_qkv,
        grad_b_qv,
        grad_w_out,
        grad_b_out,
        grad_ln2_gain,
        grad_ln2_bias,
        grad_w_fc1,
        grad_b_fc1,
        grad_w_fc2,
        grad_b_fc2,
    )
    owned = (
        lax.psum_scatter(
            gradients[0].astype(jnp.bfloat16), "fsdp", scatter_dimension=0, tiled=True
        ).astype(jnp.float32),
        lax.psum_scatter(
            gradients[1].astype(jnp.bfloat16), "fsdp", scatter_dimension=0, tiled=True
        ).astype(jnp.float32),
        lax.psum_scatter(
            gradients[2].astype(jnp.bfloat16), "fsdp", scatter_dimension=1, tiled=True
        ).astype(jnp.float32),
        lax.psum_scatter(
            gradients[3].astype(jnp.bfloat16), "fsdp", scatter_dimension=2, tiled=True
        ).astype(jnp.float32),
        lax.psum_scatter(
            gradients[4].astype(jnp.bfloat16), "fsdp", scatter_dimension=1, tiled=True
        ).astype(jnp.float32),
        lax.psum_scatter(
            gradients[5].astype(jnp.bfloat16), "fsdp", scatter_dimension=0, tiled=True
        ).astype(jnp.float32),
        lax.psum_scatter(
            gradients[6].astype(jnp.bfloat16), "fsdp", scatter_dimension=0, tiled=True
        ).astype(jnp.float32),
        lax.psum_scatter(
            gradients[7].astype(jnp.bfloat16), "fsdp", scatter_dimension=0, tiled=True
        ).astype(jnp.float32),
        lax.psum_scatter(
            gradients[8].astype(jnp.bfloat16), "fsdp", scatter_dimension=0, tiled=True
        ).astype(jnp.float32),
        lax.psum_scatter(
            gradients[9].astype(jnp.bfloat16), "fsdp", scatter_dimension=1, tiled=True
        ).astype(jnp.float32),
        lax.psum_scatter(
            gradients[10].astype(jnp.bfloat16), "fsdp", scatter_dimension=1, tiled=True
        ).astype(jnp.float32),
        lax.psum_scatter(
            gradients[11].astype(jnp.bfloat16), "fsdp", scatter_dimension=0, tiled=True
        ).astype(jnp.float32),
    )
    owned = (
        lax.psum(owned[0].astype(jnp.bfloat16), "context").astype(jnp.float32),
        lax.psum(owned[1].astype(jnp.bfloat16), "context").astype(jnp.float32),
        lax.psum(owned[2].astype(jnp.bfloat16), "context").astype(jnp.float32),
        lax.psum(owned[3].astype(jnp.bfloat16), "context").astype(jnp.float32),
        lax.psum(owned[4].astype(jnp.bfloat16), "context").astype(jnp.float32),
        lax.psum(owned[5].astype(jnp.bfloat16), "context").astype(jnp.float32),
        lax.psum(owned[6].astype(jnp.bfloat16), "context").astype(jnp.float32),
        lax.psum(owned[7].astype(jnp.bfloat16), "context").astype(jnp.float32),
        lax.psum(owned[8].astype(jnp.bfloat16), "context").astype(jnp.float32),
        lax.psum(owned[9].astype(jnp.bfloat16), "context").astype(jnp.float32),
        lax.psum(owned[10].astype(jnp.bfloat16), "context").astype(jnp.float32),
        lax.psum(owned[11].astype(jnp.bfloat16), "context").astype(jnp.float32),
    )
    output = block.astype(jnp.bfloat16).reshape(seqs, group, width)
    return (
        output,
        loss,
        input_grad,
        owned[0],
        owned[1],
        owned[2],
        owned[3],
        owned[4],
        owned[5],
        owned[6],
        owned[7],
        owned[8],
        owned[9],
        owned[10],
        owned[11],
    )


def solution(mesh):
    return jax.shard_map(
        local,
        mesh=mesh,
        in_specs=(
            P("fsdp", "context", None),
            P("fsdp", "context", None),
            P("fsdp", "context", None),
            P("fsdp", "context"),
            P("fsdp", None),
            P("fsdp"),
            P("fsdp"),
            P(None, "fsdp", "tensor"),
            P(None, "tensor", "fsdp"),
            P("tensor", "fsdp"),
            P("fsdp"),
            P("fsdp"),
            P("fsdp"),
            P("fsdp", "tensor"),
            P("tensor", "fsdp"),
            P("tensor", "fsdp"),
            P("fsdp"),
        ),
        out_specs=(
            P("fsdp", "context", None),
            P(),
            P("fsdp", "context", None),
            P("fsdp"),
            P("fsdp"),
            P(None, "fsdp", "tensor"),
            P(None, "tensor", "fsdp"),
            P("tensor", "fsdp"),
            P("fsdp"),
            P("fsdp"),
            P("fsdp"),
            P("fsdp", "tensor"),
            P("tensor", "fsdp"),
            P("tensor", "fsdp"),
            P("fsdp"),
        ),
        check_vma=False,
    )
```

profile of v0, /device:TPU:0, one launch (start us, length us, event | category | flops | bytes accessed | tf_op | source)
XLA Modules:
  0.0 1281.6 jit_solution(8862314856494309212)
XLA Ops:
  103.9 18.7 %collective-permute-done.1 = bf16[4,512,4,64]{1,0,3,2:T(4,128)(2,1)} collective-permute-done((bf16[4,512,4,64]{1,0,3,2:T(4,128)(2,1)}, bf16[4,512,4,64]{1,0,3,2:T(4,128)(2,1)}, u32[]{:S(2)}, u32[]{:S(2)}) %collective-permute-start.1) | collective-permute-done | bytes 1048608 | tf_op jit(solution)/shard_map/ppermute | solution.py:20
  122.6 21.4 %collective-permute-done = bf16[4,512,4,64]{1,0,3,2:T(4,128)(2,1)} collective-permute-done((bf16[4,512,4,64]{1,0,3,2:T(4,128)(2,1)}, bf16[4,512,4,64]{1,0,3,2:T(4,128)(2,1)}, u32[]{:S(2)}, u32[]{:S(2)}) %collective-permute-start) | collective-permute-done | bytes 1048608 | tf_op jit(solution)/shard_map/ppermute | solution.py:20
  150.8 56.6 %while.26 = (s32[]{:T(128)}, bf16[4,512,4,64]{1,3,2,0:T(8,128)(2,1)}, f32[4,4,512,1]{2,1,3,0:T(4,128)S(1)}, bf16[4,1536,4,64]{1,3,2,0:T(8,128)(2,1)}, pred[4,512...) while((s32[]{:T(128)}, ...), condition=%wide.region_5.6_spmd, body=%wide.region_2.5_spmd.sunk | while | flops 843053056 | bytes 52496540 | solution.py:142
  233.8 112.7 %all-reduce.16.cloned.1.call-done = bf16[2048,1024]{1,0:T(8,128)(2,1)} async-done(((bf16[2048,1024]{1,0:T(8,128)(2,1)}), bf16[2048,1024]{1,0:T(8,128)(2,1)}) %all-reduce.16.cloned.1.call-update) | async-done | bytes 4194320 | tf_op jit(solution)/shard_map/psum | solution.py:45
  357.3 24.2 %all-gather.12.cloned.1.call-done = bf16[1024,1024]{1,0:T(8,128)(2,1)} async-done(((bf16[512,1024]{1,0:T(8,128)(2,1)}), bf16[1024,1024]{1,0:T(8,128)(2,1)}) %all-gather.12.cloned.1.call-update) | async-done | bytes 2097168 | tf_op jit(solution)/shard_map/all_gather | solution.py:89
  381.5 11.8 fusion.106
  393.3 22.8 %all-gather.14.cloned.1.call-done = bf16[1024,1024]{1,0:T(8,128)(2,1)} async-done(((bf16[1024,512]{1,0:T(8,128)(2,1)}), bf16[1024,1024]{1,0:T(8,128)(2,1)}) %all-gather.14.cloned.1.call-update) | async-done | bytes 2097168 | tf_op jit(solution)/shard_map/all_gather | solution.py:91
  428.6 21.1 %psum.129 = f32[]{:T(128)} all-reduce(f32[]{:T(128)} %convert_reduce_fusion.1), channel_id=1, replica_groups=mesh['fsdp'=2,'context'=4,'tensor'=4] {'fsdp','context'}, use_global_device_ids=true, to_apply=%region_14.15 | all-reduce | flops 1 | bytes 8 | tf_op jit(solution)/shard_map/psum | solution.py:155
  454.8 58.8 %all-reduce.18.cloned.1.call-done = bf16[2048,1024]{1,0:T(8,128)(2,1)} async-done(((bf16[2048,1024]{1,0:T(8,128)(2,1)}), bf16[2048,1024]{1,0:T(8,128)(2,1)}) %all-reduce.18.cloned.1.call-update) | async-done | bytes 4194320 | tf_op jit(solution)/shard_map/psum | solution.py:45
  524.2 15.4 %fusion.115 = (bf16[1024]{0:T(1024)(128)(2,1)}, bf16[2048,1024]{1,0:T(8,128)(2,1)S(1)}) fusion(bf16[1024,1024]{1,0:T(8,128)(2,1)S(1)} %copy-done.52, f32[2048,1024]{1,0:T(8,128)S(1)} %get-tuple-element.261, f32[2048,1024]{1,0:T(8,128)} %fusion.106, f32[1024]{0:T(1024)S(1)} %bitcast.270), kind=kOutput, calls=%fused_computation.169 | convolution fusion | flops 4351589376 | bytes 23074816 | tf_op jit(solution)/shard_map/rd,fd->rf/dot_general | solution.py:165
  547.9 85.7 %all-reduce.20.cloned.1.call-done = bf16[2048,1024]{1,0:T(8,128)(2,1)} async-done(((bf16[2048,1024]{1,0:T(8,128)(2,1)}), bf16[2048,1024]{1,0:T(8,128)(2,1)}) %all-reduce.20.cloned.1.call-update) | async-done | bytes 4194320 | tf_op jit(solution)/shard_map/psum | solution.py:45
  667.8 101.5 %while.27 = (s32[]{:T(128)}, bf16[4,512,4,64]{1,3,2,0:T(8,128)(2,1)}, f32[4,1536,4,64]{1,3,2,0:T(8,128)}, f32[4,1536,4,64]{1,3,2,0:T(8,128)}, bf16[4,1536,4,64]{...) while((s32[]{:T(128)}, ...), condition=%wide.region_20.21_spmd, body=%wide.region_18.20_spmd.sunk | while | flops 2042099712 | bytes 162575632 | solution.py:208
  786.9 16.6 %collective-permute-done.6 = bf16[4,512,4,64]{1,3,2,0:T(8,128)(2,1)} collective-permute-done((bf16[4,512,4,64]{1,3,2,0:T(8,128)(2,1)}, bf16[4,512,4,64]{1,3,2,0:T(8,128)(2,1)}, u32[]{:S(2)}, u32[]{:S(2)}) %collective-permute-start.6) | collective-permute-done | bytes 1048608 | tf_op jit(solution)/shard_map/ppermute | solution.py:20
  803.5 67.4 %collective-permute-done.7 = bf16[4,512,4,64]{1,3,2,0:T(8,128)(2,1)} collective-permute-done((bf16[4,512,4,64]{1,3,2,0:T(8,128)(2,1)}, bf16[4,512,4,64]{1,3,2,0:T(8,128)(2,1)}, u32[]{:S(2)}, u32[]{:S(2)}) %collective-permute-start.7) | collective-permute-done | bytes 1048608 | tf_op jit(solution)/shard_map/ppermute | solution.py:20
  874.7 39.9 %collective-permute-done.5 = bf16[4,512,4,64]{1,3,2,0:T(8,128)(2,1)} collective-permute-done((bf16[4,512,4,64]{1,3,2,0:T(8,128)(2,1)}, bf16[4,512,4,64]{1,3,2,0:T(8,128)(2,1)}, u32[]{:S(2)}, u32[]{:S(2)}) %collective-permute-start.5) | collective-permute-done | bytes 1048608 | tf_op jit(solution)/shard_map/ppermute | solution.py:20
  943.1 13.2 %fusion.90 = bf16[1024,1024]{1,0:T(8,128)(2,1)} fusion(f32[2048,1024]{1,0:T(8,128)} %copy-done.7, f32[2048,1024]{1,0:T(8,128)} %fusion.106, f32[1024]{0:T(1024)S(1)} %bitcast.271), kind=kOutput, calls=%fused_computation.132 | convolution fusion | flops 4319084544 | bytes 18878464 | tf_op jit(solution)/shard_map/rf,rd->fd/dot_general | solution.py:164
  981.4 40.8 %all-reduce.22.cloned.1.call-done = bf16[2048,1024]{1,0:T(8,128)(2,1)} async-done(((bf16[2048,1024]{1,0:T(8,128)(2,1)}), bf16[2048,1024]{1,0:T(8,128)(2,1)}) %all-reduce.22.cloned.1.call-update) | async-done | bytes 4194320 | tf_op jit(solution)/shard_map/psum | solution.py:45
  1026.7 12.9 %reduce-scatter.13.cloned.1.call-done = bf16[256,512]{1,0:T(8,128)(2,1)} async-done(((bf16[256,1024]{1,0:T(8,128)(2,1)}), bf16[256,512]{1,0:T(8,128)(2,1)}) %reduce-scatter.13.cloned.1.call-update) | async-done | bytes 262160 | tf_op jit(solution)/shard_map/reduce_scatter | solution.py:279
  1039.6 34.8 %reduce-scatter.17.cloned.1.call-done = bf16[1024,512]{1,0:T(8,128)(2,1)} async-done(((bf16[1024,1024]{1,0:T(8,128)(2,1)}), bf16[1024,512]{1,0:T(8,128)(2,1)}) %reduce-scatter.17.cloned.1.call-update) | async-done | bytes 1048592 | tf_op jit(solution)/shard_map/reduce_scatter | solution.py:297
  1074.3 34.6 %reduce-scatter.15.cloned.1.call-done = bf16[512,1024]{1,0:T(8,128)(2,1)} async-done(((bf16[1024,1024]{1,0:T(8,128)(2,1)}), bf16[512,1024]{1,0:T(8,128)(2,1)}) %reduce-scatter.15.cloned.1.call-update) | async-done | bytes 1048592 | tf_op jit(solution)/shard_map/reduce_scatter | solution.py:291
  1108.9 29.0 %reduce-scatter.11.cloned.1.call-done = bf16[3,512,256]{1,2,0:T(8,128)(2,1)} async-done(((bf16[3,1024,256]{1,2,0:T(8,128)(2,1)}), bf16[3,512,256]{1,2,0:T(8,128)(2,1)}) %reduce-scatter.11.cloned.1.call-update) | async-done | bytes 786448 | tf_op jit(solution)/shard_map/reduce_scatter | solution.py:273
  1138.0 13.2 %fusion.55 = (bf16[1024]{0:T(1024)(128)(2,1)S(1)}, f32[2048]{0:T(1024)S(1)}, f32[2048]{0:T(1024)S(1)}, bf16[2048,1024]{1,0:T(8,128)(2,1)}) fusion(bf16[2048,1024]{1,0:T(8,128)(2,1)} %all-reduce.22.cloned.1.call-done, bf16[4,512,1024]{2,1,0:T(8,128)(2,1)} %param.21, f32[2048]{0:T(1024)S(1)} %copy-done.21, f32[2048]{0:T(1024)S(1)} %bitcast.240, ...), kind=kLoop, calls=%fused_computation.74 | loop fusion | flops 48229376 | bytes 25221120 | tf_op jit(solution)/shard_map/transpose(jvp())/reduce_sum | solution.py:26
  1151.9 22.3 %psum.128 = f32[]{:T(128)} all-reduce(f32[]{:T(128)} %multiply_reduce_fusion.3), channel_id=1, replica_groups=mesh['fsdp'=2,'context'=4,'tensor'=4] {'fsdp','context'}, use_global_device_ids=true, to_apply=%region_12.13 | all-reduce | flops 1 | bytes 8 | tf_op jit(solution)/shard_map/psum | solution.py:155
  1209.7 54.1 %all-reduce.24.cloned.1.call-done = (bf16[3,512,256]{1,2,0:T(8,128)(2,1)}, bf16[256,512]{1,0:T(8,128)(2,1)}, bf16[512,1024]{1,0:T(8,128)(2,1)}, bf16[1024,512]{1,0:T(8,128)(2,1)}) async-done(((bf16[3,512,256]{1,2,0:T(8,128)(2,1)}, bf16[256,512]{1,0:T(8,128)(2,1)}, bf16[512,1024]{1,0:T(8,128)(2,1)}, bf16[1024,512]{1,0:T(8,128)(2,1)}), (bf16[3,512,256]{1,2,0:T(8,128)(2,1)}, bf16[256,512]{1,0:T(8,128)(2,1)}, ...) | async-done | bytes 3145744 | tf_op jit(solution)/shard_map/psum | solution.py:307
  (396 shorter events, 491.0 us)
Async XLA Ops:
  7.2 32.7 %all-gather.10.cloned.1.call-start = ((), (), s32[]{:S(2)}) async-start(), calls=%async_computation.6 | async-start | bytes 2359296 | tf_op jit(solution)/shard_map/all_gather | solution.py:83
  7.9 338.6 %all-reduce.16.cloned.1.call-start = ((), (), s32[]{:S(2)}) async-start(), calls=%async_computation.7 | async-start | bytes 8388608 | tf_op jit(solution)/shard_map/psum | solution.py:45
  50.6 39.7 %collective-permute-start.3 = (bf16[4,512,4,64]{1,0,3,2:T(4,128)(2,1)S(1)}, bf16[4,512,4,64]{1,0,3,2:T(4,128)(2,1)}, u32[]{:S(2)}, u32[]{:S(2)}) collective-permute-start(bf16[4,512,4,64]{1,0,3,2:T(4,128)(2,1)S(1)} %convert_element_type.251), channel_id=1, source_target_pairs={{0,4},{4,8},{8,12},{1,5},{5,9},{9,13},{2,6},{6,10},{10,14},{3,7},{... | collective-permute-start | bytes 3145736 | tf_op jit(solution)/shard_map/ppermute | solution.py:20
  55.0 45.0 %collective-permute-start.2 = (bf16[4,512,4,64]{1,0,3,2:T(4,128)(2,1)S(1)}, bf16[4,512,4,64]{1,0,3,2:T(4,128)(2,1)}, u32[]{:S(2)}, u32[]{:S(2)}) collective-permute-start(bf16[4,512,4,64]{1,0,3,2:T(4,128)(2,1)S(1)} %convert_element_type.251), channel_id=1, source_target_pairs={{0,8},{4,12},{1,9},{5,13},{2,10},{6,14},{3,11},{7,15},{16,24},{20,... | collective-permute-start | bytes 3145736 | tf_op jit(solution)/shard_map/ppermute | solution.py:20
  65.2 57.4 %collective-permute-start.1 = (bf16[4,512,4,64]{1,0,3,2:T(4,128)(2,1)}, bf16[4,512,4,64]{1,0,3,2:T(4,128)(2,1)}, u32[]{:S(2)}, u32[]{:S(2)}) collective-permute-start(bf16[4,512,4,64]{1,0,3,2:T(4,128)(2,1)} %add_convert_fusion.5), channel_id=1, source_target_pairs={{0,4},{4,8},{8,12},{1,5},{5,9},{9,13},{2,6},{6,10},{10,14},{3,7},{... | collective-permute-start | bytes 3145736 | tf_op jit(solution)/shard_map/ppermute | solution.py:20
  67.4 76.5 %collective-permute-start = (bf16[4,512,4,64]{1,0,3,2:T(4,128)(2,1)}, bf16[4,512,4,64]{1,0,3,2:T(4,128)(2,1)}, u32[]{:S(2)}, u32[]{:S(2)}) collective-permute-start(bf16[4,512,4,64]{1,0,3,2:T(4,128)(2,1)} %add_convert_fusion.5), channel_id=1, source_target_pairs={{0,8},{4,12},{1,9},{5,13},{2,10},{6,14},{3,11},{7,15},{16,24},{20,... | collective-permute-start | bytes 3145736 | tf_op jit(solution)/shard_map/ppermute | solution.py:20
  215.1 166.4 %all-gather.12.cloned.1.call-start = ((), (), s32[]{:S(2)}) async-start(), calls=%async_computation.8 | async-start | bytes 3145728 | tf_op jit(solution)/shard_map/all_gather | solution.py:89
  215.8 200.3 %all-gather.14.cloned.1.call-start = ((), (), s32[]{:S(2)}) async-start(), calls=%async_computation.9 | async-start | bytes 3145728 | tf_op jit(solution)/shard_map/all_gather | solution.py:91
  216.4 297.2 %all-reduce.18.cloned.1.call-start = ((), (), s32[]{:S(2)}) async-start(), calls=%async_computation.10 | async-start | bytes 8388608 | tf_op jit(solution)/shard_map/psum | solution.py:45
  220.8 292.7 %copy-start.24 = (f32[2,1,512]{2,1,0:T(1,128)}, f32[2,1,512]{2,1,0:T(1,128)S(1)}, u32[]{:S(2)}) copy-start(f32[2,1,512]{2,1,0:T(1,128)S(1)} %convert_element_type.308) | copy-start | bytes 12292
  225.2 421.4 %copy-start.32 = (f32[2,1,512]{2,1,0:T(1,128)}, f32[2,1,512]{2,1,0:T(1,128)S(1)}, u32[]{:S(2)}) copy-start(f32[2,1,512]{2,1,0:T(1,128)S(1)} %convert_element_type.309) | copy-start | bytes 12292
  427.9 205.7 %all-reduce.20.cloned.1.call-start = ((), (), s32[]{:S(2)}) async-start(), calls=%async_computation.11 | async-start | bytes 8388608 | tf_op jit(solution)/shard_map/psum | solution.py:45
  547.9 428.9 %reduce-scatter.21.cloned.1.call-start = ((), (), s32[]{:S(2)}) async-start(), calls=%async_computation.18 | async-start | bytes 98304
  774.4 29.2 %collective-permute-start.6 = (bf16[4,512,4,64]{1,3,2,0:T(8,128)(2,1)}, bf16[4,512,4,64]{1,3,2,0:T(8,128)(2,1)}, u32[]{:S(2)}, u32[]{:S(2)}) collective-permute-start(bf16[4,512,4,64]{1,3,2,0:T(8,128)(2,1)} %get-tuple-element.273), channel_id=1, source_target_pairs={{4,0},{8,4},{12,8},{5,1},{9,5},{13,9},{6,2},{10,6},{14,10},{7,3},{... | collective-permute-start | bytes 3145736 | tf_op jit(solution)/shard_map/ppermute | solution.py:20
  775.7 95.3 %collective-permute-start.7 = (bf16[4,512,4,64]{1,3,2,0:T(8,128)(2,1)}, bf16[4,512,4,64]{1,3,2,0:T(8,128)(2,1)}, u32[]{:S(2)}, u32[]{:S(2)}) collective-permute-start(bf16[4,512,4,64]{1,3,2,0:T(8,128)(2,1)} %get-tuple-element.274), channel_id=1, source_target_pairs={{8,0},{12,4},{9,1},{13,5},{10,2},{14,6},{11,3},{15,7},{24,16},{28,... | collective-permute-start | bytes 3145736 | tf_op jit(solution)/shard_map/ppermute | solution.py:20
  779.0 95.6 %collective-permute-start.4 = (bf16[4,512,4,64]{1,3,2,0:T(8,128)(2,1)}, bf16[4,512,4,64]{1,3,2,0:T(8,128)(2,1)}, u32[]{:S(2)}, u32[]{:S(2)}) collective-permute-start(bf16[4,512,4,64]{1,3,2,0:T(8,128)(2,1)} %get-tuple-element.275), channel_id=1, source_target_pairs={{4,0},{8,4},{12,8},{5,1},{9,5},{13,9},{6,2},{10,6},{14,10},{7,3},{... | collective-permute-start | bytes 3145736 | tf_op jit(solution)/shard_map/ppermute | solution.py:20
  780.3 134.3 %collective-permute-start.5 = (bf16[4,512,4,64]{1,3,2,0:T(8,128)(2,1)}, bf16[4,512,4,64]{1,3,2,0:T(8,128)(2,1)}, u32[]{:S(2)}, u32[]{:S(2)}) collective-permute-start(bf16[4,512,4,64]{1,3,2,0:T(8,128)(2,1)} %get-tuple-element.276), channel_id=1, source_target_pairs={{8,0},{12,4},{9,1},{13,5},{10,2},{14,6},{11,3},{15,7},{24,16},{28,... | collective-permute-start | bytes 3145736 | tf_op jit(solution)/shard_map/ppermute | solution.py:20
  782.4 198.2 %reduce-scatter.19.cloned.1.call-start = ((), (), s32[]{:S(2)}) async-start(), calls=%async_computation.17 | async-start | bytes 24576
  926.0 96.2 %all-reduce.22.cloned.1.call-start = ((), (), s32[]{:S(2)}) async-start(), calls=%async_computation.12 | async-start | bytes 8388608 | tf_op jit(solution)/shard_map/psum | solution.py:45
  937.3 102.3 %reduce-scatter.13.cloned.1.call-start = ((), (), s32[]{:S(2)}) async-start(), calls=%async_computation.14 | async-start | bytes 786432 | tf_op jit(solution)/shard_map/reduce_scatter | solution.py:279
  942.9 131.5 %reduce-scatter.17.cloned.1.call-start = ((), (), s32[]{:S(2)}) async-start(), calls=%async_computation.16 | async-start | bytes 3145728 | tf_op jit(solution)/shard_map/reduce_scatter | solution.py:297
  956.3 152.6 %reduce-scatter.15.cloned.1.call-start = ((), (), s32[]{:S(2)}) async-start(), calls=%async_computation.15 | async-start | bytes 3145728 | tf_op jit(solution)/shard_map/reduce_scatter | solution.py:291
  967.7 170.2 %reduce-scatter.11.cloned.1.call-start = ((), (), s32[]{:S(2)}) async-start(), calls=%async_computation.13 | async-start | bytes 2359296 | tf_op jit(solution)/shard_map/reduce_scatter | solution.py:273
  974.6 289.1 %all-reduce.24.cloned.1.call-start = ((), (), s32[]{:S(2)}) async-start(), calls=%async_computation.19 | async-start | bytes 6291456 | tf_op jit(solution)/shard_map/psum | solution.py:307
  (78 other events, 2118.9 us)
Sparse Core Ops, SparseCore 0:
  9.6 30.2 all-gather.9
  215.2 131.3 all-reduce.15
  348.2 33.2 all-gather.11
  382.9 33.1 all-gather.13
  428.0 85.4 all-reduce.17
  548.0 85.6 all-reduce.19
  782.6 15.2 reduce-scatter.20
  926.1 7.4 reduce-scatter.18
  937.4 84.6 all-reduce.21
  1024.8 14.6 reduce-scatter.12
  1042.5 31.8 reduce-scatter.16
  1077.0 31.8 reduce-scatter.14
  1111.8 26.0 reduce-scatter.10
  1140.4 123.3 all-reduce.23
where the time goes:
time: 1290 us; the launch traced here: 1280 us
  waiting for transfers between devices  689 us (53%)
  matrix products  212 us (16%)
  other arithmetic  150 us (12%)
  blocking collectives  106 us (8%)
  local copies, waits for them, and re-layouts  86.1 us (7%)
  starting transfers between devices  19.3 us (1%)
  between operations  18.9 us (1%)
    psum x4, waiting for transfers between devices, row_total(): return lax.psum(term.astype(jnp.bfloat16), 'tensor').astype(jnp.float32)  298 us
    ppermute x8, waiting for transfers between devices, passed_along(): return lax.ppermute(block, axis, route)  174 us
    psum x1, waiting for transfers between devices, local(): lax.psum(owned[2].astype(jnp.bfloat16), 'context').astype(jnp.float32)  54.1 us
    psum x2, blocking collectives, local(): lax.psum((jnp.sum(mask_rows), jnp.sum(mask_rows * jnp.sum(difference * di...  43.4 us
    dot_general x8, matrix products, masked_scores(): jnp.einsum('qhe,khe->hqk', query_one, keys_one, preferred_element_type=jn...  36.7 us
    reduce_sum x6, other arithmetic, norm_rows(): return center * lax.rsqrt(spread + EPSILON) * gain + shift  36.4 us
    reduce_scatter x1, waiting for transfers between devices, local(): lax.psum_scatter(gradients[10].astype(jnp.bfloat16), 'fsdp', scatter_dime...  34.8 us
    reduce_scatter x1, waiting for transfers between devices, local(): lax.psum_scatter(gradients[8].astype(jnp.bfloat16), 'fsdp', scatter_dimen...  34.6 us
  transfers between devices with their start and end apart: 22, of which 18 were waited for; matrix products, arithmetic and copies ran while one was open for 13% of the time, Pallas kernels for 0%

commit v1 on v0

--- a/solution.py
+++ b/solution.py
@@ -1,17 +1,408 @@
+import functools
 import math
 
 import jax
 import jax.numpy as jnp
 from jax import lax
+from jax.experimental import pallas as pl
+from jax.experimental.pallas import tpu as pltpu
 from jax.sharding import PartitionSpec as P
 
+MESH = pl.DeviceIdType.MESH
+BF = jnp.bfloat16
+F32 = jnp.float32
 D = 1024
 HD = 64
 WINDOW = 1024
-
-
 EPSILON = 1e-05
 MASKED = -1e30
+QUARTER = 128
+HALF = 256
+
+
+def matmul(left, right, over_left, over_right):
+    dims = (((over_left,), (over_right,)), ((), ()))
+    return lax.dot_general(left, right, dims, preferred_element_type=F32)
+
+
+def norm_parts(values):
+    mean = jnp.mean(values, axis=-1, keepdims=True)
+    center = values - mean
+    spread = jnp.mean(center * center, axis=-1, keepdims=True)
+    inverse = lax.rsqrt(spread + EPSILON)
+    return center * inverse, inverse
+
+
+def column_sum(values):
+    return jnp.sum(values, axis=0, keepdims=True)
+
+
+def mid_kernel(
+    nf,
+    att,
+    wout_s,
+    wfc1_s,
+    wfc2_s,
+    tokens,
+    teacher,
+    cot,
+    vec,
+    mask,
+    out_h,
+    gmix_h,
+    gmid_h,
+    gfc1,
+    gfc2,
+    small,
+    wout,
+    wfc1,
+    wfc2,
+    ag,
+    act,
+    slope,
+    send,
+    recv_c,
+    send_y,
+    recv_y,
+    mid,
+    gblk,
+    tok_q,
+    tea_q,
+    cot_q,
+    tea_b,
+    cot_b,
+    maskc,
+    w_send,
+    w_recv,
+    w_loc,
+    sems,
+    q_sems,
+    in_sems,
+    out_sem,
+    res_sem,
+):
+    me_f, me_z, me_t = (
+        lax.axis_index("fsdp"),
+        lax.axis_index("context"),
+        lax.axis_index("tensor"),
+    )
+    me_y, me_c = me_t // 2, me_t % 2
+    mate_c = (me_f, me_z, me_t + 1 - 2 * me_c)
+    mate_y = (me_f, me_z, (me_t + 2) % 4)
+    mine = (2 * me_c + me_y) * QUARTER
+    over_y = (2 * me_c + 1 - me_y) * QUARTER
+
+    def rows(start, size=QUARTER):
+        return pl.ds(pl.multiple_of(start, QUARTER), size)
+
+    barrier = pltpu.get_barrier_semaphore()
+    peers = [(lax.rem(me_f + j, nf), me_z, me_t) for j in range(1, nf)]
+    for peer in [mate_c, mate_y] + peers:
+        pl.semaphore_signal(barrier, inc=1, device_id=peer, device_id_type=MESH)
+    pl.semaphore_wait(barrier, 1 + nf)
+
+    fs = wout_s.shape[1]
+    own = pl.ds(pl.multiple_of(me_f * fs, fs), fs)
+    places = (
+        (wout_s, wout.at[:, own]),
+        (wfc1_s, wfc1.at[own, :]),
+        (wfc2_s, wfc2.at[:, own]),
+    )
+
+    def weight_copy(i, j):
+        return pltpu.make_async_remote_copy(
+            places[i][0],
+            places[i][1],
+            w_send.at[i, j],
+            w_recv.at[i, j],
+            device_id=peers[j],
+            device_id_type=MESH,
+        )
+
+    for i in range(3):
+        for j in range(nf - 1):
+            weight_copy(i, j).start()
+        pltpu.make_async_copy(places[i][0], places[i][1], w_loc.at[i]).start()
+
+    def weight_wait(i):
+        pltpu.make_async_copy(places[i][0], places[i][1], w_loc.at[i]).wait()
+        for j in range(nf - 1):
+            weight_copy(i, j).wait()
+
+    quarters = ((tokens, tok_q), (teacher, tea_q), (cot, cot_q))
+    for i, (source, target) in enumerate(quarters):
+        pltpu.make_async_copy(source.at[:, rows(mine), :], target, q_sems.at[i]).start()
+
+    def block_copies(s):
+        slot = lax.rem(s, 2)
+        return (
+            pltpu.make_async_copy(teacher.at[s], tea_b.at[slot], in_sems.at[0, slot]),
+            pltpu.make_async_copy(cot.at[s], cot_b.at[slot], in_sems.at[1, slot]),
+        )
+
+    turned = jnp.transpose(mask[...])
+    for s in range(4):
+        maskc[s] = turned[:, s : s + 1]
+    small[...] = jnp.zeros_like(small)
+
+    RSC, RSY, AGY, AGO, AGF = range(5)
+
+    def remote(src, dst, which, s, mate):
+        return pltpu.make_async_remote_copy(
+            src,
+            dst,
+            sems.at[which, 0, s],
+            sems.at[which, 1, s],
+            device_id=mate,
+            device_id_type=MESH,
+        )
+
+    def rs_core(s):
+        half = rows((1 - me_c) * HALF, HALF)
+        return remote(send.at[s, half], recv_c.at[s], RSC, s, mate_c)
+
+    def rs_y(s):
+        return remote(send_y.at[s], recv_y.at[s], RSY, s, mate_y)
+
+    def ag_y(k, s):
+        return remote(ag.at[k, s, rows(mine)], ag.at[k, s, rows(mine)], AGY, s, mate_y)
+
+    def ag_own(k, s):
+        return remote(ag.at[k, s, rows(mine)], ag.at[k, s, rows(mine)], AGO, s, mate_c)
+
+    def ag_forward(k, s):
+        return remote(ag.at[k, s, rows(over_y)], ag.at[k, s, rows(over_y)], AGF, s, mate_c)
+
+    def step_q(s):
+        rs_core(s).wait()
+        send_y[s] = (
+            send[s, rows(over_y)].astype(F32)
+            + recv_c[s, rows((1 - me_y) * QUARTER)].astype(F32)
+        ).astype(BF)
+        rs_y(s).start()
+
+    def total(s):
+        rs_y(s).wait()
+        return (
+            send[s, rows(mine)].astype(F32)
+            + recv_c[s, rows(me_y * QUARTER)].astype(F32)
+            + recv_y[s].astype(F32)
+        )
+
+    def step_r(k, s):
+        summed = total(s)
+        if k == 0:
+            middle = tok_q[s].astype(F32) + summed + vec[0:1, :]
+            mid[s] = middle
+            xhat, _ = norm_parts(middle)
+            ag[0, s, rows(mine)] = (xhat * vec[1:2, :] + vec[2:3, :]).astype(BF)
+        elif k == 1:
+            block = mid[s] + summed + vec[4:5, :]
+            ag[1, s, rows(mine)] = block.astype(BF)
+            masks = maskc[s, rows(mine)]
+            difference = block - tea_q[s].astype(F32)
+            masked = masks * difference
+            small[5:6, :] += column_sum(masked * difference)
+            grad = cot_q[s].astype(F32) + masked * vec[5:6, :]
+            gblk[s] = grad
+            small[0:1, :] += column_sum(grad)
+        else:
+            grad_normed = summed
+            xhat, inverse = norm_parts(mid[s])
+            small[1:2, :] += column_sum(grad_normed * xhat)
+            small[2:3, :] += column_sum(grad_normed)
+            e = grad_normed * vec[1:2, :]
+            grad = gblk[s] + inverse * (
+                e
+                - jnp.mean(e, axis=-1, keepdims=True)
+                - xhat * jnp.mean(e * xhat, axis=-1, keepdims=True)
+            )
+            gblk[s] = grad
+            small[3:4, :] += column_sum(grad)
+            ag[2, s, rows(mine)] = grad.astype(BF)
+        ag_y(k, s).start()
+        ag_own(k, s).start()
+
+    def step_t(k, s):
+        ag_y(k, s).wait()
+        ag_forward(k, s).start()
+
+    def step_u(k, s):
+        ag_own(k, s).wait()
+        ag_forward(k, s).wait()
+
+    def step_p(k, s):
+        if k == 0:
+            start = pl.multiple_of(s * 512, 512)
+            send[s] = matmul(att[pl.ds(start, 512), :], wout[...], 1, 0).astype(BF)
+        elif k == 1:
+            for part in range(2):
+                here = pl.ds(part * 256, 256)
+                h = matmul(ag[0, s, here], wfc1[...], 1, 0) + vec[3:4, :]
+                t = jnp.tanh(0.7978845608028654 * (h + 0.044715 * h * h * h))
+                act[s, here] = (0.5 * h * (1.0 + t)).astype(BF)
+                slope[s, here] = (
+                    0.5 * (1.0 + t)
+                    + 0.5 * h * (1.0 - t * t) * (0.7978845608028654 * (1.0 + 0.134145 * h * h))
+                ).astype(BF)
+            send[s] = matmul(act[s], wfc2[...], 1, 0).astype(BF)
+        else:
+            slot = lax.rem(s, 2)
+            out = pltpu.make_async_copy(ag.at[1, s], out_h.at[s], out_sem)
+            out.start()
+            for copy in block_copies(s):
+                copy.wait()
+
+            @pl.when(s < 3)
+            def _():
+                for copy in block_copies(s + 1):
+                    copy.start()
+
+            out.wait()
+            for part in range(2):
+                here = pl.ds(part * 256, 256)
+                difference = ag[1, s, here].astype(F32) - tea_b[slot, here].astype(F32)
+                scaled = maskc[s, here] * vec[5:6, :]
+                down = (cot_b[slot, here].astype(F32) + scaled * difference).astype(BF)
+                ag[1, s, here] = down
+                up = matmul(down, wfc2[...], 1, 1) * slope[s, here].astype(F32)
+                rounded = up.astype(BF)
+                slope[s, here] = rounded
+                small[4:5, :] += column_sum(rounded.astype(F32))
+            send[s] = matmul(slope[s], wfc1[...], 1, 1).astype(BF)
+        rs_core(s).start()
+
+    weight_wait(0)
+    for i, (source, target) in enumerate(quarters):
+        pltpu.make_async_copy(source.at[:, rows(mine), :], target, q_sems.at[i]).wait()
+
+    for k in range(3):
+        if k == 1:
+            for copy in block_copies(0):
+                copy.start()
+
+        def tick(s, carry, k=k):
+            if k == 0:
+
+                @pl.when(s >= 3)
+                def _():
+                    step_t(0, s - 3)
+
+                @pl.when(s >= 2)
+                def _():
+                    step_r(0, s - 2)
+
+                @pl.when(s >= 1)
+                def _():
+                    step_q(s - 1)
+
+                step_p(0, s)
+            else:
+
+                @pl.when(s >= 3)
+                def _():
+                    step_t(k, s - 3)
+
+                @pl.when(s < 3)
+                def _():
+                    step_t(k - 1, s + 1)
+
+                @pl.when(s >= 2)
+                def _():
+                    step_r(k, s - 2)
+
+                @pl.when(s < 2)
+                def _():
+                    step_r(k - 1, s + 2)
+
+                step_q(lax.rem(s + 3, 4))
+                step_u(k - 1, s)
+                if k == 1:
+
+                    @pl.when(s == 0)
+                    def _():
+                        weight_wait(1)
+                        weight_wait(2)
+
+                step_p(k, s)
+            return carry
+
+        lax.fori_loop(0, 4, tick, 0)
+
+    step_t(2, 1)
+    step_r(2, 2)
+    step_q(3)
+    deep = lambda ref: ref.reshape(2048, 1024)
+    gfc2[...] = matmul(deep(act)[...], deep(ag.at[1])[...], 0, 0).astype(BF)
+    step_t(2, 2)
+    step_r(2, 3)
+    gfc1[...] = matmul(deep(ag.at[0])[...], deep(slope)[...], 0, 0).astype(BF)
+    step_t(2, 3)
+    for s in range(4):
+        step_u(2, s)
+    copies = (
+        pltpu.make_async_copy(ag.at[2], gmix_h, res_sem.at[0]),
+        pltpu.make_async_copy(gblk, gmid_h, res_sem.at[1]),
+    )
+    for copy in copies:
+        copy.start()
+    for copy in copies:
+        copy.wait()
+
+
+def mid_call(nf, att, wout_s, wfc1_s, wfc2_s, tokens, teacher, cot, vec, mask):
+    anys = pl.BlockSpec(memory_space=pl.ANY)
+    vmem = pl.BlockSpec(memory_space=pltpu.VMEM)
+    dma = pltpu.SemaphoreType.DMA
+    big = lambda *lead: pltpu.VMEM((*lead, 512, 1024), BF)
+    return pl.pallas_call(
+        functools.partial(mid_kernel, nf),
+        out_shape=(
+            jax.ShapeDtypeStruct((4, 512, 1024), BF),
+            jax.ShapeDtypeStruct((4, 512, 1024), BF),
+            jax.ShapeDtypeStruct((4, QUARTER, 1024), F32),
+            jax.ShapeDtypeStruct((1024, 1024), BF),
+            jax.ShapeDtypeStruct((1024, 1024), BF),
+            jax.ShapeDtypeStruct((8, 1024), F32),
+        ),
+        in_specs=[vmem, anys, anys, anys, anys, anys, anys, vmem, vmem],
+        out_specs=(anys, anys, anys, vmem, vmem, vmem),
+        scratch_shapes=[
+            pltpu.VMEM((256, 1024), BF),
+            pltpu.VMEM((1024, 1024), BF),
+            pltpu.VMEM((1024, 1024), BF),
+            big(3, 4),
+            big(4),
+            big(4),
+            big(4),
+            pltpu.VMEM((4, HALF, 1024), BF),
+            pltpu.VMEM((4, QUARTER, 1024), BF),
+            pltpu.VMEM((4, QUARTER, 1024), BF),
+            pltpu.VMEM((4, QUARTER, 1024), F32),
+            pltpu.VMEM((4, QUARTER, 1024), F32),
+            pltpu.VMEM((4, QUARTER, 1024), BF),
+            pltpu.VMEM((4, QUARTER, 1024), BF),
+            pltpu.VMEM((4, QUARTER, 1024), BF),
+            big(2),
+            big(2),
+            pltpu.VMEM((4, 512, 1), F32),
+            dma((3, nf - 1)),
+            dma((3, nf - 1)),
+            dma((3,)),
+            dma((5, 2, 4)),
+            dma((3,)),
+            dma((2, 2)),
+            dma,
+            dma((2,)),
+        ],
+        compiler_params=pltpu.CompilerParams(
+            collective_id=1, has_side_effects=True, vmem_limit_bytes=62 * 2**20
+        ),
+        cost_estimate=pl.CostEstimate(
+            flops=2 * 2048 * 1024 * 1024 * 7, bytes_accessed=30 * 2**20, transcendentals=0
+        ),
+        name="mid",
+    )(att, wout_s, wfc1_s, wfc2_s, tokens, teacher, cot, vec, mask)
 
 
 def passed_along(block, axis, distance):
@@ -141,42 +532,26 @@
 
     mixed, log_total = lax.map(attend_one, (query, keys_all, values_all, allowed))
     attended = mixed.reshape(rows, local_width).astype(jnp.bfloat16)
-    attn_term = jnp.dot(attended, weight_out, preferred_element_type=jnp.float32)
-    mask_rows = valid_mask.reshape(rows).astype(jnp.float32)
-    teacher_rows = teacher.astype(jnp.float32).reshape(rows, width)
-    cot_rows = cotangent.astype(jnp.float32).reshape(rows, width)
-    middle = resid_in + row_total(attn_term) + bias_out
-    normed_two = norm_rows(middle, gain_two, bias_two).astype(jnp.bfloat16)
-    hidden = jnp.dot(normed_two, weight_up, preferred_element_type=jnp.float32) + bias_up
-    activated = gelu_tanh(hidden).astype(jnp.bfloat16)
-    down_term = jnp.dot(activated, weight_down, preferred_element_type=jnp.float32)
-    block = middle + row_total(down_term) + bias_down
-    difference = block - teacher_rows
-    count, error_sum = lax.psum(
-        (jnp.sum(mask_rows), jnp.sum(mask_rows * jnp.sum(difference * difference, axis=-1))),
-        ("fsdp", "context"),
-    )
+    mask_f = jnp.concatenate([valid_mask, jnp.zeros_like(valid_mask)], axis=0).astype(jnp.float32)
+    count = lax.psum(jnp.sum(mask_f), ("fsdp", "context"))
     tokens_all = rows * lax.axis_size("fsdp") * lax.axis_size("context")
-    grad_block = cot_rows + tokens_all / count * mask_rows[:, None] * difference
-    loss = error_sum / (2.0 * D * count)
-    grad_down = grad_block.astype(jnp.bfloat16)
-    grad_b_fc2 = jnp.sum(grad_block, axis=0)
-    grad_w_fc2 = jnp.einsum("rf,rd->fd", activated, grad_down, preferred_element_type=jnp.float32)
-    grad_act = jnp.einsum("rd,fd->rf", grad_down, weight_down, preferred_element_type=jnp.float32)
-    _, gelu_pull = jax.vjp(gelu_tanh, hidden)
-    grad_hidden = gelu_pull(grad_act)[0].astype(jnp.bfloat16)
-    grad_w_fc1 = jnp.einsum(
-        "rd,rf->df", normed_two, grad_hidden, preferred_element_type=jnp.float32
-    )
-    grad_b_fc1 = jnp.sum(grad_hidden, axis=0, dtype=jnp.float32).reshape(b_fc1.shape[0], -1)
-    normed_term = jnp.einsum(
-        "rf,df->rd", grad_hidden, weight_up, preferred_element_type=jnp.float32
-    )
-    _, second_pull = jax.vjp(norm_rows, middle, gain_two, bias_two)
-    grad_mid_norm, grad_ln2_gain, grad_ln2_bias = second_pull(row_total(normed_term))
-    grad_middle = grad_block + grad_mid_norm
-    grad_mix = grad_middle.astype(jnp.bfloat16)
-    grad_b_out = jnp.sum(grad_middle, axis=0)
+    zero = jnp.zeros_like(bias_out)
+    vec = jnp.stack(
+        [bias_out, gain_two, bias_two, bias_up, bias_down, zero + tokens_all / count, zero, zero]
+    )
+    nf = lax.axis_size("fsdp")
+    output, grad_mix, grad_middle, grad_w_fc1, grad_w_fc2, small = mid_call(
+        nf, attended, w_out, w_fc1, w_fc2, tokens, teacher, cotangent, vec, mask_f
+    )
+    place_t = lax.axis_index("tensor")
+    place_q = 2 * (place_t % 2) + place_t // 2
+    summed = lax.psum(jnp.stack([small[0], small[1], small[2], small[3], small[5]]), ("tensor",))
+    loss = lax.psum(jnp.sum(summed[4]), ("fsdp", "context")) / (2.0 * D * count)
+    grad_b_fc2, grad_ln2_gain, grad_ln2_bias, grad_b_out = summed[0], summed[1], summed[2], summed[3]
+    grad_b_fc1 = small[4].reshape(b_fc1.shape[0], -1)
+    grad_mix = grad_mix.reshape(rows, width)
+    grad_middle = lax.all_gather(grad_middle, "tensor", axis=0)
+    grad_middle = grad_middle[jnp.array([0, 2, 1, 3])].transpose(1, 0, 2, 3).reshape(rows, width)
     grad_w_out = jnp.einsum("re,rd->ed", attended, grad_mix, preferred_element_type=jnp.float32)
     grad_attended = jnp.einsum(
         "rd,ed->re", grad_mix, weight_out, preferred_element_type=jnp.float32
@@ -315,7 +690,6 @@
         lax.psum(owned[10].astype(jnp.bfloat16), "context").astype(jnp.float32),
         lax.psum(owned[11].astype(jnp.bfloat16), "context").astype(jnp.float32),
     )
-    output = block.astype(jnp.bfloat16).reshape(seqs, group, width)
     return (
         output,
         loss,

time: 1290 us -> 1110 us (0.86)
  waiting for transfers between devices: 689 us -> 346 us
  Pallas kernels: 0 us -> 167 us
  blocking collectives: 106 us -> 226 us
  matrix products: 212 us -> 139 us
  other arithmetic: 150 us -> 93.7 us
    psum x4 -> x1, waiting for transfers between devices: 298 us -> 74.7 us  [row_total(): return lax.psum(term.astype(jnp.bfloat16), 'tensor').astype(jnp.float32)]
    pallas_call x0 -> x1, Pallas kernels: none -> 167 us  [mid_call(): pl.pallas_call(functools.partial(mid_kernel, nf), out_shape=(jax.ShapeDty...]
    psum x2 -> x3, blocking collectives: 43.4 us -> 156 us  [the longest x1 123 us: local(): count = lax.psum(jnp.sum(mask_f), ('fsdp', 'context'))]
    dot_general x7 -> x0, matrix products: 74.1 us -> none  [the longest x1 15.4 us: local(): jnp.einsum('rd,fd->rf', grad_down, weight_down, preferred_element_type=jn...]
    ppermute x8, waiting for transfers between devices: 174 us -> 118 us  [passed_along(): return lax.ppermute(block, axis, route)]
    reduce_scatter x1, waiting for transfers between devices: 34.8 us -> 0.02 us  [local(): lax.psum_scatter(gradients[10].astype(jnp.bfloat16), 'fsdp', scatter_dime...]
    reduce_scatter x1, waiting for transfers between devices: 34.6 us -> 0.02 us  [local(): lax.psum_scatter(gradients[8].astype(jnp.bfloat16), 'fsdp', scatter_dimen...]
    psum x1, waiting for transfers between devices: 54.1 us -> 85.1 us  [local(): lax.psum(owned[2].astype(jnp.bfloat16), 'context').astype(jnp.float32)]
  transfers between devices with their start and end apart: 22 -> 18, of which waited for: 18 -> 7; matrix products, arithmetic and copies ran while one was open for 13% -> 21% of each run, Pallas kernels for 0% -> 0%
where the time goes in v1:
time: 1110 us; the launch traced here: 1100 us
  waiting for transfers between devices  346 us (31%)
  blocking collectives  226 us (20%)
  Pallas kernels  167 us (15%)
  matrix products  139 us (13%)
  local copies, waits for them, and re-layouts  94.5 us (9%)
  other arithmetic  93.7 us (8%)
  starting transfers between devices  19.6 us (2%)
  between operations  19.1 us (2%)
    pallas_call x1, Pallas kernels, mid_call(): pl.pallas_call(functools.partial(mid_kernel, nf), out_shape=(jax.ShapeDty...  167 us
    psum x1, blocking collectives, local(): count = lax.psum(jnp.sum(mask_f), ('fsdp', 'context'))  123 us
    ppermute x8, waiting for transfers between devices, passed_along(): return lax.ppermute(block, axis, route)  118 us
    psum x1, waiting for transfers between devices, local(): lax.psum(owned[2].astype(jnp.bfloat16), 'context').astype(jnp.float32)  85.1 us
    psum x1, waiting for transfers between devices, row_total(): return lax.psum(term.astype(jnp.bfloat16), 'tensor').astype(jnp.float32)  74.7 us
    all_gather x1, waiting for transfers between devices, local(): grad_middle = lax.all_gather(grad_middle, 'tensor', axis=0)  49.9 us
    dot_general x8, matrix products, masked_scores(): jnp.einsum('qhe,khe->hqk', query_one, keys_one, preferred_element_type=jn...  37.8 us
  transfers between devices with their start and end apart: 18, of which 7 were waited for; matrix products, arithmetic and copies ran while one was open for 21% of the time, Pallas kernels for 0%

profile of v1, /device:TPU:0, one launch (start us, length us, event | category | flops | bytes accessed | tf_op | source)
XLA Modules:
  0.0 1104.7 jit_solution(10031784901056001830)
XLA Ops:
  43.2 5.6 fusion.58
  76.9 122.6 %psum.112 = f32[]{:T(128)} all-reduce(f32[]{:T(128)} %fusion.69), channel_id=1, replica_groups=mesh['fsdp'=2,'context'=4,'tensor'=4] {'fsdp','context'}, use_global_device_ids=true, to_apply=%region_7.8 | all-reduce | flops 1 | bytes 8 | tf_op jit(solution)/shard_map/psum | solution.py:536
  237.8 53.9 %while.26 = (s32[]{:T(128)}, bf16[4,512,4,64]{1,3,2,0:T(8,128)(2,1)S(1)}, f32[4,4,512,1]{2,1,3,0:T(4,128)S(1)}, bf16[4,1536,4,64]{1,3,2,0:T(8,128)(2,1)}, pred[4...) while((s32[]{:T(128)}, ...), condition=%wide.region_5.6_spmd, body=%wide.region_2.5_spmd.sunk | while | flops 843053056 | bytes 44107876 | solution.py:533
  294.1 167.2 %mid.1 = (bf16[4,512,1024]{2,1,0:T(8,128)(2,1)}, bf16[4,512,1024]{2,1,0:T(8,128)(2,1)}, f32[4,128,1024]{2,1,0:T(8,128)}, bf16[1024,1024]{1,0:T(8,128)(2,1)}, bf1...) custom-call(bf16[2048,256]{1,0:T(8,128)(2,1)} %copy.102.att, bf16[256,512]{1,0:T(8,128)(2,1)} %wout_s.1, ...), custom_call_target="tpu_custom_call" | custom-call | flops 30064771072 | bytes 31457280 | tf_op jit(solution)/shard_map/mid/pallas_call | solution.py:358
  466.4 12.6 %all_gather.47 = bf16[256,1024]{1,0:T(8,128)(2,1)S(1)} all-gather(bf16[256,512]{1,0:T(8,128)(2,1)S(1)} %copy-done.14), channel_id=1, replica_groups=mesh['fsdp'=2,'context'=4,'tensor'=4] {'fsdp'}, dimensions={1}, use_global_device_ids=true | all-gather | bytes 786432 | tf_op jit(solution)/shard_map/all_gather | solution.py:476
  485.7 100.4 %while.27 = (s32[]{:T(128)}, bf16[4,512,4,64]{1,3,2,0:T(8,128)(2,1)}, f32[4,1536,4,64]{1,3,2,0:T(8,128)}, f32[4,1536,4,64]{1,3,2,0:T(8,128)}, bf16[4,1536,4,64]{...) while((s32[]{:T(128)}, ...), condition=%wide.region_13.14_spmd, body=%wide.region_11.13_spmd.sunk | while | flops 2042099712 | bytes 145798448 | solution.py:583
  491.4 5.7 multiply_reduce_fusion.3
  516.4 5.7 multiply_reduce_fusion.3
  541.5 5.7 multiply_reduce_fusion.3
  566.5 5.7 multiply_reduce_fusion.3
  604.4 16.2 %collective-permute-done.6 = bf16[4,512,4,64]{1,3,2,0:T(8,128)(2,1)} collective-permute-done((bf16[4,512,4,64]{1,3,2,0:T(8,128)(2,1)}, bf16[4,512,4,64]{1,3,2,0:T(8,128)(2,1)}, u32[]{:S(2)}, u32[]{:S(2)}) %collective-permute-start.6) | collective-permute-done | bytes 1048608 | tf_op jit(solution)/shard_map/ppermute | solution.py:411
  620.6 68.9 %collective-permute-done.7 = bf16[4,512,4,64]{1,3,2,0:T(8,128)(2,1)} collective-permute-done((bf16[4,512,4,64]{1,3,2,0:T(8,128)(2,1)}, bf16[4,512,4,64]{1,3,2,0:T(8,128)(2,1)}, u32[]{:S(2)}, u32[]{:S(2)}) %collective-permute-start.7) | collective-permute-done | bytes 1048608 | tf_op jit(solution)/shard_map/ppermute | solution.py:411
  698.2 33.4 %collective-permute-done.5 = bf16[4,512,4,64]{1,3,2,0:T(8,128)(2,1)} collective-permute-done((bf16[4,512,4,64]{1,3,2,0:T(8,128)(2,1)}, bf16[4,512,4,64]{1,3,2,0:T(8,128)(2,1)}, u32[]{:S(2)}, u32[]{:S(2)}) %collective-permute-start.5) | collective-permute-done | bytes 1048608 | tf_op jit(solution)/shard_map/ppermute | solution.py:411
  744.9 7.9 fusion.65
  754.8 6.9 bitcast_convert_fusion
  761.9 15.5 %reduce-scatter.11.cloned.1.call-done = bf16[3,512,256]{1,2,0:T(8,128)(2,1)} async-done(((bf16[3,1024,256]{1,2,0:T(8,128)(2,1)}), bf16[3,512,256]{1,2,0:T(8,128)(2,1)}) %reduce-scatter.11.cloned.1.call-update) | async-done | bytes 786448 | tf_op jit(solution)/shard_map/reduce_scatter | solution.py:648
  779.3 11.8 %psum.113 = f32[5,1024]{1,0:T(8,128)S(1)} all-reduce(f32[5,1024]{1,0:T(8,128)S(1)} %pad_maximum_fusion.2), channel_id=1, replica_groups=mesh['fsdp'=2,'context'=4,'tensor'=4] {'tensor'}, use_global_device_ids=true, to_apply=%region_8.9 | all-reduce | flops 5120 | bytes 40960 | tf_op jit(solution)/shard_map/psum | solution.py:548
  792.4 21.4 %psum.114 = f32[]{:T(128)} all-reduce(f32[]{:T(128)} %slice_reduce_fusion.4), channel_id=1, replica_groups=mesh['fsdp'=2,'context'=4,'tensor'=4] {'fsdp','context'}, use_global_device_ids=true, to_apply=%region_10.11 | all-reduce | flops 1 | bytes 8 | tf_op jit(solution)/shard_map/psum | solution.py:549
  816.3 74.7 %all-reduce.14.cloned.1.call-done = bf16[2048,1024]{1,0:T(8,128)(2,1)} async-done(((bf16[2048,1024]{1,0:T(8,128)(2,1)}), bf16[2048,1024]{1,0:T(8,128)(2,1)}) %all-reduce.14.cloned.1.call-update) | async-done | bytes 4194320 | tf_op jit(solution)/shard_map/psum | solution.py:436
  905.6 7.8 all-reduce.10
  913.8 13.2 %all-reduce.8 = (bf16[512]{0:T(512)(128)(2,1)S(1)}, bf16[512]{0:T(512)(128)(2,1)S(1)}, bf16[2,4,32]{2,1,0:T(4,128)(2,1)S(1)}, bf16[512]{0:T(512)(128)(2,1)S(1)},...) all-reduce(bf16[512]{0:T(512)(128)(2,1)S(1)} %dynamic-slice.1, ...), channel_id=1, replica_groups=mesh['fsdp'=2,'context'=4,'tensor'=4] {'context'}, use_global_device_ids=true, to_apply=%region_19.20 | all-reduce | flops 3840 | bytes 15360 | tf_op jit(solution)/shard_map/psum | solution.py:680
  931.7 85.1 %all-reduce.16.cloned.1.call-done = (bf16[3,512,256]{1,2,0:T(8,128)(2,1)}, bf16[256,512]{1,0:T(8,128)(2,1)}, bf16[512,1024]{1,0:T(8,128)(2,1)}, bf16[1024,512]{1,0:T(8,128)(2,1)}) async-done(((bf16[3,512,256]{1,2,0:T(8,128)(2,1)}, bf16[256,512]{1,0:T(8,128)(2,1)}, bf16[512,1024]{1,0:T(8,128)(2,1)}, bf16[1024,512]{1,0:T(8,128)(2,1)}), (bf16[3,512,256]{1,2,0:T(8,128)(2,1)}, bf16[256,512]{1,0:T(8,128)(2,1)}, ...) | async-done | bytes 3145744 | tf_op jit(solution)/shard_map/psum | solution.py:682
  1025.7 49.9 %all-gather.12.cloned.1.call-done = f32[16,128,1024]{2,1,0:T(8,128)} async-done(((f32[4,128,1024]{2,1,0:T(8,128)}), f32[16,128,1024]{2,1,0:T(8,128)}) %all-gather.12.cloned.1.call-update) | async-done | bytes 8388624 | tf_op jit(solution)/shard_map/all_gather | solution.py:553
  1075.6 7.7 gather_fusion
  (317 shorter events, 333.8 us)
Async XLA Ops:
  7.2 36.0 %all-gather.10.cloned.1.call-start = ((), (), s32[]{:S(2)}) async-start(), calls=%async_computation.6 | async-start | bytes 2359296 | tf_op jit(solution)/shard_map/all_gather | solution.py:474
  7.9 753.9 %reduce-scatter.13.cloned.1.call-start = ((), (), s32[]{:S(2)}) async-start(), calls=%async_computation.9 | async-start | bytes 786432 | tf_op jit(solution)/shard_map/reduce_scatter | solution.py:654
  53.1 173.2 %collective-permute-start.3 = (bf16[4,512,4,64]{1,0,3,2:T(4,128)(2,1)S(1)}, bf16[4,512,4,64]{1,0,3,2:T(4,128)(2,1)}, u32[]{:S(2)}, u32[]{:S(2)}) collective-permute-start(bf16[4,512,4,64]{1,0,3,2:T(4,128)(2,1)S(1)} %convert_element_type.196), channel_id=1, source_target_pairs={{0,4},{4,8},{8,12},{1,5},{5,9},{9,13},{2,6},{6,10},{10,14},{3,7},{... | collective-permute-start | bytes 3145736 | tf_op jit(solution)/shard_map/ppermute | solution.py:411
  58.1 168.3 %collective-permute-start.2 = (bf16[4,512,4,64]{1,0,3,2:T(4,128)(2,1)S(1)}, bf16[4,512,4,64]{1,0,3,2:T(4,128)(2,1)}, u32[]{:S(2)}, u32[]{:S(2)}) collective-permute-start(bf16[4,512,4,64]{1,0,3,2:T(4,128)(2,1)S(1)} %convert_element_type.196), channel_id=1, source_target_pairs={{0,8},{4,12},{1,9},{5,13},{2,10},{6,14},{3,11},{7,15},{16,24},{20,... | collective-permute-start | bytes 3145736 | tf_op jit(solution)/shard_map/ppermute | solution.py:411
  66.4 133.1 %copy-start.27 = (bf16[512]{0:T(512)(128)(2,1)S(1)}, bf16[512]{0:T(512)(128)(2,1)}, u32[]{:S(2)}) copy-start(bf16[512]{0:T(512)(128)(2,1)} %param.32) | copy-start | bytes 3076
  66.4 133.2 %copy-start.28 = (bf16[512]{0:T(512)(128)(2,1)S(1)}, bf16[512]{0:T(512)(128)(2,1)}, u32[]{:S(2)}) copy-start(bf16[512]{0:T(512)(128)(2,1)} %param.33) | copy-start | bytes 3076
  66.4 133.2 %copy-start.29 = (bf16[512]{0:T(512)(128)(2,1)S(1)}, bf16[512]{0:T(512)(128)(2,1)}, u32[]{:S(2)}) copy-start(bf16[512]{0:T(512)(128)(2,1)} %param.34) | copy-start | bytes 3076
  66.4 133.2 %copy-start.30 = (bf16[512]{0:T(512)(128)(2,1)S(1)}, bf16[512]{0:T(512)(128)(2,1)}, u32[]{:S(2)}) copy-start(bf16[512]{0:T(512)(128)(2,1)} %param.38) | copy-start | bytes 3076
  66.4 152.2 %copy-start.24 = (s32[4,512]{1,0:T(4,128)S(1)}, s32[4,512]{1,0:T(4,128)}, u32[]{:S(2)}) copy-start(s32[4,512]{1,0:T(4,128)} %param.25) | copy-start | bytes 24580
  72.3 159.6 %collective-permute-start.1 = (bf16[4,512,4,64]{1,0,3,2:T(4,128)(2,1)}, bf16[4,512,4,64]{1,0,3,2:T(4,128)(2,1)}, u32[]{:S(2)}, u32[]{:S(2)}) collective-permute-start(bf16[4,512,4,64]{1,0,3,2:T(4,128)(2,1)} %add_convert_fusion.4), channel_id=1, source_target_pairs={{0,4},{4,8},{8,12},{1,5},{5,9},{9,13},{2,6},{6,10},{10,14},{3,7},{... | collective-permute-start | bytes 3145736 | tf_op jit(solution)/shard_map/ppermute | solution.py:411
  74.7 157.2 %collective-permute-start = (bf16[4,512,4,64]{1,0,3,2:T(4,128)(2,1)}, bf16[4,512,4,64]{1,0,3,2:T(4,128)(2,1)}, u32[]{:S(2)}, u32[]{:S(2)}) collective-permute-start(bf16[4,512,4,64]{1,0,3,2:T(4,128)(2,1)} %add_convert_fusion.4), channel_id=1, source_target_pairs={{0,8},{4,12},{1,9},{5,13},{2,10},{6,14},{3,11},{7,15},{16,24},{20,... | collective-permute-start | bytes 3145736 | tf_op jit(solution)/shard_map/ppermute | solution.py:411
  465.6 296.3 %reduce-scatter.15.cloned.1.call-start = ((), (), s32[]{:S(2)}) async-start(), calls=%async_computation.10 | async-start | bytes 3145728 | tf_op jit(solution)/shard_map/reduce_scatter | solution.py:666
  466.3 295.6 %reduce-scatter.17.cloned.1.call-start = ((), (), s32[]{:S(2)}) async-start(), calls=%async_computation.11 | async-start | bytes 3145728 | tf_op jit(solution)/shard_map/reduce_scatter | solution.py:672
  484.6 292.8 %reduce-scatter.11.cloned.1.call-start = ((), (), s32[]{:S(2)}) async-start(), calls=%async_computation.8 | async-start | bytes 2359296 | tf_op jit(solution)/shard_map/reduce_scatter | solution.py:648
  591.1 29.5 %collective-permute-start.6 = (bf16[4,512,4,64]{1,3,2,0:T(8,128)(2,1)}, bf16[4,512,4,64]{1,3,2,0:T(8,128)(2,1)}, u32[]{:S(2)}, u32[]{:S(2)}) collective-permute-start(bf16[4,512,4,64]{1,3,2,0:T(8,128)(2,1)} %get-tuple-element.311), channel_id=1, source_target_pairs={{4,0},{8,4},{12,8},{5,1},{9,5},{13,9},{6,2},{10,6},{14,10},{7,3},{... | collective-permute-start | bytes 3145736 | tf_op jit(solution)/shard_map/ppermute | solution.py:411
  592.4 97.1 %collective-permute-start.7 = (bf16[4,512,4,64]{1,3,2,0:T(8,128)(2,1)}, bf16[4,512,4,64]{1,3,2,0:T(8,128)(2,1)}, u32[]{:S(2)}, u32[]{:S(2)}) collective-permute-start(bf16[4,512,4,64]{1,3,2,0:T(8,128)(2,1)} %get-tuple-element.312), channel_id=1, source_target_pairs={{8,0},{12,4},{9,1},{13,5},{10,2},{14,6},{11,3},{15,7},{24,16},{28,... | collective-permute-start | bytes 3145736 | tf_op jit(solution)/shard_map/ppermute | solution.py:411
  595.8 102.5 %collective-permute-start.4 = (bf16[4,512,4,64]{1,3,2,0:T(8,128)(2,1)}, bf16[4,512,4,64]{1,3,2,0:T(8,128)(2,1)}, u32[]{:S(2)}, u32[]{:S(2)}) collective-permute-start(bf16[4,512,4,64]{1,3,2,0:T(8,128)(2,1)} %get-tuple-element.313), channel_id=1, source_target_pairs={{4,0},{8,4},{12,8},{5,1},{9,5},{13,9},{6,2},{10,6},{14,10},{7,3},{... | collective-permute-start | bytes 3145736 | tf_op jit(solution)/shard_map/ppermute | solution.py:411
  597.1 134.6 %collective-permute-start.5 = (bf16[4,512,4,64]{1,3,2,0:T(8,128)(2,1)}, bf16[4,512,4,64]{1,3,2,0:T(8,128)(2,1)}, u32[]{:S(2)}, u32[]{:S(2)}) collective-permute-start(bf16[4,512,4,64]{1,3,2,0:T(8,128)(2,1)} %get-tuple-element.314), channel_id=1, source_target_pairs={{8,0},{12,4},{9,1},{13,5},{10,2},{14,6},{11,3},{15,7},{24,16},{28,... | collective-permute-start | bytes 3145736 | tf_op jit(solution)/shard_map/ppermute | solution.py:411
  752.8 61.8 %reduce-scatter.21.cloned.1.call-start = ((), (), s32[]{:S(2)}) async-start(), calls=%async_computation.14 | async-start | bytes 98304
  753.9 61.5 %reduce-scatter.19.cloned.1.call-start = ((), (), s32[]{:S(2)}) async-start(), calls=%async_computation.13 | async-start | bytes 24576
  754.8 136.2 %all-reduce.14.cloned.1.call-start = ((), (), s32[]{:S(2)}) async-start(), calls=%async_computation.7 | async-start | bytes 8388608 | tf_op jit(solution)/shard_map/psum | solution.py:436
  761.8 132.1 %copy-start.20 = (f32[2,1,512]{2,1,0:T(1,128)S(1)}, f32[2,1,512]{2,1,0:T(1,128)}, u32[]{:S(2)}) copy-start(f32[2,1,512]{2,1,0:T(1,128)} %copy-done.19) | copy-start | bytes 12292
  761.8 255.0 %all-reduce.16.cloned.1.call-start = ((), (), s32[]{:S(2)}) async-start(), calls=%async_computation.15 | async-start | bytes 6291456 | tf_op jit(solution)/shard_map/psum | solution.py:682
  777.4 298.2 %all-gather.12.cloned.1.call-start = ((), (), s32[]{:S(2)}) async-start(), calls=%async_computation.12 | async-start | bytes 10485760 | tf_op jit(solution)/shard_map/all_gather | solution.py:553
  (45 other events, 614.0 us)
Sparse Core Ops, SparseCore 0:
  9.6 30.2 all-gather.9
  465.7 16.5 reduce-scatter.12
  484.6 31.4 reduce-scatter.14
  518.2 31.7 reduce-scatter.16
  752.9 24.4 reduce-scatter.10
  780.0 9.8 reduce-scatter.20
  792.7 9.7 reduce-scatter.18
  805.4 85.4 all-reduce.13
  893.8 122.9 all-reduce.15
  1018.3 57.2 all-gather.11

commit v2 on v0

v2 whole, which is shorter than its diff:
```python
import functools
import math

import jax
import jax.numpy as jnp
from jax import lax
from jax.experimental import pallas as pl
from jax.experimental.pallas import tpu as pltpu
from jax.sharding import PartitionSpec as P

MESH = pl.DeviceIdType.MESH
BF = jnp.bfloat16
F32 = jnp.float32
D = 1024
HD = 64
WINDOW = 1024
EPSILON = 1e-05
MASKED = -1e30
SEQS = 4
GROUP = 512
QUARTER = 128
HALF = 256
SPAN = 1280
LOCAL = 256


def matmul(left, right, over_left, over_right):
    dims = (((over_left,), (over_right,)), ((), ()))
    return lax.dot_general(left, right, dims, preferred_element_type=F32)


def norm_parts(values):
    mean = jnp.mean(values, axis=-1, keepdims=True)
    center = values - mean
    spread = jnp.mean(center * center, axis=-1, keepdims=True)
    inverse = lax.rsqrt(spread + EPSILON)
    return center * inverse, inverse


def norm_back(grad_normed, xhat, inverse, gain):
    e = grad_normed * gain
    return inverse * (
        e
        - jnp.mean(e, axis=-1, keepdims=True)
        - xhat * jnp.mean(e * xhat, axis=-1, keepdims=True)
    )


def column_sum(values):
    return jnp.sum(values, axis=0, keepdims=True)


def aligned(start, size, unit=128):
    return pl.ds(pl.multiple_of(start, unit), size)


def allowed_bias(query_seg, key_seg):
    ahead = lax.broadcasted_iota(jnp.int32, (HALF, SPAN), 1) - lax.broadcasted_iota(
        jnp.int32, (HALF, SPAN), 0
    )
    allowed = (ahead > 0) & (ahead <= WINDOW) & (query_seg == key_seg)
    return jnp.where(allowed, 0.0, MASKED)


class Place:
    def __init__(self, nf):
        self.nf = nf
        self.f = lax.axis_index("fsdp")
        self.z = lax.axis_index("context")
        self.t = lax.axis_index("tensor")
        self.y, self.c = self.t // 2, lax.rem(self.t, 2)
        self.mate_c = (self.f, self.z, self.t + 1 - 2 * self.c)
        self.mate_y = (self.f, self.z, lax.rem(self.t + 2, 4))
        self.mine = (2 * self.c + self.y) * QUARTER
        self.over_y = (2 * self.c + 1 - self.y) * QUARTER
        self.peers_f = [(lax.rem(self.f + j, nf), self.z, self.t) for j in range(1, nf)]
        self.peers_z = [(self.f, lax.rem(self.z + j, 4), self.t) for j in range(1, 4)]
        self.up = (self.f, lax.rem(self.z + 1, 4), self.t)
        self.down = (self.f, lax.rem(self.z + 3, 4), self.t)

    def barrier(self):
        semaphore = pltpu.get_barrier_semaphore()
        everyone = [self.mate_c, self.mate_y] + self.peers_f + self.peers_z
        for peer in everyone:
            pl.semaphore_signal(semaphore, inc=1, device_id=peer, device_id_type=MESH)
        pl.semaphore_wait(semaphore, len(everyone))


def remote(src, dst, pair, mate):
    return pltpu.make_async_remote_copy(
        src, dst, pair[0], pair[1], device_id=mate, device_id_type=MESH
    )


class Ring:
    def __init__(self, at, send, recv_c, send_y, recv_y, sems):
        self.at, self.send, self.recv_c = at, send, recv_c
        self.send_y, self.recv_y, self.sems = send_y, recv_y, sems

    def pair(self, which, s):
        return self.sems.at[which, 0, s], self.sems.at[which, 1, s]

    def rs_core(self, s):
        half = aligned((1 - self.at.c) * HALF, HALF)
        return remote(self.send.at[s, half], self.recv_c.at[s], self.pair(0, s), self.at.mate_c)

    def rs_y(self, s):
        return remote(self.send_y.at[s], self.recv_y.at[s], self.pair(1, s), self.at.mate_y)

    def back_y(self, src, dst, s):
        return remote(
            src, dst.at[s, aligned(self.at.mine, QUARTER)], self.pair(2, s), self.at.mate_y
        )

    def back_own(self, src, dst, s):
        return remote(
            src, dst.at[s, aligned(self.at.mine, QUARTER)], self.pair(3, s), self.at.mate_c
        )

    def back_over(self, dst, s):
        there = dst.at[s, aligned(self.at.over_y, QUARTER)]
        return remote(there, there, self.pair(4, s), self.at.mate_c)

    def step_q(self, s):
        self.rs_core(s).wait()
        self.send_y[s] = (
            self.send[s, aligned(self.at.over_y, QUARTER)].astype(F32)
            + self.recv_c[s, aligned((1 - self.at.y) * QUARTER, QUARTER)].astype(F32)
        ).astype(BF)
        self.rs_y(s).start()

    def total(self, s):
        self.rs_y(s).wait()
        return (
            self.send[s, aligned(self.at.mine, QUARTER)].astype(F32)
            + self.recv_c[s, aligned(self.at.y * QUARTER, QUARTER)].astype(F32)
            + self.recv_y[s].astype(F32)
        )

    def spread(self, src, dst, s):
        self.back_y(src, dst, s).start()
        self.back_own(src, dst, s).start()

    def step_t(self, src, dst, s):
        self.back_y(src, dst, s).wait()
        self.back_over(dst, s).start()

    def step_u(self, src, dst, s):
        self.back_own(src, dst, s).wait()
        self.back_over(dst, s).wait()


def front_kernel(
    nf,
    wqkv_s,
    wout_s,
    wfc1_s,
    wfc2_s,
    tokens,
    teacher,
    cot,
    vec,
    mask,
    segs,
    out_h,
    gmix_h,
    gmid_h,
    gfc1,
    gfc2,
    small,
    att,
    q,
    kv_h,
    lse,
    n1_h,
    wqkv_h,
    wout_h,
    wqkv,
    wout,
    wfc1,
    wfc2,
    n2,
    blk,
    act,
    slope,
    send,
    recv_c,
    send_y,
    recv_y,
    mid,
    gblk,
    tok_q,
    tea_q,
    cot_q,
    stage,
    segk,
    bias,
    kv,
    cnt,
    w_send,
    w_recv,
    w_loc,
    ring_sems,
    q_sems,
    in_sems,
    n1_sem,
    out_sem,
    mix_sem,
    near_sems,
    far_sems,
    cz_sems,
    cf_sems,
    res_sem,
    keep_sem,
):
    at = Place(nf)
    at.barrier()
    ring = Ring(at, send, recv_c, send_y, recv_y, ring_sems)
    mine = aligned(at.mine, QUARTER)

    fs = wout_s.shape[1]
    own = aligned(at.f * fs, fs)
    places = (
        (wqkv_s, wqkv.at[:, own, :]),
        (wout_s, wout.at[:, own]),
        (wfc1_s, wfc1.at[own, :]),
        (wfc2_s, wfc2.at[:, own]),
    )

    def weight_copy(i, j):
        pair = (w_send.at[i, j], w_recv.at[i, j])
        return remote(places[i][0], places[i][1], pair, at.peers_f[j])

    def weight_start(i):
        for j in range(nf - 1):
            weight_copy(i, j).start()
        pltpu.make_async_copy(places[i][0], places[i][1], w_loc.at[i]).start()

    def weight_wait(i):
        pltpu.make_async_copy(places[i][0], places[i][1], w_loc.at[i]).wait()
        for j in range(nf - 1):
            weight_copy(i, j).wait()

    weight_start(0)

    def token_copy(s):
        slot = lax.rem(s, 2)
        return pltpu.make_async_copy(tokens.at[s], stage.at[slot], in_sems.at[slot])

    token_copy(0).start()
    quarters = ((tokens, tok_q), (teacher, tea_q), (cot, cot_q))
    for i, (source, target) in enumerate(quarters):
        pltpu.make_async_copy(source.at[:, mine, :], target, q_sems.at[i]).start()

    masks = mask[...]
    cnt[0] = jnp.broadcast_to(jnp.sum(masks, keepdims=True), (8, 128))

    def count_z(j):
        pair = (cz_sems.at[0, j], cz_sems.at[1, j])
        return remote(cnt.at[0], cnt.at[1 + j], pair, at.peers_z[j])

    def count_f(j):
        pair = (cf_sems.at[0, j], cf_sems.at[1, j])
        return remote(cnt.at[4], cnt.at[5 + j], pair, at.peers_f[j])

    for j in range(3):
        count_z(j).start()

    turned = jnp.transpose(masks)
    segk[...] = jnp.full(segk.shape, -1.0, F32)
    segk[0:4, 1024:3072] = segs[...].astype(F32)
    seg_turned = jnp.transpose(segk[:, aligned(1024 + at.z * GROUP, GROUP)])
    column = lax.broadcasted_iota(jnp.int32, (1, 128), 1)
    for s in range(SEQS):
        lse[s] = jnp.where(column == 4, turned[:, s : s + 1], seg_turned[:, s : s + 1])
    small[...] = jnp.zeros_like(small)
    @pl.when(at.z < 2)
    def _():
        def clear(s, carry):
            kv[s, 0] = jnp.zeros((GROUP, 2 * LOCAL), BF)
            return carry

        lax.fori_loop(0, SEQS, clear, 0)

    @pl.when(at.z < 1)
    def _():
        def clear(s, carry):
            kv[s, 1] = jnp.zeros((GROUP, 2 * LOCAL), BF)
            return carry

        lax.fori_loop(0, SEQS, clear, 0)

    def near_copy(s):
        return remote(
            kv.at[s, 2], kv.at[s, 1], (near_sems.at[0, s], near_sems.at[1, s]), at.up
        )

    def far_copy(s):
        return remote(kv.at[s, 1], kv.at[s, 0], (far_sems.at[0, s], far_sems.at[1, s]), at.up)

    def norm_copy(s):
        return pltpu.make_async_copy(act.at[s], n1_h.at[s], n1_sem.at[s])

    def step_norm(s, carry):
        token_copy(s).wait()

        @pl.when(s < 3)
        def _():
            token_copy(s + 1).start()

        for part in range(2):
            here = pl.ds(part * 256, 256)
            xhat, _ = norm_parts(stage[lax.rem(s, 2), here].astype(F32))
            act[s, here] = (xhat * vec[5:6, :] + vec[6:7, :]).astype(BF)
        norm_copy(s).start()
        return carry

    def step_a(s, carry):
        normed = act[s]
        q[s] = ((matmul(normed, wqkv[0], 1, 0) + vec[7:8, 0:256]) * 0.125).astype(BF)
        kv[s, 2, :, 0:LOCAL] = matmul(normed, wqkv[1], 1, 0).astype(BF)
        kv[s, 2, :, LOCAL:] = (matmul(normed, wqkv[2], 1, 0) + vec[7:8, 256:512]).astype(BF)

        @pl.when(at.z < 3)
        def _():
            near_copy(s).start()

        return carry

    lax.fori_loop(0, SEQS, step_norm, 0)
    weight_wait(0)
    lax.fori_loop(0, SEQS, step_a, 0)
    for i in range(1, 4):
        weight_start(i)
    for j in range(3):
        count_z(j).wait()
    cnt[4] = cnt[0] + cnt[1] + cnt[2] + cnt[3]
    for j in range(nf - 1):
        count_f(j).start()
    for i, (source, target) in enumerate(quarters):
        pltpu.make_async_copy(source.at[:, mine, :], target, q_sems.at[i]).wait()
    for s in range(SEQS):
        norm_copy(s).wait()
    for j in range(nf - 1):
        count_f(j).wait()
    total_count = cnt[4]
    for j in range(nf - 1):
        total_count = total_count + cnt[5 + j]
    small[6:7, 0:128] = total_count[0:1, :]
    cnt[0] = (SEQS * GROUP * nf * 4) / total_count

    def factor():
        return cnt[0, 0:1, 0:1]

    def block_copies(s):
        return (
            pltpu.make_async_copy(teacher.at[s], stage.at[0], in_sems.at[0]),
            pltpu.make_async_copy(cot.at[s], stage.at[1], in_sems.at[1]),
        )

    for copy in block_copies(0):
        copy.start()

    def kv_out(s):
        return pltpu.make_async_copy(kv.at[s], kv_h.at[s], res_sem.at[s])

    def mix_copy(s):
        return pltpu.make_async_copy(tok_q.at[s], gmix_h.at[s, mine], mix_sem.at[s])

    def ends(k, s):
        if k == 2:
            return tok_q.at[s], gmix_h
        target = (n2, blk)[k]
        return target.at[s, mine], target

    def step_r(k, s):
        summed = ring.total(s)
        if k == 0:
            middle = tok_q[s].astype(F32) + summed + vec[0:1, :]
            mid[s] = middle
            xhat, _ = norm_parts(middle)
            n2[s, mine] = (xhat * vec[1:2, :] + vec[2:3, :]).astype(BF)
        elif k == 1:
            block = mid[s] + summed + vec[4:5, :]
            blk[s, mine] = block.astype(BF)
            difference = block - tea_q[s].astype(F32)
            masked = lse[s, mine, 4:5] * difference
            small[5:6, :] += column_sum(masked * difference)
            grad = cot_q[s].astype(F32) + masked * factor()
            gblk[s] = grad
            small[0:1, :] += column_sum(grad)
        else:
            xhat, inverse = norm_parts(mid[s])
            small[1:2, :] += column_sum(summed * xhat)
            small[2:3, :] += column_sum(summed)
            grad = gblk[s] + norm_back(summed, xhat, inverse, vec[1:2, :])
            gblk[s] = grad
            small[3:4, :] += column_sum(grad)
            tok_q[s] = grad.astype(BF)
            mix_copy(s).start()
        ring.spread(*ends(k, s), s)

    def halo(s):
        @pl.when(at.z > 0)
        def _():
            near_copy(s).wait_recv()

        @pl.when((at.z > 0) & (at.z < 3))
        def _():
            far_copy(s).start()

    def step_p0(s):
        @pl.when(at.z < 3)
        def _():
            near_copy(s).wait_send()

        @pl.when((at.z > 0) & (at.z < 3))
        def _():
            far_copy(s).wait_send()

        @pl.when(at.z > 1)
        def _():
            far_copy(s).wait_recv()

        kv_out(s).start()
        lane = lax.broadcasted_iota(jnp.int32, (1, LOCAL), 1) // HD
        slot = lax.broadcasted_iota(jnp.int32, (1, 128), 1)
        keys = kv.at[s].reshape(3 * GROUP, 2 * LOCAL)
        here_segs = segk.at[:, aligned(at.z * GROUP, 3 * GROUP)]
        which = lax.broadcasted_iota(jnp.int32, (8, SPAN), 0) == s

        def block(b, carry):
            start = pl.multiple_of(b * HALF, HALF)
            here = pl.ds(start, HALF)
            span = pl.ds(start, SPAN)
            seg_row = jnp.sum(
                jnp.where(which, here_segs[:, span], 0.0), axis=0, keepdims=True
            )
            columns = lse[s, here]
            bias[...] = allowed_bias(columns[:, 5:6], seg_row)
            query = q[s, here]
            k_block = keys[span, 0:LOCAL]
            v_block = keys[span, LOCAL:]
            mixed = jnp.zeros((HALF, LOCAL), F32)
            logs = columns
            for h in range(LOCAL // HD):
                one = jnp.where(lane == h, query, jnp.zeros_like(query))
                scores = matmul(one, k_block, 1, 1) + bias[...]
                top = jnp.max(scores, axis=-1, keepdims=True)
                weights = jnp.exp(scores - top)
                whole = jnp.sum(weights, axis=-1, keepdims=True)
                part = matmul(weights.astype(BF), v_block, 1, 0) / whole
                mixed = jnp.where(lane == h, part, mixed)
                logs = jnp.where(slot == h, top + jnp.log(whole), logs)
            att[s, here] = mixed.astype(BF)
            lse[s, here] = logs
            return carry

        lax.fori_loop(0, 2, block, 0)
        send[s] = matmul(att[s], wout[...], 1, 0).astype(BF)
        ring.rs_core(s).start()

    def step_p1(s):
        ring.step_u(*ends(0, s), s)
        for part in range(2):
            here = pl.ds(part * 256, 256)
            h = matmul(n2[s, here], wfc1[...], 1, 0) + vec[3:4, :]
            t = jnp.tanh(0.7978845608028654 * (h + 0.044715 * h * h * h))
            act[s, here] = (0.5 * h * (1.0 + t)).astype(BF)
            slope[s, here] = (
                0.5 * (1.0 + t)
                + 0.5 * h * (1.0 - t * t) * (0.7978845608028654 * (1.0 + 0.134145 * h * h))
            ).astype(BF)
        send[s] = matmul(act[s], wfc2[...], 1, 0).astype(BF)
        ring.rs_core(s).start()

    def step_p2(s):
        ring.step_u(*ends(1, s), s)
        out = pltpu.make_async_copy(blk.at[s], out_h.at[s], out_sem)
        out.start()
        for copy in block_copies(s):
            copy.wait()
        out.wait()
        for part in range(2):
            here = pl.ds(part * 256, 256)
            difference = blk[s, here].astype(F32) - stage[0, here].astype(F32)
            scaled = lse[s, here, 4:5] * factor()
            down = (stage[1, here].astype(F32) + scaled * difference).astype(BF)
            blk[s, here] = down
            up = matmul(down, wfc2[...], 1, 1) * slope[s, here].astype(F32)
            rounded = up.astype(BF)
            slope[s, here] = rounded
            small[4:5, :] += column_sum(rounded.astype(F32))

        @pl.when(s < 3)
        def _():
            for copy in block_copies(s + 1):
                copy.start()

        send[s] = matmul(slope[s], wfc1[...], 1, 1).astype(BF)
        ring.rs_core(s).start()

    steps_p = (step_p0, step_p1, step_p2)

    def inside(s, action):
        @pl.when((s >= 0) & (s < SEQS))
        def _():
            action(s)

    halo(0)

    def wave(m, carry):
        for k in range(3):
            for lag in (3, 2):
                kind = (k - lag) % 3
                s = m + (k - lag - kind) // 3 - kind
                if lag == 3:
                    inside(s, lambda s: ring.step_t(*ends(kind, s), s))
                else:
                    inside(s, lambda s: step_r(kind, s))
            if k == 0:
                inside(m + 1, halo)

                @pl.when(m == 0)
                def _():
                    weight_wait(1)

            if k == 1:

                @pl.when(m == 1)
                def _():
                    weight_wait(2)
                    weight_wait(3)

            inside(m - k, steps_p[k])
            inside(m - k, ring.step_q)
        return carry

    lax.fori_loop(0, 7, wave, 0)
    deep = lambda ref: ref.reshape(SEQS * GROUP, 1024)
    last = pltpu.make_async_copy(gblk, gmid_h, out_sem)
    last.start()
    kept = (
        pltpu.make_async_copy(wqkv, wqkv_h, keep_sem.at[0]),
        pltpu.make_async_copy(wout, wout_h, keep_sem.at[1]),
    )
    for copy in kept:
        copy.start()
    deep(send)[0:1024, :] = matmul(deep(act)[...], deep(blk)[...], 0, 0).astype(BF)
    down_out = pltpu.make_async_copy(deep(send).at[0:1024], gfc2, in_sems.at[0])
    down_out.start()
    deep(send)[1024:2048, :] = matmul(deep(n2)[...], deep(slope)[...], 0, 0).astype(BF)
    up_out = pltpu.make_async_copy(deep(send).at[1024:2048], gfc1, in_sems.at[1])
    up_out.start()
    for s in range(SEQS):
        ring.step_u(*ends(2, s), s)
        mix_copy(s).wait()
        kv_out(s).wait()
    last.wait()
    down_out.wait()
    up_out.wait()
    for copy in kept:
        copy.wait()


def front_call(nf, *args):
    anys = pl.BlockSpec(memory_space=pl.ANY)
    vmem = pl.BlockSpec(memory_space=pltpu.VMEM)
    dma = pltpu.SemaphoreType.DMA
    big = lambda *lead: pltpu.VMEM((*lead, GROUP, 1024), BF)
    shape = jax.ShapeDtypeStruct
    return pl.pallas_call(
        functools.partial(front_kernel, nf),
        out_shape=(
            shape((SEQS, GROUP, 1024), BF),
            shape((SEQS, GROUP, 1024), BF),
            shape((SEQS, QUARTER, 1024), F32),
            shape((1024, 1024), BF),
            shape((1024, 1024), BF),
            shape((8, 1024), F32),
            shape((SEQS, GROUP, LOCAL), BF),
            shape((SEQS, GROUP, LOCAL), BF),
            shape((SEQS, 3, GROUP, 2 * LOCAL), BF),
            shape((SEQS, GROUP, 128), F32),
            shape((SEQS, GROUP, 1024), BF),
            shape((3, 1024, LOCAL), BF),
            shape((LOCAL, 1024), BF),
        ),
        in_specs=[anys] * 7 + [vmem] * 3,
        out_specs=(anys, anys, anys, anys, anys, vmem, vmem, vmem, anys, vmem, anys, anys, anys),
        scratch_shapes=[
            pltpu.VMEM((3, 1024, LOCAL), BF),
            pltpu.VMEM((LOCAL, 1024), BF),
            pltpu.VMEM((1024, 1024), BF),
            pltpu.VMEM((1024, 1024), BF),
            big(SEQS),
            big(SEQS),
            big(SEQS),
            big(SEQS),
            big(SEQS),
            pltpu.VMEM((SEQS, HALF, 1024), BF),
            pltpu.VMEM((SEQS, QUARTER, 1024), BF),
            pltpu.VMEM((SEQS, QUARTER, 1024), BF),
            pltpu.VMEM((SEQS, QUARTER, 1024), F32),
            pltpu.VMEM((SEQS, QUARTER, 1024), F32),
            pltpu.VMEM((SEQS, QUARTER, 1024), BF),
            pltpu.VMEM((SEQS, QUARTER, 1024), BF),
            pltpu.VMEM((SEQS, QUARTER, 1024), BF),
            big(2),
            pltpu.VMEM((8, 3072), F32),
            pltpu.VMEM((HALF, SPAN), F32),
            pltpu.VMEM((SEQS, 3, GROUP, 2 * LOCAL), BF),
            pltpu.VMEM((4 + nf, 8, 128), F32),
            dma((4, nf - 1)),
            dma((4, nf - 1)),
            dma((4,)),
            dma((5, 2, SEQS)),
            dma((3,)),
            dma((2,)),
            dma((SEQS,)),
            dma,
            dma((SEQS,)),
            dma((2, SEQS)),
            dma((2, SEQS)),
            dma((2, 3)),
            dma((2, nf - 1)),
            dma((SEQS,)),
            dma((2,)),
        ],
        compiler_params=pltpu.CompilerParams(
            collective_id=1, has_side_effects=True, vmem_limit_bytes=63 * 2**20
        ),
        cost_estimate=pl.CostEstimate(
            flops=2 * 2048 * 1024 * 1024 * 9, bytes_accessed=30 * 2**20, transcendentals=0
        ),
        name="front",
    )(*args)


class Reduce:
    def __init__(self, at, cut, size, rows, full, arrived, shard, half, quarter, sems):
        self.at, self.cut, self.size, self.rows = at, cut, size, rows
        self.full, self.arrived, self.shard = full, arrived, shard
        self.half, self.quarter = half, quarter
        self.x_sems, self.z_sems = sems
        self.a, self.b = lax.rem(at.z, 2), at.z // 2
        self.side = (at.f, at.z + 1 - 2 * self.a, at.t)
        self.across = (at.f, lax.rem(at.z + 2, 4), at.t)

    def own(self, f):
        return self.cut(self.full, aligned(f * self.size, self.size, math.gcd(self.size, 128)))

    def part(self, ref, start, size):
        where = aligned(start, size, 16)
        return ref.at[:, where, :] if len(ref.shape) == 3 else ref.at[where, :]

    def x_copy(self, j):
        there = lax.rem(self.at.f + 1 + j, self.at.nf)
        pair = (self.x_sems.at[0, j], self.x_sems.at[1, j])
        return remote(self.own(there), self.arrived.at[j], pair, self.at.peers_f[j])

    def z_copy(self, stage):
        h, q = self.rows // 2, self.rows // 4
        pair = (self.z_sems.at[0, stage], self.z_sems.at[1, stage])
        own = self.own(self.at.f)
        if stage == 0:
            return remote(self.part(own, (1 - self.a) * h, h), self.half, pair, self.side)
        if stage == 1:
            src = self.part(own, self.a * h + (1 - self.b) * q, q)
            return remote(src, self.quarter, pair, self.across)
        if stage == 2:
            kept = self.part(self.shard, self.a * h + self.b * q, q)
            return remote(kept, kept, pair, self.across)
        kept = self.part(self.shard, self.a * h, h)
        return remote(kept, kept, pair, self.side)

    def add(self, target, first, others):
        total = first[...].astype(F32)
        for other in others:
            total = total + other[...].astype(F32)
        target[...] = total.astype(BF)

    def run(self, stage):
        h, q = self.rows // 2, self.rows // 4
        peers = range(self.at.nf - 1)
        own = self.own(self.at.f)
        if stage == 0:
            for j in peers:
                self.x_copy(j).start()
            return
        if stage == 1:
            for j in peers:
                self.x_copy(j).wait()
            self.add(own, own, [self.arrived.at[j] for j in peers])
        else:
            self.z_copy(stage - 2).wait()
        if stage == 2:
            kept = self.part(own, self.a * h, h)
            self.add(kept, kept, [self.half])
        elif stage == 3:
            start = self.a * h + self.b * q
            self.add(self.part(self.shard, start, q), self.part(own, start, q), [self.quarter])
        if stage < 5:
            self.z_copy(stage - 1).start()


def back_kernel(
    nf,
    gmix_h,
    gmid_h,
    gfc1_h,
    gfc2_h,
    att,
    q,
    kv_h,
    lse,
    n1_h,
    tokens,
    wqkv,
    wout,
    vec,
    segs,
    ig_h,
    small,
    s_qkv,
    s_out,
    s_fc1,
    s_fc2,
    gm,
    kvs,
    n1s,
    ga,
    dots,
    bias,
    segk,
    dkvt,
    dfar,
    dnear,
    down,
    m1,
    m2,
    gq,
    send,
    recv_c,
    send_y,
    recv_y,
    gmid,
    tok_q,
    a_qkv,
    a_out,
    f_qkv,
    f_fc1,
    f_fc2,
    x_qkv,
    x_out,
    x_fc1,
    x_fc2,
    h_qkv,
    h_out,
    h_fc1,
    h_fc2,
    k_qkv,
    k_out,
    k_fc1,
    k_fc2,
    ring_sems,
    load_sems,
    first_sems,
    m1_sems,
    m2_sems,
    red_x,
    red_z,
):
    at = Place(nf)
    at.barrier()
    ring = Ring(at, send, recv_c, send_y, recv_y, ring_sems)
    mine = aligned(at.mine, QUARTER)
    rows_cut = lambda ref, where: ref.at[where, :]
    cols_cut = lambda ref, where: ref.at[:, where]
    deep_cut = lambda ref, where: ref.at[:, where, :]
    fs = 1024 // nf
    f_out = gm.at[0:LOCAL]

    def reducer(i, cut, rows, full, arrived, shard, half, quarter):
        sems = (red_x.at[i], red_z.at[i])
        return Reduce(at, cut, fs, rows, full, arrived, shard, half, quarter, sems)

    red_qkv = reducer(0, deep_cut, fs, f_qkv, x_qkv, s_qkv, h_qkv, k_qkv)
    red_out = reducer(1, cols_cut, LOCAL, f_out, x_out, s_out, h_out, k_out)
    red_fc1 = reducer(2, rows_cut, fs, f_fc1, x_fc1, s_fc1, h_fc1, k_fc1)
    red_fc2 = reducer(3, cols_cut, 1024, f_fc2, x_fc2, s_fc2, h_fc2, k_fc2)

    firsts = (
        (gfc1_h, f_fc1),
        (gfc2_h, f_fc2),
        (gmid_h.at[0], gmid),
        (tokens.at[:, mine, :], tok_q),
    )

    def first_copy(i):
        return pltpu.make_async_copy(firsts[i][0], firsts[i][1], first_sems.at[i])

    def load_copies(s):
        return (
            pltpu.make_async_copy(gmix_h.at[s], gm, load_sems.at[0, 0]),
            pltpu.make_async_copy(kv_h.at[s], kvs, load_sems.at[1, 0]),
        )

    def norm_load(s):
        return pltpu.make_async_copy(n1_h.at[s], n1s, load_sems.at[2, 0])

    def mid_load(s):
        return pltpu.make_async_copy(gmid_h.at[s], gmid, load_sems.at[2, 1])

    for copy in load_copies(0):
        copy.start()
    for i in range(4):
        first_copy(i).start()
    norm_load(0).start()

    segk[...] = jnp.full(segk.shape, -1.0, F32)
    segk[0:4, 1024:3072] = segs[...].astype(F32)
    small[...] = jnp.zeros_like(small)
    a_qkv[...] = jnp.zeros_like(a_qkv)
    a_out[...] = jnp.zeros_like(a_out)
    def m1_copy(s):
        return remote(dfar.at[s], m1.at[s], (m1_sems.at[0, s], m1_sems.at[1, s]), at.down)

    def m2_copy(s):
        return remote(dnear.at[s], m2.at[s], (m2_sems.at[0, s], m2_sems.at[1, s]), at.down)

    def step_e(s):
        for copy in load_copies(s):
            copy.wait()

        ga[...] = matmul(gm[...], wout[...], 1, 1).astype(BF)
        a_out[...] += matmul(att[s], gm[...], 0, 0)

        lane = lax.broadcasted_iota(jnp.int32, (1, LOCAL), 1) // HD
        keys = kvs.reshape(3 * GROUP, 2 * LOCAL)
        here_segs = segk.at[:, aligned(at.z * GROUP, 3 * GROUP)]
        which = lax.broadcasted_iota(jnp.int32, (8, SPAN), 0) == s
        dkvt[...] = jnp.zeros_like(dkvt)

        def block(b, carry):
            start = pl.multiple_of(b * HALF, HALF)
            here = pl.ds(start, HALF)
            span = pl.ds(start, SPAN)
            seg_row = jnp.sum(
                jnp.where(which, here_segs[:, span], 0.0), axis=0, keepdims=True
            )
            logs = lse[s, here]
            bias[...] = allowed_bias(logs[:, 5:6], seg_row)
            query = q[s, here]
            grad = ga[here]
            k_block = keys[span, 0:LOCAL]
            v_block = keys[span, LOCAL:]
            dots[0] = jnp.transpose(query)
            dots[1] = jnp.transpose(grad)
            product = grad.astype(F32) * att[s, here].astype(F32)
            grad_query = jnp.zeros((HALF, LOCAL), F32)
            for h in range(LOCAL // HD):
                mine_h = lane == h
                one = jnp.where(mine_h, query, jnp.zeros_like(query))
                grad_one = jnp.where(mine_h, grad, jnp.zeros_like(grad))
                delta = jnp.sum(jnp.where(mine_h, product, 0.0), axis=-1, keepdims=True)
                scores = matmul(one, k_block, 1, 1) + bias[...]
                probs = jnp.exp(scores - logs[:, h : h + 1])
                dprobs = matmul(grad_one, v_block, 1, 1)
                grad_scores = (probs * (dprobs - delta)).astype(BF)
                grad_query = jnp.where(mine_h, matmul(grad_scores, k_block, 1, 0), grad_query)
                k_rows = pl.ds(h * HD, HD)
                v_rows = pl.ds(LOCAL + h * HD, HD)
                dkvt[k_rows, span] += matmul(dots[0, k_rows], grad_scores, 1, 0)
                dkvt[v_rows, span] += matmul(dots[1, k_rows], probs.astype(BF), 1, 0)
            gq[s, here] = (grad_query * 0.125).astype(BF)
            return carry

        lax.fori_loop(0, 2, block, 0)

        @pl.when(s < 3)
        def _():
            for copy in load_copies(s + 1):
                copy.start()

        for i, target in enumerate((dfar, dnear, down)):
            target[s] = jnp.transpose(dkvt[:, i * GROUP : (i + 1) * GROUP].astype(BF))

        @pl.when(at.z > 1)
        def _():
            m1_copy(s).start()

    def step_i(s):
        @pl.when((at.z > 0) & (at.z < 3))
        def _():
            m1_copy(s).wait_recv()
            dnear[s] = (dnear[s].astype(F32) + m1[s].astype(F32)).astype(BF)

        @pl.when(at.z > 0)
        def _():
            m2_copy(s).start()

    def step_f(s):
        @pl.when(at.z < 3)
        def _():
            m2_copy(s).wait_recv()
            down[s] = (down[s].astype(F32) + m2[s].astype(F32)).astype(BF)

        norm_load(s).wait()
        grads = (gq[s], down[s, :, 0:LOCAL], down[s, :, LOCAL:])
        send[s] = (
            matmul(grads[0], wqkv[0], 1, 1)
            + matmul(grads[1], wqkv[1], 1, 1)
            + matmul(grads[2], wqkv[2], 1, 1)
        ).astype(BF)
        ring.rs_core(s).start()
        normed = n1s[...]
        for i in range(3):
            a_qkv[i] += matmul(normed, grads[i], 0, 0)

        @pl.when(s < 3)
        def _():
            norm_load(s + 1).start()

        small[2:3, 0:LOCAL] += column_sum(grads[0].astype(F32))
        small[2:3, LOCAL : 2 * LOCAL] += column_sum(grads[2].astype(F32))

    def ends(s):
        return tok_q.at[s], ig_h

    def ig_copy(s):
        return pltpu.make_async_copy(tok_q.at[s], ig_h.at[s, mine], first_sems.at[s])

    def step_r(s):
        summed = ring.total(s)
        xhat, inverse = norm_parts(tok_q[s].astype(F32))
        small[0:1, :] += column_sum(summed * xhat)
        small[1:2, :] += column_sum(summed)
        @pl.when(s > 0)
        def _():
            mid_load(s).wait()

        grad = gmid[...] + norm_back(summed, xhat, inverse, vec[5:6, :])
        tok_q[s] = grad.astype(BF)

        @pl.when(s < 3)
        def _():
            mid_load(s + 1).start()

        ig_copy(s).start()
        ring.spread(*ends(s), s)

    def inside(s, action):
        @pl.when((s >= 0) & (s < SEQS))
        def _():
            action(s)

    for i in range(4):
        first_copy(i).wait()
    red_fc1.run(0)
    red_fc2.run(0)

    def wave(m, carry):
        inside(m, step_e)
        inside(m - 1, step_i)
        inside(m - 4, lambda s: ring.step_t(*ends(s), s))
        inside(m - 3, step_r)
        inside(m - 2, step_f)
        inside(m - 2, ring.step_q)
        return carry

    lax.fori_loop(0, 6, wave, 0)
    f_out[...] = a_out[...].astype(BF)
    f_qkv[...] = a_qkv[...].astype(BF)
    red_out.run(0)
    red_qkv.run(0)
    for reduce in (red_fc1, red_fc2):
        reduce.run(1)
    ring.step_t(*ends(2), 2)
    step_r(3)
    for reduce in (red_out, red_qkv):
        reduce.run(1)
    ring.step_t(*ends(3), 3)
    for stage in (2, 3, 4, 5):
        for reduce in (red_fc1, red_fc2, red_out, red_qkv):
            reduce.run(stage)
    for s in range(SEQS):
        ring.step_u(*ends(s), s)
        ig_copy(s).wait()

        @pl.when(at.z > 1)
        def _():
            m1_copy(s).wait_send()

        @pl.when(at.z > 0)
        def _():
            m2_copy(s).wait_send()


def back_call(nf, *args):
    anys = pl.BlockSpec(memory_space=pl.ANY)
    vmem = pl.BlockSpec(memory_space=pltpu.VMEM)
    dma = pltpu.SemaphoreType.DMA
    big = lambda *lead: pltpu.VMEM((*lead, GROUP, 1024), BF)
    shape = jax.ShapeDtypeStruct
    fs = 1024 // nf
    low = lambda *dims: pltpu.VMEM(dims, BF)
    return pl.pallas_call(
        functools.partial(back_kernel, nf),
        out_shape=(
            shape((SEQS, GROUP, 1024), BF),
            shape((8, 1024), F32),
            shape((3, fs, LOCAL), BF),
            shape((LOCAL, fs), BF),
            shape((fs, 1024), BF),
            shape((1024, fs), BF),
        ),
        in_specs=[anys] * 4 + [vmem, vmem, anys, vmem, anys, anys, vmem, vmem, vmem, vmem],
        out_specs=(anys, vmem, vmem, vmem, vmem, vmem),
        scratch_shapes=[
            low(GROUP, 1024),
            low(3, GROUP, 2 * LOCAL),
            low(GROUP, 1024),
            low(GROUP, LOCAL),
            low(2, LOCAL, HALF),
            pltpu.VMEM((HALF, SPAN), F32),
            pltpu.VMEM((8, 3072), F32),
            pltpu.VMEM((2 * LOCAL, 3 * GROUP), F32),
            low(SEQS, GROUP, 2 * LOCAL),
            low(SEQS, GROUP, 2 * LOCAL),
            low(SEQS, GROUP, 2 * LOCAL),
            low(SEQS, GROUP, 2 * LOCAL),
            low(SEQS, GROUP, 2 * LOCAL),
            low(SEQS, GROUP, LOCAL),
            big(SEQS),
            low(SEQS, HALF, 1024),
            low(SEQS, QUARTER, 1024),
            low(SEQS, QUARTER, 1024),
            pltpu.VMEM((QUARTER, 1024), F32),
            low(SEQS, QUARTER, 1024),
            pltpu.VMEM((3, 1024, LOCAL), F32),
            pltpu.VMEM((LOCAL, 1024), F32),
            low(3, 1024, LOCAL),
            low(1024, 1024),
            low(1024, 1024),
            low(nf - 1, 3, fs, LOCAL),
            low(nf - 1, LOCAL, fs),
            low(nf - 1, fs, 1024),
            low(nf - 1, 1024, fs),
            low(3, fs // 2, LOCAL),
            low(LOCAL // 2, fs),
            low(fs // 2, 1024),
            low(512, fs),
            low(3, fs // 4, LOCAL),
            low(LOCAL // 4, fs),
            low(fs // 4, 1024),
            low(256, fs),
            dma((5, 2, SEQS)),
            dma((3, 2)),
            dma((4,)),
            dma((2, SEQS)),
            dma((2, SEQS)),
            dma((4, 2, nf - 1)),
            dma((4, 2, 4)),
        ],
        compiler_params=pltpu.CompilerParams(
            collective_id=2, has_side_effects=True, vmem_limit_bytes=63 * 2**20
        ),
        cost_estimate=pl.CostEstimate(
            flops=2 * 2048 * 1024 * 1024 * 6, bytes_accessed=30 * 2**20, transcendentals=0
        ),
        name="back",
    )(*args)


def local(
    tokens,
    cotangent,
    teacher,
    valid_mask,
    segment_ids,
    ln1_gain,
    ln1_bias,
    w_qkv,
    b_qv,
    w_out,
    b_out,
    ln2_gain,
    ln2_bias,
    w_fc1,
    b_fc1,
    w_fc2,
    b_fc2,
):
    nf = lax.axis_size("fsdp")
    pieces = (b_out, ln2_gain, ln2_bias, b_fc2, ln1_gain, ln1_bias, b_qv, b_fc1)
    flat = lax.all_gather(jnp.concatenate([piece.reshape(-1) for piece in pieces]), "fsdp", axis=0)
    flat = flat.astype(F32)
    wide = b_out.shape[0]
    rows = [flat[:, i * wide : (i + 1) * wide].reshape(1, D) for i in range(6)]
    small_qv = flat[:, 6 * wide : 6 * wide + b_qv.size].reshape(nf, *b_qv.shape)
    small_up = flat[:, 6 * wide + b_qv.size :].reshape(nf, *b_fc1.shape)
    bias_qv = jnp.moveaxis(small_qv, 0, 2).reshape(1, 2 * LOCAL)
    bias_up = jnp.moveaxis(small_up, 0, 1).reshape(1, D)
    vec = jnp.concatenate(
        rows[:3]
        + [bias_up]
        + rows[3:]
        + [jnp.concatenate([bias_qv, jnp.zeros((1, D - 2 * LOCAL), F32)], axis=1)],
        axis=0,
    )
    mask_f = jnp.concatenate([valid_mask, jnp.zeros_like(valid_mask)], axis=0).astype(F32)
    front = front_call(
        nf, w_qkv, w_out, w_fc1, w_fc2, tokens, teacher, cotangent, vec, mask_f, segment_ids
    )
    (output, grad_mix, grad_middle, gfc1, gfc2, sums_one, att, q, kv, lse, n1, wqkv, wout) = front
    input_grad, sums_two, s_qkv, s_out, s_fc1, s_fc2 = back_call(
        nf, grad_mix, grad_middle, gfc1, gfc2, att, q, kv, lse, n1, tokens, wqkv, wout, vec, segment_ids
    )
    place_f = lax.axis_index("fsdp")
    place_t = lax.axis_index("tensor")
    by_tensor = jnp.stack([sums_one[4], sums_two[2]])
    slots = jnp.where(jnp.arange(4)[:, None, None] == place_t, by_tensor[None], 0.0)
    everything = jnp.concatenate([sums_one[0:4], sums_one[5:6], sums_two[0:2], slots.reshape(8, D)])
    everything = lax.psum(everything, ("fsdp", "context", "tensor"))
    loss = jnp.sum(everything[4]) / (2.0 * D * sums_one[6, 0])
    ours = lax.dynamic_index_in_dim(everything[7:].reshape(4, 2, D), place_t, 0, keepdims=False)
    part = lax.dynamic_slice_in_dim(everything[0:7], place_f * wide, wide, 1)
    grad_up = ours[0].reshape(b_fc1.shape[0], -1)
    grad_up = lax.dynamic_slice_in_dim(grad_up, place_f * b_fc1.shape[1], b_fc1.shape[1], 1)
    grad_qv = ours[1, : 2 * LOCAL].reshape(2, LOCAL // HD, HD)
    grad_qv = lax.dynamic_slice_in_dim(grad_qv, place_f * b_qv.shape[2], b_qv.shape[2], 2)
    return (
        output,
        loss,
        input_grad,
        part[5],
        part[6],
        s_qkv.astype(F32),
        grad_qv,
        s_out.astype(F32),
        part[3],
        part[1],
        part[2],
        s_fc1.astype(F32),
        grad_up,
        s_fc2.astype(F32),
        part[0],
    )


def solution(mesh):
    return jax.shard_map(
        local,
        mesh=mesh,
        in_specs=(
            P("fsdp", "context", None),
            P("fsdp", "context", None),
            P("fsdp", "context", None),
            P("fsdp", "context"),
            P("fsdp", None),
            P("fsdp"),
            P("fsdp"),
            P(None, "fsdp", "tensor"),
            P(None, "tensor", "fsdp"),
            P("tensor", "fsdp"),
            P("fsdp"),
            P("fsdp"),
            P("fsdp"),
            P("fsdp", "tensor"),
            P("tensor", "fsdp"),
            P("tensor", "fsdp"),
            P("fsdp"),
        ),
        out_specs=(
            P("fsdp", "context", None),
            P(),
            P("fsdp", "context", None),
            P("fsdp"),
            P("fsdp"),
            P(None, "fsdp", "tensor"),
            P(None, "tensor", "fsdp"),
            P("tensor", "fsdp"),
            P("fsdp"),
            P("fsdp"),
            P("fsdp"),
            P("fsdp", "tensor"),
            P("tensor", "fsdp"),
            P("tensor", "fsdp"),
            P("fsdp"),
        ),
        check_vma=False,
    )
```

time: 1290 us -> 600 us (0.47)
  waiting for transfers between devices: 689 us -> 0 us
  Pallas kernels: 0 us -> 523 us
  matrix products: 212 us -> 0 us
  other arithmetic: 150 us -> 9.57 us
  local copies, waits for them, and re-layouts: 86.1 us -> 20.4 us
  blocking collectives: 106 us -> 42.9 us
  starting transfers between devices: 19.3 us -> 0 us
  between operations: 18.9 us -> 3.29 us
    pallas_call x0 -> x2, Pallas kernels: none -> 523 us  [the longest x1 267 us: front_call(): pl.pallas_call(functools.partial(front_kernel, nf), out_shape=(shape((SEQ...]
    psum x5 -> x0, waiting for transfers between devices: 352 us -> none  [the longest x4 298 us: row_total(): return lax.psum(term.astype(jnp.bfloat16), 'tensor').astype(jnp.float32)]
    dot_general x40 -> x0, matrix products: 212 us -> none  [the longest x8 36.7 us: masked_scores(): jnp.einsum('qhe,khe->hqk', query_one, keys_one, preferred_element_type=jn...]
    ppermute x8 -> x0, waiting for transfers between devices: 174 us -> none  [passed_along(): return lax.ppermute(block, axis, route)]
    reduce_scatter x4 -> x0, waiting for transfers between devices: 111 us -> none  [the longest x1 34.8 us: local(): lax.psum_scatter(gradients[10].astype(jnp.bfloat16), 'fsdp', scatter_dime...]
    reduce_sum x20 -> x1, other arithmetic: 88.4 us -> 0.61 us  [local(): loss = jnp.sum(everything[4]) / (2.0 * D * sums_one[6, 0])]
    all_gather x3 -> x0, waiting for transfers between devices: 50 us -> none  [the longest x1 24.2 us: local(): lax.all_gather(w_fc1, 'fsdp', axis=0, tiled=True)]
    all_gather x9 -> x1, blocking collectives: 44.3 us -> 5.32 us  [local(): lax.all_gather(jnp.concatenate([piece.reshape(-1) for piece in pieces]),...]
  transfers between devices with their start and end apart: 22 -> 0, of which waited for: 18 -> 0; matrix products, arithmetic and copies ran while one was open for 13% -> 0% of each run, Pallas kernels for 0% -> 0%
where the time goes in v2:
time: 600 us; the launch traced here: 599 us
  Pallas kernels  523 us (87%)
  blocking collectives  42.9 us (7%)
  local copies, waits for them, and re-layouts  20.4 us (3%)
  other arithmetic  9.57 us (2%)
    pallas_call x1, Pallas kernels, front_call(): pl.pallas_call(functools.partial(front_kernel, nf), out_shape=(shape((SEQ...  267 us
    pallas_call x1, Pallas kernels, back_call(): pl.pallas_call(functools.partial(back_kernel, nf), out_shape=(shape((SEQS...  256 us
    psum x1, blocking collectives, local(): everything = lax.psum(everything, ('fsdp', 'context', 'tensor'))  37.6 us

profile of v2, /device:TPU:0, one launch (start us, length us, event | category | flops | bytes accessed | tf_op | source)
XLA Modules:
  0.0 598.7 jit_solution(16294315419306136511)
XLA Ops:
  0.8 0.8 reshape.82
  1.6 0.9 dynamic-update-slice
  2.5 0.9 dynamic-update-slice.1
  3.3 0.9 dynamic-update-slice.2
  4.2 0.9 dynamic-update-slice.3
  5.0 0.9 dynamic-update-slice.4
  5.9 0.9 dynamic-update-slice.5
  6.9 0.9 dynamic-update-slice.7
  7.8 5.3 all-gather.1
  14.1 1.3 pad_convert_fusion.mask
  15.4 266.6 %front.1 = (bf16[4,512,1024]{2,1,0:T(8,128)(2,1)}, bf16[4,512,1024]{2,1,0:T(8,128)(2,1)}, f32[4,128,1024]{2,1,0:T(8,128)}, bf16[1024,1024]{1,0:T(8,128)(2,1)}, b...) custom-call(bf16[3,512,256]{2,1,0:T(8,128)(2,1)} %wqkv_s.1, ...), custom_call_target="tpu_custom_call" | custom-call | flops 38654705664 | bytes 31457280 | tf_op jit(solution)/shard_map/front/pallas_call | solution.py:572
  282.1 1.2 slice.90
  283.9 0.8 fusion
  284.8 0.8 slice.84
  285.5 255.9 %back.1 = (bf16[4,512,1024]{2,1,0:T(8,128)(2,1)}, f32[8,1024]{1,0:T(8,128)}, bf16[3,512,256]{2,1,0:T(8,128)(2,1)}, bf16[256,512]{1,0:T(8,128)(2,1)}, bf16[512,10...) custom-call(bf16[4,512,1024]{2,1,0:T(8,128)(2,1)} %get-tuple-element.36.gmix_h, f32[4,128,1024]{2,1,0:T(8,128)} %get-tuple-element.37.gmid_h, ...), custom_call_target="tpu_custom_call" | custom-call | flops 25769803776 | bytes 31457280 | tf_op jit(solution)/shard_map/back/pallas_call | solution.py:1008
  541.4 0.9 slice.88
  543.3 37.6 %psum.7 = f32[15,1024]{1,0:T(8,128)S(1)} all-reduce(f32[15,1024]{1,0:T(8,128)S(1)} %pad_maximum_fusion), channel_id=1, replica_groups=mesh['fsdp'=2,'context'=4,'tensor'=4] {'fsdp','context','tensor'}, use_global_device_ids=true, to_apply=%region_0.1 | all-reduce | flops 15360 | bytes 122880 | tf_op jit(solution)/shard_map/psum | solution.py:1125
  584.3 1.8 convert_element_type.21
  586.1 2.6 convert_element_type.20
  588.7 1.6 convert_element_type.22
  590.3 1.6 convert_element_type.23
  591.9 2.1 copy.56
  594.0 1.6 copy-done.1
  595.6 2.0 copy.57
  (45 shorter events, 4.9 us)
Async XLA Ops:
  541.4 47.3 %copy-start.3 = (bf16[512,1024]{1,0:T(8,128)(2,1)S(1)}, bf16[512,1024]{1,0:T(8,128)(2,1)}, u32[]{:S(2)}) copy-start(bf16[512,1024]{1,0:T(8,128)(2,1)} %get-tuple-element.51) | copy-start | bytes 3145732
  541.4 48.8 %copy-start.2 = (bf16[1024,512]{1,0:T(8,128)(2,1)S(1)}, bf16[1024,512]{1,0:T(8,128)(2,1)}, u32[]{:S(2)}) copy-start(bf16[1024,512]{1,0:T(8,128)(2,1)} %get-tuple-element.52) | copy-start | bytes 3145732
  586.1 5.7 copy-start
  591.9 3.7 copy-start.1

commit v3 on v2

--- a/solution.py
+++ b/solution.py
@@ -92,6 +92,26 @@
     )
 
 
+def run_order(actions, order):
+    names = list(actions)
+    codes = [names.index(name) * 8 + s for name, s in order]
+
+    def step(i, carry):
+        code = jnp.int32(codes[0])
+        for j, other in enumerate(codes[1:]):
+            code = jnp.where(i == j + 1, other, code)
+        kind, s = code // 8, lax.rem(code, 8)
+        for j, name in enumerate(names):
+
+            @pl.when(kind == j)
+            def _(action=actions[name]):
+                action(s)
+
+        return carry
+
+    lax.fori_loop(0, len(order), step, 0)
+
+
 class Ring:
     def __init__(self, at, send, recv_c, send_y, recv_y, sems):
         self.at, self.send, self.recv_c = at, send, recv_c
@@ -148,6 +168,72 @@
     def step_u(self, src, dst, s):
         self.back_own(src, dst, s).wait()
         self.back_over(dst, s).wait()
+
+
+FRONT_ORDER = (
+    ("A", 0),
+    ("A", 1),
+    ("A", 2),
+    ("A", 3),
+    ("C", 0),
+    ("H", 0),
+    ("V", 0),
+    ("P0", 0),
+    ("Q", 0),
+    ("H", 1),
+    ("R0", 0),
+    ("P0", 1),
+    ("T0", 0),
+    ("Q", 1),
+    ("D", 0),
+    ("W", 0),
+    ("P1", 0),
+    ("H", 2),
+    ("Q", 0),
+    ("R0", 1),
+    ("R1", 0),
+    ("P0", 2),
+    ("T0", 1),
+    ("T1", 0),
+    ("Q", 2),
+    ("P1", 1),
+    ("H", 3),
+    ("P2", 0),
+    ("Q", 1),
+    ("R0", 2),
+    ("Q", 0),
+    ("P0", 3),
+    ("R1", 1),
+    ("T0", 2),
+    ("Q", 3),
+    ("P1", 2),
+    ("R2", 0),
+    ("T1", 1),
+    ("Q", 2),
+    ("P2", 1),
+    ("R0", 3),
+    ("Q", 1),
+    ("T2", 0),
+    ("R1", 2),
+    ("T0", 3),
+    ("P1", 3),
+    ("R2", 1),
+    ("Q", 3),
+    ("T1", 2),
+    ("P2", 2),
+    ("T2", 1),
+    ("Q", 2),
+    ("R1", 3),
+    ("R2", 2),
+    ("T1", 3),
+    ("P2", 3),
+    ("T2", 2),
+    ("Q", 3),
+    ("gdown", 0),
+    ("R2", 3),
+    ("gup", 0),
+    ("T2", 3),
+)
 
 
 def front_kernel(
@@ -315,39 +401,42 @@
         norm_copy(s).start()
         return carry
 
-    def step_a(s, carry):
+    def step_a(s):
         normed = act[s]
         q[s] = ((matmul(normed, wqkv[0], 1, 0) + vec[7:8, 0:256]) * 0.125).astype(BF)
         kv[s, 2, :, 0:LOCAL] = matmul(normed, wqkv[1], 1, 0).astype(BF)
         kv[s, 2, :, LOCAL:] = (matmul(normed, wqkv[2], 1, 0) + vec[7:8, 256:512]).astype(BF)
 
-        @pl.when(at.z < 3)
+        @pl.when((at.z < 3) & ((at.z == 0) | (s == 0)))
         def _():
             near_copy(s).start()
-
-        return carry
 
     lax.fori_loop(0, SEQS, step_norm, 0)
     weight_wait(0)
-    lax.fori_loop(0, SEQS, step_a, 0)
     for i in range(1, 4):
         weight_start(i)
-    for j in range(3):
-        count_z(j).wait()
-    cnt[4] = cnt[0] + cnt[1] + cnt[2] + cnt[3]
-    for j in range(nf - 1):
-        count_f(j).start()
     for i, (source, target) in enumerate(quarters):
         pltpu.make_async_copy(source.at[:, mine, :], target, q_sems.at[i]).wait()
-    for s in range(SEQS):
-        norm_copy(s).wait()
-    for j in range(nf - 1):
-        count_f(j).wait()
-    total_count = cnt[4]
-    for j in range(nf - 1):
-        total_count = total_count + cnt[5 + j]
-    small[6:7, 0:128] = total_count[0:1, :]
-    cnt[0] = (SEQS * GROUP * nf * 4) / total_count
+
+    def step_count(s):
+        for j in range(3):
+            count_z(j).wait()
+        cnt[4] = cnt[0] + cnt[1] + cnt[2] + cnt[3]
+        for j in range(nf - 1):
+            count_f(j).start()
+
+    def step_counted(s):
+        for j in range(nf - 1):
+            count_f(j).wait()
+        total_count = cnt[4]
+        for j in range(nf - 1):
+            total_count = total_count + cnt[5 + j]
+        small[6:7, 0:128] = total_count[0:1, :]
+        cnt[0] = (SEQS * GROUP * nf * 4) / total_count
+        for i in range(SEQS):
+            norm_copy(i).wait()
+        for copy in block_copies(0):
+            copy.start()
 
     def factor():
         return cnt[0, 0:1, 0:1]
@@ -357,9 +446,6 @@
             pltpu.make_async_copy(teacher.at[s], stage.at[0], in_sems.at[0]),
             pltpu.make_async_copy(cot.at[s], stage.at[1], in_sems.at[1]),
         )
-
-    for copy in block_copies(0):
-        copy.start()
 
     def kv_out(s):
         return pltpu.make_async_copy(kv.at[s], kv_h.at[s], res_sem.at[s])
@@ -409,6 +495,10 @@
         def _():
             far_copy(s).start()
 
+            @pl.when(s < 3)
+            def _():
+                near_copy(s + 1).start()
+
     def step_p0(s):
         @pl.when(at.z < 3)
         def _():
@@ -500,44 +590,41 @@
         send[s] = matmul(slope[s], wfc1[...], 1, 1).astype(BF)
         ring.rs_core(s).start()
 
-    steps_p = (step_p0, step_p1, step_p2)
-
-    def inside(s, action):
-        @pl.when((s >= 0) & (s < SEQS))
-        def _():
-            action(s)
-
-    halo(0)
-
-    def wave(m, carry):
-        for k in range(3):
-            for lag in (3, 2):
-                kind = (k - lag) % 3
-                s = m + (k - lag - kind) // 3 - kind
-                if lag == 3:
-                    inside(s, lambda s: ring.step_t(*ends(kind, s), s))
-                else:
-                    inside(s, lambda s: step_r(kind, s))
-            if k == 0:
-                inside(m + 1, halo)
-
-                @pl.when(m == 0)
-                def _():
-                    weight_wait(1)
-
-            if k == 1:
-
-                @pl.when(m == 1)
-                def _():
-                    weight_wait(2)
-                    weight_wait(3)
-
-            inside(m - k, steps_p[k])
-            inside(m - k, ring.step_q)
-        return carry
-
-    lax.fori_loop(0, 7, wave, 0)
     deep = lambda ref: ref.reshape(SEQS * GROUP, 1024)
+
+    def down_out():
+        return pltpu.make_async_copy(deep(send).at[0:1024], gfc2, in_sems.at[0])
+
+    def up_out():
+        return pltpu.make_async_copy(deep(act).at[0:1024], gfc1, in_sems.at[1])
+
+    def step_gdown(s):
+        deep(send)[0:1024, :] = matmul(deep(act)[...], deep(blk)[...], 0, 0).astype(BF)
+        down_out().start()
+
+    def step_gup(s):
+        deep(act)[0:1024, :] = matmul(deep(n2)[...], deep(slope)[...], 0, 0).astype(BF)
+        up_out().start()
+
+    actions = {
+        "A": step_a,
+        "H": halo,
+        "C": step_count,
+        "D": step_counted,
+        "W": lambda s: weight_wait(s),
+        "P0": step_p0,
+        "P1": step_p1,
+        "P2": step_p2,
+        "Q": ring.step_q,
+        "gdown": step_gdown,
+        "gup": step_gup,
+    }
+    for k in range(3):
+        actions[f"R{k}"] = functools.partial(step_r, k)
+        actions[f"T{k}"] = lambda s, k=k: ring.step_t(*ends(k, s), s)
+    actions["W"] = lambda s: [weight_wait(i) for i in (2, 3)]
+    actions["V"] = lambda s: weight_wait(1)
+    run_order(actions, FRONT_ORDER)
     last = pltpu.make_async_copy(gblk, gmid_h, out_sem)
     last.start()
     kept = (
@@ -546,19 +633,13 @@
     )
     for copy in kept:
         copy.start()
-    deep(send)[0:1024, :] = matmul(deep(act)[...], deep(blk)[...], 0, 0).astype(BF)
-    down_out = pltpu.make_async_copy(deep(send).at[0:1024], gfc2, in_sems.at[0])
-    down_out.start()
-    deep(send)[1024:2048, :] = matmul(deep(n2)[...], deep(slope)[...], 0, 0).astype(BF)
-    up_out = pltpu.make_async_copy(deep(send).at[1024:2048], gfc1, in_sems.at[1])
-    up_out.start()
     for s in range(SEQS):
         ring.step_u(*ends(2, s), s)
         mix_copy(s).wait()
         kv_out(s).wait()
     last.wait()
-    down_out.wait()
-    up_out.wait()
+    down_out().wait()
+    up_out().wait()
     for copy in kept:
         copy.wait()
 
@@ -704,6 +785,64 @@
             self.z_copy(stage - 1).start()
 
 
+BACK_ORDER = (
+    ("A0", 0),
+    ("G0", 0),
+    ("E", 0),
+    ("E", 1),
+    ("E", 2),
+    ("I", 0),
+    ("A1", 0),
+    ("E", 3),
+    ("I", 1),
+    ("B0", 0),
+    ("I", 2),
+    ("G1", 0),
+    ("F", 0),
+    ("B1", 0),
+    ("Q", 0),
+    ("A2", 0),
+    ("R", 0),
+    ("I", 3),
+    ("T", 0),
+    ("F", 1),
+    ("Q", 1),
+    ("F", 2),
+    ("R", 1),
+    ("Q", 2),
+    ("G2", 0),
+    ("T", 1),
+    ("B2", 0),
+    ("R", 2),
+    ("A3", 0),
+    ("T", 2),
+    ("F", 3),
+    ("C0", 0),
+    ("Q", 3),
+    ("G3", 0),
+    ("B3", 0),
+    ("R", 3),
+    ("S0", 0),
+    ("C1", 0),
+    ("A4", 0),
+    ("S1", 0),
+    ("S2", 0),
+    ("T", 3),
+    ("G4", 0),
+    ("S3", 0),
+    ("B4", 0),
+    ("S4", 0),
+    ("S5", 0),
+    ("C2", 0),
+    ("A5", 0),
+    ("G5", 0),
+    ("B5", 0),
+    ("C3", 0),
+    ("C4", 0),
+    ("C5", 0),
+)
+
+
 def back_kernel(
     nf,
     gmix_h,
@@ -720,6 +859,7 @@
     wout,
     vec,
     segs,
+    sums_one,
     ig_h,
     small,
     s_qkv,
@@ -770,6 +910,13 @@
     m2_sems,
     red_x,
     red_z,
+    got_core,
+    got_y,
+    got_f,
+    got_z,
+    sum_sems,
+    sum_f_sems,
+    n1e,
 ):
     at = Place(nf)
     at.barrier()
@@ -785,7 +932,13 @@
         sems = (red_x.at[i], red_z.at[i])
         return Reduce(at, cut, fs, rows, full, arrived, shard, half, quarter, sems)
 
-    red_qkv = reducer(0, deep_cut, fs, f_qkv, x_qkv, s_qkv, h_qkv, k_qkv)
+    first, rest = pl.ds(0, 1), pl.ds(1, 2)
+    red_q = reducer(
+        0, deep_cut, fs, f_qkv.at[first], x_qkv.at[:, first], s_qkv.at[first], h_qkv.at[first], k_qkv.at[first]
+    )
+    red_kv = reducer(
+        4, deep_cut, fs, f_qkv.at[rest], x_qkv.at[:, rest], s_qkv.at[rest], h_qkv.at[rest], k_qkv.at[rest]
+    )
     red_out = reducer(1, cols_cut, LOCAL, f_out, x_out, s_out, h_out, k_out)
     red_fc1 = reducer(2, rows_cut, fs, f_fc1, x_fc1, s_fc1, h_fc1, k_fc1)
     red_fc2 = reducer(3, cols_cut, 1024, f_fc2, x_fc2, s_fc2, h_fc2, k_fc2)
@@ -809,6 +962,9 @@
     def norm_load(s):
         return pltpu.make_async_copy(n1_h.at[s], n1s, load_sems.at[2, 0])
 
+    def norm_early(s):
+        return pltpu.make_async_copy(n1_h.at[s], n1e, load_sems.at[0, 1])
+
     def mid_load(s):
         return pltpu.make_async_copy(gmid_h.at[s], gmid, load_sems.at[2, 1])
 
@@ -817,6 +973,7 @@
     for i in range(4):
         first_copy(i).start()
     norm_load(0).start()
+    norm_early(0).start()
 
     segk[...] = jnp.full(segk.shape, -1.0, F32)
     segk[0:4, 1024:3072] = segs[...].astype(F32)
@@ -890,6 +1047,13 @@
         def _():
             m1_copy(s).start()
 
+        norm_early(s).wait()
+        a_qkv[0] += matmul(n1e[...], gq[s], 0, 0)
+
+        @pl.when(s < 3)
+        def _():
+            norm_early(s + 1).start()
+
     def step_i(s):
         @pl.when((at.z > 0) & (at.z < 3))
         def _():
@@ -915,15 +1079,15 @@
         ).astype(BF)
         ring.rs_core(s).start()
         normed = n1s[...]
-        for i in range(3):
+        for i in (1, 2):
             a_qkv[i] += matmul(normed, grads[i], 0, 0)
 
         @pl.when(s < 3)
         def _():
             norm_load(s + 1).start()
 
-        small[2:3, 0:LOCAL] += column_sum(grads[0].astype(F32))
-        small[2:3, LOCAL : 2 * LOCAL] += column_sum(grads[2].astype(F32))
+        small[9:10, 0:LOCAL] += column_sum(grads[0].astype(F32))
+        small[9:10, LOCAL : 2 * LOCAL] += column_sum(grads[2].astype(F32))
 
     def ends(s):
         return tok_q.at[s], ig_h
@@ -950,40 +1114,70 @@
         ig_copy(s).start()
         ring.spread(*ends(s), s)
 
-    def inside(s, action):
-        @pl.when((s >= 0) & (s < SEQS))
-        def _():
-            action(s)
-
+    def sum_copy(stage, j=0):
+        pair = (sum_sems.at[0, stage], sum_sems.at[1, stage])
+        top = small.at[0:8]
+        if stage == 0:
+            return remote(top, got_core, pair, at.mate_c)
+        if stage == 1:
+            return remote(top, got_y, pair, at.mate_y)
+        if stage == 2:
+            pair = (sum_f_sems.at[0, j], sum_f_sems.at[1, j])
+            return remote(small, got_f.at[j], pair, at.peers_f[j])
+        mate = red_q.side if stage == 3 else red_q.across
+        return remote(small, got_z.at[stage - 3], pair, mate)
+
+    def step_sum(stage, s):
+        if stage == 0:
+            small[2:6, :] = sums_one[0:4, :]
+            small[6:7, :] = sums_one[5:6, :]
+            small[8:9, :] = sums_one[4:5, :]
+        elif stage == 3:
+            for j in range(nf - 1):
+                sum_copy(2, j).wait()
+            for j in range(nf - 1):
+                small[...] += got_f[j]
+        else:
+            sum_copy(stage - 1).wait()
+            if stage == 1:
+                small[0:8, :] += got_core[...]
+            elif stage == 2:
+                small[0:8, :] += got_y[...]
+            else:
+                small[...] += got_z[stage - 4]
+        if stage == 2:
+            for j in range(nf - 1):
+                sum_copy(2, j).start()
+        elif stage < 5:
+            sum_copy(stage).start()
+
+    def step_group(group, stage, s):
+        if stage == 0:
+            if group == "B":
+                f_out[...] = a_out[...].astype(BF)
+                f_qkv[0] = a_qkv[0].astype(BF)
+            elif group == "C":
+                for i in (1, 2):
+                    f_qkv[i] = a_qkv[i].astype(BF)
+        for reduce in groups[group]:
+            reduce.run(stage)
+
+    groups = {"A": (red_fc2,), "G": (red_fc1,), "B": (red_out, red_q), "C": (red_kv,)}
     for i in range(4):
         first_copy(i).wait()
-    red_fc1.run(0)
-    red_fc2.run(0)
-
-    def wave(m, carry):
-        inside(m, step_e)
-        inside(m - 1, step_i)
-        inside(m - 4, lambda s: ring.step_t(*ends(s), s))
-        inside(m - 3, step_r)
-        inside(m - 2, step_f)
-        inside(m - 2, ring.step_q)
-        return carry
-
-    lax.fori_loop(0, 6, wave, 0)
-    f_out[...] = a_out[...].astype(BF)
-    f_qkv[...] = a_qkv[...].astype(BF)
-    red_out.run(0)
-    red_qkv.run(0)
-    for reduce in (red_fc1, red_fc2):
-        reduce.run(1)
-    ring.step_t(*ends(2), 2)
-    step_r(3)
-    for reduce in (red_out, red_qkv):
-        reduce.run(1)
-    ring.step_t(*ends(3), 3)
-    for stage in (2, 3, 4, 5):
-        for reduce in (red_fc1, red_fc2, red_out, red_qkv):
-            reduce.run(stage)
+    actions = {
+        "E": step_e,
+        "I": step_i,
+        "F": step_f,
+        "Q": ring.step_q,
+        "R": step_r,
+        "T": lambda s: ring.step_t(*ends(s), s),
+    }
+    for stage in range(6):
+        actions[f"S{stage}"] = functools.partial(step_sum, stage)
+        for group in groups:
+            actions[f"{group}{stage}"] = functools.partial(step_group, group, stage)
+    run_order(actions, BACK_ORDER)
     for s in range(SEQS):
         ring.step_u(*ends(s), s)
         ig_copy(s).wait()
@@ -1009,13 +1203,13 @@
         functools.partial(back_kernel, nf),
         out_shape=(
             shape((SEQS, GROUP, 1024), BF),
-            shape((8, 1024), F32),
+            shape((16, 1024), F32),
             shape((3, fs, LOCAL), BF),
             shape((LOCAL, fs), BF),
             shape((fs, 1024), BF),
             shape((1024, fs), BF),
         ),
-        in_specs=[anys] * 4 + [vmem, vmem, anys, vmem, anys, anys, vmem, vmem, vmem, vmem],
+        in_specs=[anys] * 4 + [vmem, vmem, anys, vmem, anys, anys, vmem, vmem, vmem, vmem, vmem],
         out_specs=(anys, vmem, vmem, vmem, vmem, vmem),
         scratch_shapes=[
             low(GROUP, 1024),
@@ -1060,8 +1254,15 @@
             dma((4,)),
             dma((2, SEQS)),
             dma((2, SEQS)),
-            dma((4, 2, nf - 1)),
-            dma((4, 2, 4)),
+            dma((5, 2, nf - 1)),
+            dma((5, 2, 4)),
+            pltpu.VMEM((8, 1024), F32),
+            pltpu.VMEM((8, 1024), F32),
+            pltpu.VMEM((nf - 1, 16, 1024), F32),
+            pltpu.VMEM((2, 16, 1024), F32),
+            dma((2, 5)),
+            dma((2, nf - 1)),
+            low(GROUP, 1024),
         ],
         compiler_params=pltpu.CompilerParams(
             collective_id=2, has_side_effects=True, vmem_limit_bytes=63 * 2**20
@@ -1114,17 +1315,12 @@
         nf, w_qkv, w_out, w_fc1, w_fc2, tokens, teacher, cotangent, vec, mask_f, segment_ids
     )
     (output, grad_mix, grad_middle, gfc1, gfc2, sums_one, att, q, kv, lse, n1, wqkv, wout) = front
-    input_grad, sums_two, s_qkv, s_out, s_fc1, s_fc2 = back_call(
-        nf, grad_mix, grad_middle, gfc1, gfc2, att, q, kv, lse, n1, tokens, wqkv, wout, vec, segment_ids
+    input_grad, everything, s_qkv, s_out, s_fc1, s_fc2 = back_call(
+        nf, grad_mix, grad_middle, gfc1, gfc2, att, q, kv, lse, n1, tokens, wqkv, wout, vec, segment_ids, sums_one
     )
     place_f = lax.axis_index("fsdp")
-    place_t = lax.axis_index("tensor")
-    by_tensor = jnp.stack([sums_one[4], sums_two[2]])
-    slots = jnp.where(jnp.arange(4)[:, None, None] == place_t, by_tensor[None], 0.0)
-    everything = jnp.concatenate([sums_one[0:4], sums_one[5:6], sums_two[0:2], slots.reshape(8, D)])
-    everything = lax.psum(everything, ("fsdp", "context", "tensor"))
-    loss = jnp.sum(everything[4]) / (2.0 * D * sums_one[6, 0])
-    ours = lax.dynamic_index_in_dim(everything[7:].reshape(4, 2, D), place_t, 0, keepdims=False)
+    loss = jnp.sum(everything[6]) / (2.0 * D * sums_one[6, 0])
+    ours = everything[8:10]
     part = lax.dynamic_slice_in_dim(everything[0:7], place_f * wide, wide, 1)
     grad_up = ours[0].reshape(b_fc1.shape[0], -1)
     grad_up = lax.dynamic_slice_in_dim(grad_up, place_f * b_fc1.shape[1], b_fc1.shape[1], 1)
@@ -1134,18 +1330,18 @@
         output,
         loss,
         input_grad,
-        part[5],
-        part[6],
+        part[0],
+        part[1],
         s_qkv.astype(F32),
         grad_qv,
         s_out.astype(F32),
+        part[5],
         part[3],
-        part[1],
-        part[2],
+        part[4],
         s_fc1.astype(F32),
         grad_up,
         s_fc2.astype(F32),
-        part[0],
+        part[2],
     )
 
 

time: 600 us -> 481 us (0.80)
  Pallas kernels: 523 us -> 441 us
  blocking collectives: 42.9 us -> 5.32 us
    pallas_call x1, Pallas kernels: 267 us -> 214 us  [front_call(): pl.pallas_call(functools.partial(front_kernel, nf), out_shape=(shape((SEQ...]
    psum x1 -> x0, blocking collectives: 37.6 us -> none  [local(): everything = lax.psum(everything, ('fsdp', 'context', 'tensor'))]
    pallas_call x1, Pallas kernels: 256 us -> 227 us  [back_call(): pl.pallas_call(functools.partial(back_kernel, nf), out_shape=(shape((SEQS...]
    unnamed x26 -> x22, local copies, waits for them, and re-layouts: 11.1 us -> 12.2 us
where the time goes in v3:
time: 481 us; the launch traced here: 480 us
  Pallas kernels  441 us (92%)
  local copies, waits for them, and re-layouts  19.4 us (4%)
  other arithmetic  11.4 us (2%)
  blocking collectives  5.32 us (1%)
    pallas_call x1, Pallas kernels, back_call(): pl.pallas_call(functools.partial(back_kernel, nf), out_shape=(shape((SEQS...  227 us
    pallas_call x1, Pallas kernels, front_call(): pl.pallas_call(functools.partial(front_kernel, nf), out_shape=(shape((SEQ...  214 us
    unnamed x22, local copies, waits for them, and re-layouts  12.2 us

profile of v3, /device:TPU:0, one launch (start us, length us, event | category | flops | bytes accessed | tf_op | source)
XLA Modules:
  0.0 480.2 jit_solution(14579551427548095254)
XLA Ops:
  0.7 0.9 dynamic-update-slice
  1.5 0.9 dynamic-update-slice.1
  2.4 0.9 dynamic-update-slice.2
  3.3 0.9 dynamic-update-slice.3
  4.1 0.9 dynamic-update-slice.4
  5.0 0.9 dynamic-update-slice.5
  5.8 0.8 reshape.68
  6.8 0.9 dynamic-update-slice.7
  7.6 5.3 %all-gather.1 = bf16[2,1,3840]{2,1,0:T(2,128)(2,1)S(1)} all-gather(bf16[1,1,3840]{2,1,0:T(2,128)(2,1)S(1)} %reshape.82), channel_id=2, replica_groups=mesh['fsdp'=2,'context'=4,'tensor'=4] {'fsdp'}, dimensions={0}, use_global_device_ids=true | all-gather | bytes 23040 | tf_op jit(solution)/shard_map/all_gather | solution.py:1298
  13.3 0.7 concatenate.14.vec
  13.9 1.3 pad_convert_fusion.mask
  15.2 213.6 %front.1 = (bf16[4,512,1024]{2,1,0:T(8,128)(2,1)}, bf16[4,512,1024]{2,1,0:T(8,128)(2,1)}, f32[4,128,1024]{2,1,0:T(8,128)}, bf16[1024,1024]{1,0:T(8,128)(2,1)}, b...) custom-call(bf16[3,512,256]{2,1,0:T(8,128)(2,1)} %wqkv_s.1, ...), custom_call_target="tpu_custom_call" | custom-call | flops 38654705664 | bytes 31457280 | tf_op jit(solution)/shard_map/front/pallas_call | solution.py:653
  228.9 227.3 %back.1 = (bf16[4,512,1024]{2,1,0:T(8,128)(2,1)}, f32[16,1024]{1,0:T(8,128)}, bf16[3,512,256]{2,1,0:T(8,128)(2,1)}, bf16[256,512]{1,0:T(8,128)(2,1)}, bf16[512,1...) custom-call(bf16[4,512,1024]{2,1,0:T(8,128)(2,1)} %get-tuple-element.35.gmix_h, f32[4,128,1024]{2,1,0:T(8,128)} %get-tuple-element.36.gmid_h, ...), custom_call_target="tpu_custom_call" | custom-call | flops 25769803776 | bytes 31457280 | tf_op jit(solution)/shard_map/back/pallas_call | solution.py:1202
  456.2 1.5 slice_reduce_fusion
  457.6 1.2 slice.69
  460.1 0.8 slice.70
  460.9 0.7 fusion
  461.6 2.4 convert_element_type.20
  464.0 0.7 slice_reduce_fusion.2
  465.5 1.8 convert_element_type.21
  467.3 2.8 convert_element_type.22
  470.7 1.6 convert_element_type.23
  472.3 4.8 %copy.56 = bf16[4,512,1024]{2,1,0:T(8,128)(2,1)} copy(bf16[4,512,1024]{2,1,0:T(8,128)(2,1)} %get-tuple-element.83) | data formatting | bytes 8388608
  477.1 2.0 copy.57
  (24 shorter events, 1.8 us)
Async XLA Ops:
  456.1 14.5 %copy-start.1 = (bf16[1024,512]{1,0:T(8,128)(2,1)S(1)}, bf16[1024,512]{1,0:T(8,128)(2,1)}, u32[]{:S(2)}) copy-start(bf16[1024,512]{1,0:T(8,128)(2,1)} %get-tuple-element.52) | copy-start | bytes 3145732
  472.3 4.8 %copy-start = (bf16[4,512,1024]{2,1,0:T(8,128)(2,1)S(1)}, bf16[4,512,1024]{2,1,0:T(8,128)(2,1)}, u32[]{:S(2)}) copy-start(bf16[4,512,1024]{2,1,0:T(8,128)(2,1)} %get-tuple-element.85) | copy-start | bytes 12582916

commit v4 on v3

--- a/solution.py
+++ b/solution.py
@@ -173,65 +173,65 @@
 FRONT_ORDER = (
     ("A", 0),
     ("A", 1),
+    ("H", 0),
     ("A", 2),
+    ("V", 0),
+    ("P0", 0),
     ("A", 3),
     ("C", 0),
-    ("H", 0),
-    ("V", 0),
-    ("P0", 0),
     ("Q", 0),
     ("H", 1),
     ("R0", 0),
     ("P0", 1),
     ("T0", 0),
+    ("H", 2),
     ("Q", 1),
     ("D", 0),
     ("W", 0),
     ("P1", 0),
-    ("H", 2),
     ("Q", 0),
     ("R0", 1),
+    ("P0", 2),
     ("R1", 0),
-    ("P0", 2),
     ("T0", 1),
-    ("T1", 0),
     ("Q", 2),
+    ("H", 3),
     ("P1", 1),
-    ("H", 3),
-    ("P2", 0),
     ("Q", 1),
     ("R0", 2),
-    ("Q", 0),
     ("P0", 3),
     ("R1", 1),
+    ("Q", 3),
     ("T0", 2),
-    ("Q", 3),
     ("P1", 2),
-    ("R2", 0),
+    ("T1", 0),
     ("T1", 1),
     ("Q", 2),
+    ("P2", 0),
+    ("R0", 3),
     ("P2", 1),
-    ("R0", 3),
-    ("Q", 1),
-    ("T2", 0),
+    ("Q", 0),
+    ("T0", 3),
     ("R1", 2),
-    ("T0", 3),
     ("P1", 3),
-    ("R2", 1),
     ("Q", 3),
     ("T1", 2),
+    ("Q", 1),
     ("P2", 2),
-    ("T2", 1),
+    ("R1", 3),
+    ("R2", 1),
     ("Q", 2),
-    ("R1", 3),
-    ("R2", 2),
     ("T1", 3),
     ("P2", 3),
-    ("T2", 2),
+    ("R2", 0),
     ("Q", 3),
     ("gdown", 0),
+    ("T2", 0),
+    ("R2", 2),
+    ("T2", 1),
+    ("gup", 0),
     ("R2", 3),
-    ("gup", 0),
+    ("T2", 2),
     ("T2", 3),
 )
 
@@ -245,7 +245,14 @@
     tokens,
     teacher,
     cot,
-    vec,
+    part_bo,
+    part_g2,
+    part_b2,
+    part_bd,
+    part_g1,
+    part_b1,
+    part_qv,
+    part_up,
     mask,
     segs,
     out_h,
@@ -298,6 +305,10 @@
     cf_sems,
     res_sem,
     keep_sem,
+    vec,
+    vec_own,
+    vec_got,
+    v_sems,
 ):
     at = Place(nf)
     at.barrier()
@@ -338,7 +349,36 @@
     for i, (source, target) in enumerate(quarters):
         pltpu.make_async_copy(source.at[:, mine, :], target, q_sems.at[i]).start()
 
-    masks = mask[...]
+    vec_own[...] = jnp.zeros_like(vec_own)
+    rows = ((0, part_bo), (1, part_g2), (2, part_b2), (4, part_bd), (5, part_g1), (6, part_b1))
+    for i, part in rows:
+        vec_own[i : i + 1, own] = part[...].astype(F32).reshape(1, fs)
+
+    def scatter(part, count):
+        wide = part.shape[1]
+        unit = wide * nf
+        column = lax.broadcasted_iota(jnp.int32, (wide, count * unit), 1)
+        inside = lax.broadcasted_iota(jnp.int32, (wide, count * unit), 0) + at.f * wide
+        spread = (lax.rem(column, unit) == inside).astype(BF)
+        full = matmul(part, spread, 1, 0)
+        group = lax.broadcasted_iota(jnp.int32, full.shape, 1) // unit
+        owner = lax.broadcasted_iota(jnp.int32, full.shape, 0)
+        return jnp.sum(jnp.where(group == owner, full, 0.0), axis=0, keepdims=True)
+
+    vec_own[3:4, :] = scatter(part_up[...], part_up.shape[0])
+    for i in range(2):
+        columns = pl.ds(i * LOCAL, LOCAL)
+        vec_own[7:8, columns] = scatter(part_qv[i], part_qv.shape[1])
+
+    def vec_copy(j):
+        pair = (v_sems.at[0, j], v_sems.at[1, j])
+        return remote(vec_own, vec_got.at[j], pair, at.peers_f[j])
+
+    for j in range(nf - 1):
+        vec_copy(j).start()
+
+    valid = mask[...].astype(F32)
+    masks = jnp.concatenate([valid, jnp.zeros_like(valid)], axis=0)
     cnt[0] = jnp.broadcast_to(jnp.sum(masks, keepdims=True), (8, 128))
 
     def count_z(j):
@@ -411,6 +451,13 @@
         def _():
             near_copy(s).start()
 
+    for j in range(nf - 1):
+        vec_copy(j).wait()
+    whole = vec_own[...]
+    for j in range(nf - 1):
+        whole = whole + vec_got[j]
+    vec[...] = whole
+    small[7:8, :] = vec[5:6, :]
     lax.fori_loop(0, SEQS, step_norm, 0)
     weight_wait(0)
     for i in range(1, 4):
@@ -667,7 +714,7 @@
             shape((3, 1024, LOCAL), BF),
             shape((LOCAL, 1024), BF),
         ),
-        in_specs=[anys] * 7 + [vmem] * 3,
+        in_specs=[anys] * 7 + [vmem] * 10,
         out_specs=(anys, anys, anys, anys, anys, vmem, vmem, vmem, anys, vmem, anys, anys, anys),
         scratch_shapes=[
             pltpu.VMEM((3, 1024, LOCAL), BF),
@@ -707,6 +754,10 @@
             dma((2, nf - 1)),
             dma((SEQS,)),
             dma((2,)),
+            pltpu.VMEM((8, 1024), F32),
+            pltpu.VMEM((8, 1024), F32),
+            pltpu.VMEM((nf - 1, 8, 1024), F32),
+            dma((2, nf - 1)),
         ],
         compiler_params=pltpu.CompilerParams(
             collective_id=1, has_side_effects=True, vmem_limit_bytes=63 * 2**20
@@ -786,61 +837,159 @@
 
 
 BACK_ORDER = (
-    ("A0", 0),
-    ("G0", 0),
     ("E", 0),
+    ("K0", 0),
     ("E", 1),
+    ("K1", 0),
+    ("K0", 1),
+    ("K0", 2),
+    ("I", 0),
     ("E", 2),
-    ("I", 0),
-    ("A1", 0),
+    ("K2", 0),
+    ("K1", 1),
     ("E", 3),
+    ("K0", 3),
+    ("K3", 0),
+    ("K1", 2),
+    ("K2", 1),
+    ("K3", 1),
     ("I", 1),
     ("B0", 0),
+    ("K2", 2),
+    ("K4", 0),
+    ("F", 0),
     ("I", 2),
-    ("G1", 0),
-    ("F", 0),
+    ("K4", 1),
+    ("D1", 0),
+    ("I", 3),
+    ("F", 1),
+    ("D2", 0),
+    ("Q", 1),
+    ("K1", 3),
+    ("Q", 0),
+    ("K3", 2),
+    ("D1", 1),
     ("B1", 0),
-    ("Q", 0),
-    ("A2", 0),
+    ("F", 2),
+    ("D1", 3),
+    ("D1", 2),
+    ("K2", 3),
+    ("K3", 3),
+    ("F", 3),
+    ("Q", 2),
+    ("D2", 1),
+    ("C0", 0),
+    ("B2", 0),
     ("R", 0),
-    ("I", 3),
+    ("D2", 3),
+    ("R", 1),
+    ("D2", 2),
+    ("B3", 0),
+    ("Q", 3),
+    ("K4", 2),
+    ("D1", 4),
+    ("K4", 3),
+    ("D1", 5),
+    ("D3", 0),
+    ("D1", 6),
+    ("C1", 0),
+    ("B4", 0),
+    ("T", 1),
+    ("D2", 4),
+    ("R", 2),
+    ("D1", 7),
     ("T", 0),
-    ("F", 1),
-    ("Q", 1),
-    ("F", 2),
-    ("R", 1),
-    ("Q", 2),
-    ("G2", 0),
-    ("T", 1),
-    ("B2", 0),
-    ("R", 2),
-    ("A3", 0),
-    ("T", 2),
-    ("F", 3),
-    ("C0", 0),
-    ("Q", 3),
-    ("G3", 0),
-    ("B3", 0),
+    ("D3", 3),
+    ("D2", 5),
     ("R", 3),
     ("S0", 0),
-    ("C1", 0),
-    ("A4", 0),
     ("S1", 0),
+    ("D2", 6),
     ("S2", 0),
+    ("D3", 2),
+    ("C2", 0),
+    ("C3", 0),
+    ("D3", 6),
     ("T", 3),
-    ("G4", 0),
+    ("D2", 7),
     ("S3", 0),
-    ("B4", 0),
+    ("D3", 5),
+    ("C4", 0),
+    ("D3", 7),
+    ("T", 2),
     ("S4", 0),
+    ("D3", 1),
+    ("B5", 0),
+    ("D3", 4),
     ("S5", 0),
-    ("C2", 0),
-    ("A5", 0),
-    ("G5", 0),
-    ("B5", 0),
-    ("C3", 0),
-    ("C4", 0),
     ("C5", 0),
 )
+
+
+class Chain(Reduce):
+    def piece(self, ref, half):
+        return self.part(ref, half * (self.rows // 2), self.rows // 2)
+
+    def x_half(self, j, half):
+        there = lax.rem(self.at.f + 1 + j, self.at.nf)
+        pair = (self.x_sems.at[0, j, half], self.x_sems.at[1, j, half])
+        src = self.piece(self.own(there), half)
+        return remote(src, self.piece(self.arrived.at[j], half), pair, self.at.peers_f[j])
+
+    def up_copy(self, half):
+        pair = (self.z_sems.at[0, half], self.z_sems.at[1, half])
+        src = self.piece(self.own(self.at.f), half)
+        return remote(src, self.piece(self.shard, half), pair, self.at.up)
+
+    def down_copy(self, half, j):
+        q = self.rows // 4
+        part = self.part(self.shard, half * (self.rows // 2) + j * q, q)
+        which = 2 + half * 2 + j
+        pair = (self.z_sems.at[0, which], self.z_sems.at[1, which])
+        return remote(part, part, pair, self.at.down)
+
+    def climb(self, stage, half):
+        own = self.piece(self.own(self.at.f), half)
+        peers = range(self.at.nf - 1)
+        if stage == 0:
+            for j in peers:
+                self.x_half(j, half).start()
+            return
+        if stage == 1:
+            for j in peers:
+                self.x_half(j, half).wait()
+            self.add(own, own, [self.piece(self.arrived.at[j], half) for j in peers])
+
+        @pl.when(self.at.z == stage - 1)
+        def _():
+            shard = self.piece(self.shard, half)
+            if stage > 1:
+                self.up_copy(half).wait_recv()
+                self.add(own if stage < 4 else shard, own, [shard])
+            if stage < 4:
+                self.up_copy(half).start()
+            else:
+                for j in range(2):
+                    self.down_copy(half, j).start()
+
+    def hand_down(self, hop, half, j):
+        @pl.when(self.at.z == 3 - hop)
+        def _():
+            self.down_copy(half, j).wait_recv()
+            if hop < 3:
+                self.down_copy(half, j).start()
+
+    def finish(self):
+        for half in range(2):
+
+            @pl.when(self.at.z < 3)
+            def _():
+                self.up_copy(half).wait_send()
+
+            @pl.when(self.at.z > 0)
+            def _():
+                for j in range(2):
+                    self.down_copy(half, j).wait_send()
 
 
 def back_kernel(
@@ -857,7 +1006,6 @@
     tokens,
     wqkv,
     wout,
-    vec,
     segs,
     sums_one,
     ig_h,
@@ -897,12 +1045,8 @@
     x_fc2,
     h_qkv,
     h_out,
-    h_fc1,
-    h_fc2,
     k_qkv,
     k_out,
-    k_fc1,
-    k_fc2,
     ring_sems,
     load_sems,
     first_sems,
@@ -910,6 +1054,8 @@
     m2_sems,
     red_x,
     red_z,
+    chain_x,
+    chain_z,
     got_core,
     got_y,
     got_f,
@@ -928,9 +1074,9 @@
     fs = 1024 // nf
     f_out = gm.at[0:LOCAL]
 
-    def reducer(i, cut, rows, full, arrived, shard, half, quarter):
-        sems = (red_x.at[i], red_z.at[i])
-        return Reduce(at, cut, fs, rows, full, arrived, shard, half, quarter, sems)
+    def reducer(i, cut, rows, full, arrived, shard, half, quarter, kind=Reduce):
+        sems = (chain_x.at[i - 2], chain_z.at[i - 2]) if kind is Chain else (red_x.at[i], red_z.at[i])
+        return kind(at, cut, fs, rows, full, arrived, shard, half, quarter, sems)
 
     first, rest = pl.ds(0, 1), pl.ds(1, 2)
     red_q = reducer(
@@ -940,8 +1086,8 @@
         4, deep_cut, fs, f_qkv.at[rest], x_qkv.at[:, rest], s_qkv.at[rest], h_qkv.at[rest], k_qkv.at[rest]
     )
     red_out = reducer(1, cols_cut, LOCAL, f_out, x_out, s_out, h_out, k_out)
-    red_fc1 = reducer(2, rows_cut, fs, f_fc1, x_fc1, s_fc1, h_fc1, k_fc1)
-    red_fc2 = reducer(3, cols_cut, 1024, f_fc2, x_fc2, s_fc2, h_fc2, k_fc2)
+    red_fc1 = reducer(2, rows_cut, fs, f_fc1, x_fc1, s_fc1, None, None, Chain)
+    red_fc2 = reducer(3, cols_cut, 1024, f_fc2, x_fc2, s_fc2, None, None, Chain)
 
     firsts = (
         (gfc1_h, f_fc1),
@@ -949,6 +1095,9 @@
         (gmid_h.at[0], gmid),
         (tokens.at[:, mine, :], tok_q),
     )
+
+    def first_copy_of(i):
+        return pltpu.make_async_copy(gfc1_h, f_fc1, first_sems.at[i])
 
     def first_copy(i):
         return pltpu.make_async_copy(firsts[i][0], firsts[i][1], first_sems.at[i])
@@ -1096,6 +1245,11 @@
         return pltpu.make_async_copy(tok_q.at[s], ig_h.at[s, mine], first_sems.at[s])
 
     def step_r(s):
+        @pl.when(s == 0)
+        def _():
+            first_copy(2).wait()
+            first_copy(3).wait()
+
         summed = ring.total(s)
         xhat, inverse = norm_parts(tok_q[s].astype(F32))
         small[0:1, :] += column_sum(summed * xhat)
@@ -1104,7 +1258,7 @@
         def _():
             mid_load(s).wait()
 
-        grad = gmid[...] + norm_back(summed, xhat, inverse, vec[5:6, :])
+        grad = gmid[...] + norm_back(summed, xhat, inverse, sums_one[7:8, :])
         tok_q[s] = grad.astype(BF)
 
         @pl.when(s < 3)
@@ -1162,9 +1316,8 @@
         for reduce in groups[group]:
             reduce.run(stage)
 
-    groups = {"A": (red_fc2,), "G": (red_fc1,), "B": (red_out, red_q), "C": (red_kv,)}
-    for i in range(4):
-        first_copy(i).wait()
+    groups = {"B": (red_out, red_q), "C": (red_kv,)}
+    chains = (red_fc2, red_fc1)
     actions = {
         "E": step_e,
         "I": step_i,
@@ -1177,7 +1330,34 @@
         actions[f"S{stage}"] = functools.partial(step_sum, stage)
         for group in groups:
             actions[f"{group}{stage}"] = functools.partial(step_group, group, stage)
+
+    def step_climb(stage, s):
+        if stage == 0:
+
+            @pl.when(lax.rem(s, 2) == 0)
+            def _():
+                first_copy_of(1 - s // 2).wait()
+
+        for i, chain in enumerate(chains):
+
+            @pl.when(s // 2 == i)
+            def _(chain=chain):
+                chain.climb(stage, lax.rem(s, 2))
+
+    def step_down(hop, s):
+        for i, chain in enumerate(chains):
+
+            @pl.when(s // 4 == i)
+            def _(chain=chain):
+                chain.hand_down(hop, lax.rem(s // 2, 2), lax.rem(s, 2))
+
+    for stage in range(5):
+        actions[f"K{stage}"] = functools.partial(step_climb, stage)
+    for hop in (1, 2, 3):
+        actions[f"D{hop}"] = functools.partial(step_down, hop)
     run_order(actions, BACK_ORDER)
+    for chain in chains:
+        chain.finish()
     for s in range(SEQS):
         ring.step_u(*ends(s), s)
         ig_copy(s).wait()
@@ -1209,7 +1389,7 @@
             shape((fs, 1024), BF),
             shape((1024, fs), BF),
         ),
-        in_specs=[anys] * 4 + [vmem, vmem, anys, vmem, anys, anys, vmem, vmem, vmem, vmem, vmem],
+        in_specs=[anys] * 4 + [vmem, vmem, anys, vmem, anys, anys, vmem, vmem, vmem, vmem],
         out_specs=(anys, vmem, vmem, vmem, vmem, vmem),
         scratch_shapes=[
             low(GROUP, 1024),
@@ -1243,12 +1423,8 @@
             low(nf - 1, 1024, fs),
             low(3, fs // 2, LOCAL),
             low(LOCAL // 2, fs),
-            low(fs // 2, 1024),
-            low(512, fs),
             low(3, fs // 4, LOCAL),
             low(LOCAL // 4, fs),
-            low(fs // 4, 1024),
-            low(256, fs),
             dma((5, 2, SEQS)),
             dma((3, 2)),
             dma((4,)),
@@ -1256,6 +1432,8 @@
             dma((2, SEQS)),
             dma((5, 2, nf - 1)),
             dma((5, 2, 4)),
+            dma((2, 2, nf - 1, 2)),
+            dma((2, 2, 6)),
             pltpu.VMEM((8, 1024), F32),
             pltpu.VMEM((8, 1024), F32),
             pltpu.VMEM((nf - 1, 16, 1024), F32),
@@ -1294,29 +1472,30 @@
     b_fc2,
 ):
     nf = lax.axis_size("fsdp")
-    pieces = (b_out, ln2_gain, ln2_bias, b_fc2, ln1_gain, ln1_bias, b_qv, b_fc1)
-    flat = lax.all_gather(jnp.concatenate([piece.reshape(-1) for piece in pieces]), "fsdp", axis=0)
-    flat = flat.astype(F32)
     wide = b_out.shape[0]
-    rows = [flat[:, i * wide : (i + 1) * wide].reshape(1, D) for i in range(6)]
-    small_qv = flat[:, 6 * wide : 6 * wide + b_qv.size].reshape(nf, *b_qv.shape)
-    small_up = flat[:, 6 * wide + b_qv.size :].reshape(nf, *b_fc1.shape)
-    bias_qv = jnp.moveaxis(small_qv, 0, 2).reshape(1, 2 * LOCAL)
-    bias_up = jnp.moveaxis(small_up, 0, 1).reshape(1, D)
-    vec = jnp.concatenate(
-        rows[:3]
-        + [bias_up]
-        + rows[3:]
-        + [jnp.concatenate([bias_qv, jnp.zeros((1, D - 2 * LOCAL), F32)], axis=1)],
-        axis=0,
-    )
-    mask_f = jnp.concatenate([valid_mask, jnp.zeros_like(valid_mask)], axis=0).astype(F32)
     front = front_call(
-        nf, w_qkv, w_out, w_fc1, w_fc2, tokens, teacher, cotangent, vec, mask_f, segment_ids
+        nf,
+        w_qkv,
+        w_out,
+        w_fc1,
+        w_fc2,
+        tokens,
+        teacher,
+        cotangent,
+        b_out,
+        ln2_gain,
+        ln2_bias,
+        b_fc2,
+        ln1_gain,
+        ln1_bias,
+        b_qv,
+        b_fc1,
+        valid_mask,
+        segment_ids,
     )
     (output, grad_mix, grad_middle, gfc1, gfc2, sums_one, att, q, kv, lse, n1, wqkv, wout) = front
     input_grad, everything, s_qkv, s_out, s_fc1, s_fc2 = back_call(
-        nf, grad_mix, grad_middle, gfc1, gfc2, att, q, kv, lse, n1, tokens, wqkv, wout, vec, segment_ids, sums_one
+        nf, grad_mix, grad_middle, gfc1, gfc2, att, q, kv, lse, n1, tokens, wqkv, wout, segment_ids, sums_one
     )
     place_f = lax.axis_index("fsdp")
     loss = jnp.sum(everything[6]) / (2.0 * D * sums_one[6, 0])

time: 481 us -> 445 us (0.925)
  Pallas kernels: 441 us -> 420 us
  local copies, waits for them, and re-layouts: 19.4 us -> 11.5 us
  blocking collectives: 5.32 us -> 0 us
    pallas_call x1, Pallas kernels: 227 us -> 208 us  [back_call(): pl.pallas_call(functools.partial(back_kernel, nf), out_shape=(shape((SEQS...]
    unnamed x22 -> x6, local copies, waits for them, and re-layouts: 12.2 us -> 6.84 us
    all_gather x1 -> x0, blocking collectives: 5.32 us -> none  [local(): lax.all_gather(jnp.concatenate([piece.reshape(-1) for piece in pieces]),...]
where the time goes in v4:
time: 445 us
  Pallas kernels  420 us (94%)
  local copies, waits for them, and re-layouts  11.5 us (3%)
  other arithmetic  10.1 us (2%)
    pallas_call x1, Pallas kernels, front_call(): pl.pallas_call(functools.partial(front_kernel, nf), out_shape=(shape((SEQ...  212 us
    pallas_call x1, Pallas kernels, back_call(): pl.pallas_call(functools.partial(back_kernel, nf), out_shape=(shape((SEQS...  208 us

profile of v4, /device:TPU:0, one launch (start us, length us, event | category | flops | bytes accessed | tf_op | source)
XLA Modules:
  0.0 444.8 jit_solution(11376435528450825811)
XLA Ops:
  0.7 212.0 %front.1 = (bf16[4,512,1024]{2,1,0:T(8,128)(2,1)}, bf16[4,512,1024]{2,1,0:T(8,128)(2,1)}, f32[4,128,1024]{2,1,0:T(8,128)}, bf16[1024,1024]{1,0:T(8,128)(2,1)}, b...) custom-call(bf16[3,512,256]{2,1,0:T(8,128)(2,1)} %wqkv_s.1, ...), custom_call_target="tpu_custom_call" | custom-call | flops 38654705664 | bytes 31457280 | tf_op jit(solution)/shard_map/front/pallas_call | solution.py:700
  212.6 208.1 %back.1 = (bf16[4,512,1024]{2,1,0:T(8,128)(2,1)}, f32[16,1024]{1,0:T(8,128)}, bf16[3,512,256]{2,1,0:T(8,128)(2,1)}, bf16[256,512]{1,0:T(8,128)(2,1)}, bf16[512,1...) custom-call(bf16[4,512,1024]{2,1,0:T(8,128)(2,1)} %get-tuple-element.35.gmix_h, f32[4,128,1024]{2,1,0:T(8,128)} %get-tuple-element.36.gmid_h, ...), custom_call_target="tpu_custom_call" | custom-call | flops 25769803776 | bytes 31457280 | tf_op jit(solution)/shard_map/back/pallas_call | solution.py:1382
  420.7 0.0 copy-start.1
  420.7 1.5 slice_reduce_fusion
  422.2 1.2 slice.37
  424.7 0.8 slice.38
  425.4 0.7 fusion
  426.1 2.4 convert_element_type.12
  428.5 0.7 slice_reduce_fusion.2
  429.3 0.1 reshape_squeeze.6
  429.3 0.7 constant_dynamic-slice_fusion.2
  430.0 1.8 convert_element_type.13
  431.8 2.8 convert_element_type.14
  434.6 0.6 constant_dynamic-slice_fusion.1
  435.2 0.0 copy-done.1
  435.2 1.6 convert_element_type.15
  436.8 0.0 copy-start
  436.8 4.8 %copy.34 = bf16[4,512,1024]{2,1,0:T(8,128)(2,1)} copy(bf16[4,512,1024]{2,1,0:T(8,128)(2,1)} %get-tuple-element.76) | data formatting | bytes 8388608
  441.6 0.0 copy-done
  441.6 2.0 copy.35
  (1 shorter events, 0.0 us)
Async XLA Ops:
  420.7 14.5 %copy-start.1 = (bf16[1024,512]{1,0:T(8,128)(2,1)S(1)}, bf16[1024,512]{1,0:T(8,128)(2,1)}, u32[]{:S(2)}) copy-start(bf16[1024,512]{1,0:T(8,128)(2,1)} %get-tuple-element.52) | copy-start | bytes 3145732
  436.8 4.8 %copy-start = (bf16[4,512,1024]{2,1,0:T(8,128)(2,1)S(1)}, bf16[4,512,1024]{2,1,0:T(8,128)(2,1)}, u32[]{:S(2)}) copy-start(bf16[4,512,1024]{2,1,0:T(8,128)(2,1)} %get-tuple-element.78) | copy-start | bytes 12582916

commit v5 on v4

--- a/solution.py
+++ b/solution.py
@@ -54,10 +54,9 @@
     return pl.ds(pl.multiple_of(start, unit), size)
 
 
-def allowed_bias(query_seg, key_seg):
-    ahead = lax.broadcasted_iota(jnp.int32, (HALF, SPAN), 1) - lax.broadcasted_iota(
-        jnp.int32, (HALF, SPAN), 0
-    )
+def allowed_bias(query_seg, key_seg, skipped=0, size=SPAN):
+    column = lax.broadcasted_iota(jnp.int32, (HALF, size), 1) + skipped
+    ahead = column - lax.broadcasted_iota(jnp.int32, (HALF, size), 0)
     allowed = (ahead > 0) & (ahead <= WINDOW) & (query_seg == key_seg)
     return jnp.where(allowed, 0.0, MASKED)
 
@@ -317,11 +316,13 @@
 
     fs = wout_s.shape[1]
     own = aligned(at.f * fs, fs)
+    query, pair_kv = pl.ds(0, 1), pl.ds(1, 2)
     places = (
-        (wqkv_s, wqkv.at[:, own, :]),
+        (wqkv_s.at[pair_kv], wqkv.at[pair_kv, own, :]),
         (wout_s, wout.at[:, own]),
         (wfc1_s, wfc1.at[own, :]),
         (wfc2_s, wfc2.at[:, own]),
+        (wqkv_s.at[query], wqkv.at[query, own, :]),
     )
 
     def weight_copy(i, j):
@@ -416,13 +417,19 @@
 
         lax.fori_loop(0, SEQS, clear, 0)
 
-    def near_copy(s):
-        return remote(
-            kv.at[s, 2], kv.at[s, 1], (near_sems.at[0, s], near_sems.at[1, s]), at.up
-        )
-
-    def far_copy(s):
-        return remote(kv.at[s, 1], kv.at[s, 0], (far_sems.at[0, s], far_sems.at[1, s]), at.up)
+    def near_copy(s, half):
+        part = pl.ds(half * HALF, HALF)
+        pair = (near_sems.at[0, s, half], near_sems.at[1, s, half])
+        return remote(kv.at[s, 2, part], kv.at[s, 1, part], pair, at.up)
+
+    def far_copy(s, half):
+        part = pl.ds(half * HALF, HALF)
+        pair = (far_sems.at[0, s, half], far_sems.at[1, s, half])
+        return remote(kv.at[s, 1, part], kv.at[s, 0, part], pair, at.up)
+
+    def near_start(s):
+        for half in range(2):
+            near_copy(s, half).start()
 
     def norm_copy(s):
         return pltpu.make_async_copy(act.at[s], n1_h.at[s], n1_sem.at[s])
@@ -443,13 +450,12 @@
 
     def step_a(s):
         normed = act[s]
-        q[s] = ((matmul(normed, wqkv[0], 1, 0) + vec[7:8, 0:256]) * 0.125).astype(BF)
         kv[s, 2, :, 0:LOCAL] = matmul(normed, wqkv[1], 1, 0).astype(BF)
         kv[s, 2, :, LOCAL:] = (matmul(normed, wqkv[2], 1, 0) + vec[7:8, 256:512]).astype(BF)
 
         @pl.when((at.z < 3) & ((at.z == 0) | (s == 0)))
         def _():
-            near_copy(s).start()
+            near_start(s)
 
     for j in range(nf - 1):
         vec_copy(j).wait()
@@ -460,7 +466,7 @@
     small[7:8, :] = vec[5:6, :]
     lax.fori_loop(0, SEQS, step_norm, 0)
     weight_wait(0)
-    for i in range(1, 4):
+    for i in (4, 1, 2, 3):
         weight_start(i)
     for i, (source, target) in enumerate(quarters):
         pltpu.make_async_copy(source.at[:, mine, :], target, q_sems.at[i]).wait()
@@ -534,32 +540,37 @@
         ring.spread(*ends(k, s), s)
 
     def halo(s):
-        @pl.when(at.z > 0)
-        def _():
-            near_copy(s).wait_recv()
-
-        @pl.when((at.z > 0) & (at.z < 3))
-        def _():
-            far_copy(s).start()
-
-            @pl.when(s < 3)
+        for half in range(2):
+
+            @pl.when(at.z > 0)
             def _():
-                near_copy(s + 1).start()
+                near_copy(s, half).wait_recv()
+
+            @pl.when((at.z > 0) & (at.z < 3))
+            def _():
+                far_copy(s, half).start()
+
+        @pl.when((at.z > 0) & (at.z < 3) & (s < 3))
+        def _():
+            near_start(s + 1)
 
     def step_p0(s):
-        @pl.when(at.z < 3)
-        def _():
-            near_copy(s).wait_send()
-
-        @pl.when((at.z > 0) & (at.z < 3))
-        def _():
-            far_copy(s).wait_send()
-
-        @pl.when(at.z > 1)
-        def _():
-            far_copy(s).wait_recv()
+        for half in range(2):
+
+            @pl.when(at.z < 3)
+            def _():
+                near_copy(s, half).wait_send()
+
+            @pl.when((at.z > 0) & (at.z < 3))
+            def _():
+                far_copy(s, half).wait_send()
+
+            @pl.when(at.z > 1)
+            def _():
+                far_copy(s, half).wait_recv()
 
         kv_out(s).start()
+        q[s] = ((matmul(act[s], wqkv[0], 1, 0) + vec[7:8, 0:256]) * 0.125).astype(BF)
         lane = lax.broadcasted_iota(jnp.int32, (1, LOCAL), 1) // HD
         slot = lax.broadcasted_iota(jnp.int32, (1, 128), 1)
         keys = kv.at[s].reshape(3 * GROUP, 2 * LOCAL)
@@ -599,6 +610,11 @@
 
     def step_p1(s):
         ring.step_u(*ends(0, s), s)
+
+        @pl.when(s == 0)
+        def _():
+            weight_wait(2)
+
         for part in range(2):
             here = pl.ds(part * 256, 256)
             h = matmul(n2[s, here], wfc1[...], 1, 0) + vec[3:4, :]
@@ -608,6 +624,11 @@
                 0.5 * (1.0 + t)
                 + 0.5 * h * (1.0 - t * t) * (0.7978845608028654 * (1.0 + 0.134145 * h * h))
             ).astype(BF)
+
+        @pl.when(s == 0)
+        def _():
+            weight_wait(3)
+
         send[s] = matmul(act[s], wfc2[...], 1, 0).astype(BF)
         ring.rs_core(s).start()
 
@@ -669,8 +690,8 @@
     for k in range(3):
         actions[f"R{k}"] = functools.partial(step_r, k)
         actions[f"T{k}"] = lambda s, k=k: ring.step_t(*ends(k, s), s)
-    actions["W"] = lambda s: [weight_wait(i) for i in (2, 3)]
-    actions["V"] = lambda s: weight_wait(1)
+    actions["W"] = lambda s: None
+    actions["V"] = lambda s: [weight_wait(i) for i in (4, 1)]
     run_order(actions, FRONT_ORDER)
     last = pltpu.make_async_copy(gblk, gmid_h, out_sem)
     last.start()
@@ -739,17 +760,17 @@
             pltpu.VMEM((HALF, SPAN), F32),
             pltpu.VMEM((SEQS, 3, GROUP, 2 * LOCAL), BF),
             pltpu.VMEM((4 + nf, 8, 128), F32),
-            dma((4, nf - 1)),
-            dma((4, nf - 1)),
-            dma((4,)),
+            dma((5, nf - 1)),
+            dma((5, nf - 1)),
+            dma((5,)),
             dma((5, 2, SEQS)),
             dma((3,)),
             dma((2,)),
             dma((SEQS,)),
             dma,
             dma((SEQS,)),
-            dma((2, SEQS)),
-            dma((2, SEQS)),
+            dma((2, SEQS, 2)),
+            dma((2, SEQS, 2)),
             dma((2, 3)),
             dma((2, nf - 1)),
             dma((SEQS,)),
@@ -837,8 +858,8 @@
 
 
 BACK_ORDER = (
+    ("K0", 0),
     ("E", 0),
-    ("K0", 0),
     ("E", 1),
     ("K1", 0),
     ("K0", 1),
@@ -852,10 +873,10 @@
     ("K3", 0),
     ("K1", 2),
     ("K2", 1),
-    ("K3", 1),
     ("I", 1),
     ("B0", 0),
     ("K2", 2),
+    ("K3", 1),
     ("K4", 0),
     ("F", 0),
     ("I", 2),
@@ -894,11 +915,11 @@
     ("D1", 6),
     ("C1", 0),
     ("B4", 0),
-    ("T", 1),
     ("D2", 4),
     ("R", 2),
     ("D1", 7),
     ("T", 0),
+    ("T", 1),
     ("D3", 3),
     ("D2", 5),
     ("R", 3),
@@ -1018,6 +1039,7 @@
     kvs,
     n1s,
     ga,
+    dq,
     dots,
     bias,
     segk,
@@ -1140,23 +1162,19 @@
             copy.wait()
 
         ga[...] = matmul(gm[...], wout[...], 1, 1).astype(BF)
-        a_out[...] += matmul(att[s], gm[...], 0, 0)
-
         lane = lax.broadcasted_iota(jnp.int32, (1, LOCAL), 1) // HD
         keys = kvs.reshape(3 * GROUP, 2 * LOCAL)
         here_segs = segk.at[:, aligned(at.z * GROUP, 3 * GROUP)]
-        which = lax.broadcasted_iota(jnp.int32, (8, SPAN), 0) == s
         dkvt[...] = jnp.zeros_like(dkvt)
 
-        def block(b, carry):
-            start = pl.multiple_of(b * HALF, HALF)
-            here = pl.ds(start, HALF)
-            span = pl.ds(start, SPAN)
+        def pairs(b, low, size, first):
+            here, span = pl.ds(b * HALF, HALF), pl.ds(low, size)
+            which = lax.broadcasted_iota(jnp.int32, (8, size), 0) == s
             seg_row = jnp.sum(
                 jnp.where(which, here_segs[:, span], 0.0), axis=0, keepdims=True
             )
             logs = lse[s, here]
-            bias[...] = allowed_bias(logs[:, 5:6], seg_row)
+            bias[:, 0:size] = allowed_bias(logs[:, 5:6], seg_row, low - b * HALF, size)
             query = q[s, here]
             grad = ga[here]
             k_block = keys[span, 0:LOCAL]
@@ -1164,37 +1182,48 @@
             dots[0] = jnp.transpose(query)
             dots[1] = jnp.transpose(grad)
             product = grad.astype(F32) * att[s, here].astype(F32)
-            grad_query = jnp.zeros((HALF, LOCAL), F32)
+            grad_query = jnp.zeros((HALF, LOCAL), F32) if first else dq[here]
             for h in range(LOCAL // HD):
                 mine_h = lane == h
                 one = jnp.where(mine_h, query, jnp.zeros_like(query))
                 grad_one = jnp.where(mine_h, grad, jnp.zeros_like(grad))
                 delta = jnp.sum(jnp.where(mine_h, product, 0.0), axis=-1, keepdims=True)
-                scores = matmul(one, k_block, 1, 1) + bias[...]
+                scores = matmul(one, k_block, 1, 1) + bias[:, 0:size]
                 probs = jnp.exp(scores - logs[:, h : h + 1])
                 dprobs = matmul(grad_one, v_block, 1, 1)
                 grad_scores = (probs * (dprobs - delta)).astype(BF)
-                grad_query = jnp.where(mine_h, matmul(grad_scores, k_block, 1, 0), grad_query)
+                part = matmul(grad_scores, k_block, 1, 0)
+                grad_query = jnp.where(mine_h, grad_query + part, grad_query)
                 k_rows = pl.ds(h * HD, HD)
                 v_rows = pl.ds(LOCAL + h * HD, HD)
                 dkvt[k_rows, span] += matmul(dots[0, k_rows], grad_scores, 1, 0)
                 dkvt[v_rows, span] += matmul(dots[1, k_rows], probs.astype(BF), 1, 0)
-            gq[s, here] = (grad_query * 0.125).astype(BF)
-            return carry
-
-        lax.fori_loop(0, 2, block, 0)
+            if first:
+                dq[here] = grad_query
+            else:
+                gq[s, here] = (grad_query * 0.125).astype(BF)
+
+        def turned(i):
+            return jnp.transpose(dkvt[:, i * GROUP : (i + 1) * GROUP].astype(BF))
+
+        pairs(0, 0, GROUP, True)
+        pairs(1, HALF, HALF, True)
+        dfar[s] = turned(0)
+
+        @pl.when(at.z > 1)
+        def _():
+            m1_copy(s).start()
+
+        pairs(0, GROUP, SPAN - GROUP, False)
+        pairs(1, GROUP, SPAN - HALF, False)
+        dnear[s] = turned(1)
+        down[s] = turned(2)
+        a_out[...] += matmul(att[s], gm[...], 0, 0)
 
         @pl.when(s < 3)
         def _():
             for copy in load_copies(s + 1):
                 copy.start()
-
-        for i, target in enumerate((dfar, dnear, down)):
-            target[s] = jnp.transpose(dkvt[:, i * GROUP : (i + 1) * GROUP].astype(BF))
-
-        @pl.when(at.z > 1)
-        def _():
-            m1_copy(s).start()
 
         norm_early(s).wait()
         a_qkv[0] += matmul(n1e[...], gq[s], 0, 0)
@@ -1396,6 +1425,7 @@
             low(3, GROUP, 2 * LOCAL),
             low(GROUP, 1024),
             low(GROUP, LOCAL),
+            pltpu.VMEM((GROUP, LOCAL), F32),
             low(2, LOCAL, HALF),
             pltpu.VMEM((HALF, SPAN), F32),
             pltpu.VMEM((8, 3072), F32),
@@ -1452,6 +1482,140 @@
     )(*args)
 
 
+def finish_kernel(
+    nf,
+    out_in,
+    ig_in,
+    sums,
+    sums_one,
+    s_qkv,
+    s_out,
+    s_fc1,
+    s_fc2,
+    out,
+    loss,
+    ig,
+    g_g1,
+    g_b1,
+    g_qkv,
+    g_qv,
+    g_out,
+    g_bo,
+    g_g2,
+    g_b2,
+    g_fc1,
+    g_up,
+    g_fc2,
+    g_bd,
+    low,
+    wide_qkv,
+    wide_out,
+    wide_fc1,
+    wide_fc2,
+    low_qkv,
+    low_out,
+    low_fc1,
+    low_fc2,
+    in_sems,
+    out_sems,
+):
+    shards = (
+        (s_fc1, low_fc1, wide_fc1, g_fc1),
+        (s_fc2, low_fc2, wide_fc2, g_fc2),
+        (s_qkv, low_qkv, wide_qkv, g_qkv),
+        (s_out, low_out, wide_out, g_out),
+    )
+    inward, outward = [], []
+    for i, (source, kept, widened, target) in enumerate(shards):
+        inward.append(pltpu.make_async_copy(source, kept, in_sems.at[i]))
+        outward.append(pltpu.make_async_copy(widened, target, out_sems.at[i]))
+    for i, (source, target) in enumerate(((out_in, out), (ig_in, ig))):
+        for s in range(SEQS):
+            which = 4 + i * SEQS + s
+            inward.append(
+                pltpu.make_async_copy(source.at[s], low.at[i, s], in_sems.at[which])
+            )
+            outward.append(
+                pltpu.make_async_copy(low.at[i, s], target.at[s], out_sems.at[which])
+            )
+    for copy in inward:
+        copy.start()
+    for i, (_, kept, widened, _) in enumerate(shards):
+        inward[i].wait()
+        widened[...] = kept[...].astype(F32)
+        outward[i].start()
+    for i in range(4, len(inward)):
+        inward[i].wait()
+        outward[i].start()
+    place = lax.axis_index("fsdp")
+    fs = g_g1.shape[0]
+    here = aligned(place * fs, fs)
+    for i, target in enumerate((g_g1, g_b1, g_bd, g_g2, g_b2, g_bo)):
+        target[...] = sums[i : i + 1, here].reshape(fs)
+    scale = 1.0 / (2.0 * D * sums_one[6:7, 0:1])
+    loss[...] = jnp.sum(sums[6:7, :], axis=1, keepdims=True) * scale
+    own = sums[8:16, :]
+    wide = g_up.shape[1]
+    up = pltpu.roll(own, lax.rem(1024 - place * wide, 1024), 1)
+    for i in range(g_up.shape[0]):
+        g_up[i : i + 1, :] = up[0:1, i * nf * wide : i * nf * wide + wide]
+    wide = g_qv.shape[2]
+    qv = pltpu.roll(own, lax.rem(1024 - place * wide, 1024), 1)
+    for i in range(2):
+        for h in range(LOCAL // HD):
+            start = i * LOCAL + h * HD
+            g_qv[i, h : h + 1, :] = qv[1:2, start : start + wide]
+    for copy in outward:
+        copy.wait()
+
+
+def finish_call(nf, *args):
+    anys = pl.BlockSpec(memory_space=pl.ANY)
+    vmem = pl.BlockSpec(memory_space=pltpu.VMEM)
+    shape = jax.ShapeDtypeStruct
+    fs = 1024 // nf
+    block = shape((SEQS, GROUP, 1024), BF)
+    row = shape((fs,), F32)
+    return pl.pallas_call(
+        functools.partial(finish_kernel, nf),
+        out_shape=(
+            block,
+            shape((1, 1), F32),
+            block,
+            row,
+            row,
+            shape((3, fs, LOCAL), F32),
+            shape((2, LOCAL // HD, HD // nf), F32),
+            shape((LOCAL, fs), F32),
+            row,
+            row,
+            row,
+            shape((fs, 1024), F32),
+            shape((4, 256 // nf), F32),
+            shape((1024, fs), F32),
+            row,
+        ),
+        in_specs=[anys, anys, vmem, vmem] + [anys] * 4,
+        out_specs=(anys, vmem, anys, vmem, vmem, anys, vmem, anys)
+        + (vmem, vmem, vmem, anys, vmem, anys, vmem),
+        scratch_shapes=[
+            pltpu.VMEM((2, SEQS, GROUP, 1024), BF),
+            pltpu.VMEM((3, fs, LOCAL), F32),
+            pltpu.VMEM((LOCAL, fs), F32),
+            pltpu.VMEM((fs, 1024), F32),
+            pltpu.VMEM((1024, fs), F32),
+            pltpu.VMEM((3, fs, LOCAL), BF),
+            pltpu.VMEM((LOCAL, fs), BF),
+            pltpu.VMEM((fs, 1024), BF),
+            pltpu.VMEM((1024, fs), BF),
+            pltpu.SemaphoreType.DMA((4 + 2 * SEQS,)),
+            pltpu.SemaphoreType.DMA((4 + 2 * SEQS,)),
+        ],
+        compiler_params=pltpu.CompilerParams(vmem_limit_bytes=63 * 2**20),
+        name="finish",
+    )(*args)
+
+
 def local(
     tokens,
     cotangent,
@@ -1472,7 +1636,6 @@
     b_fc2,
 ):
     nf = lax.axis_size("fsdp")
-    wide = b_out.shape[0]
     front = front_call(
         nf,
         w_qkv,
@@ -1497,31 +1660,10 @@
     input_grad, everything, s_qkv, s_out, s_fc1, s_fc2 = back_call(
         nf, grad_mix, grad_middle, gfc1, gfc2, att, q, kv, lse, n1, tokens, wqkv, wout, segment_ids, sums_one
     )
-    place_f = lax.axis_index("fsdp")
-    loss = jnp.sum(everything[6]) / (2.0 * D * sums_one[6, 0])
-    ours = everything[8:10]
-    part = lax.dynamic_slice_in_dim(everything[0:7], place_f * wide, wide, 1)
-    grad_up = ours[0].reshape(b_fc1.shape[0], -1)
-    grad_up = lax.dynamic_slice_in_dim(grad_up, place_f * b_fc1.shape[1], b_fc1.shape[1], 1)
-    grad_qv = ours[1, : 2 * LOCAL].reshape(2, LOCAL // HD, HD)
-    grad_qv = lax.dynamic_slice_in_dim(grad_qv, place_f * b_qv.shape[2], b_qv.shape[2], 2)
-    return (
-        output,
-        loss,
-        input_grad,
-        part[0],
-        part[1],
-        s_qkv.astype(F32),
-        grad_qv,
-        s_out.astype(F32),
-        part[5],
-        part[3],
-        part[4],
-        s_fc1.astype(F32),
-        grad_up,
-        s_fc2.astype(F32),
-        part[2],
+    results = finish_call(
+        nf, output, input_grad, everything, sums_one, s_qkv, s_out, s_fc1, s_fc2
     )
+    return (results[0], results[1].reshape(()), *results[2:])
 
 
 def solution(mesh):

time: 445 us -> 421 us (0.946)
  local copies, waits for them, and re-layouts: 11.5 us -> 0 us
  other arithmetic: 10.1 us -> 0 us
    pallas_call x1, Pallas kernels: 208 us -> 196 us  [back_call(): pl.pallas_call(functools.partial(back_kernel, nf), out_shape=(shape((SEQS...]
    pallas_call x0 -> x1, Pallas kernels: none -> 11.3 us  [finish_call(): pl.pallas_call(functools.partial(finish_kernel, nf), out_shape=(block, sh...]
    convert_element_type x4 -> x0, other arithmetic: 8.61 us -> none  [the longest x1 2.79 us: local(): s_fc1.astype(F32)]
    unnamed x6 -> x0, local copies, waits for them, and re-layouts: 6.84 us -> none
where the time goes in v5:
time: 421 us
  Pallas kernels  420 us (100%)
    pallas_call x1, Pallas kernels, front_call(): pl.pallas_call(functools.partial(front_kernel, nf), out_shape=(shape((SEQ...  212 us
    pallas_call x1, Pallas kernels, back_call(): pl.pallas_call(functools.partial(back_kernel, nf), out_shape=(shape((SEQS...  196 us
    pallas_call x1, Pallas kernels, finish_call(): pl.pallas_call(functools.partial(finish_kernel, nf), out_shape=(block, sh...  11.3 us

profile of v5, /device:TPU:0, one launch (start us, length us, event | category | flops | bytes accessed | tf_op | source)
XLA Modules:
  0.0 420.5 jit_solution(11988514169412318546)
XLA Ops:
  0.7 212.2 %front.1 = (bf16[4,512,1024]{2,1,0:T(8,128)(2,1)}, bf16[4,512,1024]{2,1,0:T(8,128)(2,1)}, f32[4,128,1024]{2,1,0:T(8,128)}, bf16[1024,1024]{1,0:T(8,128)(2,1)}, b...) custom-call(bf16[3,512,256]{2,1,0:T(8,128)(2,1)} %wqkv_s.1, ...), custom_call_target="tpu_custom_call" | custom-call | flops 38654705664 | bytes 31457280 | tf_op jit(solution)/shard_map/front/pallas_call | solution.py:721
  212.8 196.2 %back.1 = (bf16[4,512,1024]{2,1,0:T(8,128)(2,1)}, f32[16,1024]{1,0:T(8,128)}, bf16[3,512,256]{2,1,0:T(8,128)(2,1)}, bf16[256,512]{1,0:T(8,128)(2,1)}, bf16[512,1...) custom-call(bf16[4,512,1024]{2,1,0:T(8,128)(2,1)} %get-tuple-element.50.gmix_h, f32[4,128,1024]{2,1,0:T(8,128)} %get-tuple-element.51.gmid_h, ...), custom_call_target="tpu_custom_call" | custom-call | flops 25769803776 | bytes 31457280 | tf_op jit(solution)/shard_map/back/pallas_call | solution.py:1411
  409.1 11.3 %finish.1 = (bf16[4,512,1024]{2,1,0:T(8,128)(2,1)}, f32[1,1]{1,0:T(1,128)}, bf16[4,512,1024]{2,1,0:T(8,128)(2,1)}, f32[512]{0:T(512)}, f32[512]{0:T(512)}, /*ind...) custom-call(bf16[4,512,1024]{2,1,0:T(8,128)(2,1)} %get-tuple-element, ...), custom_call_target="tpu_custom_call" | custom-call | tf_op jit(solution)/shard_map/finish/pallas_call | solution.py:1579

commit v6 on v5

--- a/solution.py
+++ b/solution.py
@@ -231,7 +231,6 @@
     ("gup", 0),
     ("R2", 3),
     ("T2", 2),
-    ("T2", 3),
 )
 
 
@@ -537,7 +536,14 @@
             small[3:4, :] += column_sum(grad)
             tok_q[s] = grad.astype(BF)
             mix_copy(s).start()
-        ring.spread(*ends(k, s), s)
+        if k < 2:
+            ring.spread(*ends(k, s), s)
+        else:
+
+            @pl.when(s < SEQS - 1)
+            def _():
+                ring.spread(*ends(k, s), s)
+
 
     def halo(s):
         for half in range(2):
@@ -702,7 +708,8 @@
     for copy in kept:
         copy.start()
     for s in range(SEQS):
-        ring.step_u(*ends(2, s), s)
+        if s < SEQS - 1:
+            ring.step_u(*ends(2, s), s)
         mix_copy(s).wait()
         kv_out(s).wait()
     last.wait()
@@ -861,6 +868,7 @@
     ("K0", 0),
     ("E", 0),
     ("E", 1),
+    ("L", 0),
     ("K1", 0),
     ("K0", 1),
     ("K0", 2),
@@ -1036,6 +1044,7 @@
     s_fc1,
     s_fc2,
     gm,
+    gm_last,
     kvs,
     n1s,
     ga,
@@ -1071,6 +1080,7 @@
     k_out,
     ring_sems,
     load_sems,
+    last_sem,
     first_sems,
     m1_sems,
     m2_sems,
@@ -1124,11 +1134,22 @@
     def first_copy(i):
         return pltpu.make_async_copy(firsts[i][0], firsts[i][1], first_sems.at[i])
 
-    def load_copies(s):
-        return (
-            pltpu.make_async_copy(gmix_h.at[s], gm, load_sems.at[0, 0]),
-            pltpu.make_async_copy(kv_h.at[s], kvs, load_sems.at[1, 0]),
-        )
+    def mix_load(s):
+        return pltpu.make_async_copy(gmix_h.at[s], gm, load_sems.at[0, 0])
+
+    def kv_load(s):
+        return pltpu.make_async_copy(kv_h.at[s], kvs, load_sems.at[1, 0])
+
+    last = SEQS - 1
+    over = aligned(at.over_y, QUARTER)
+    last_own = pltpu.make_async_copy(gmix_h.at[last, mine], gm_last.at[mine], last_sem)
+    last_y = remote(gmix_h.at[last, mine], gm_last.at[mine], ring.pair(2, last), at.mate_y)
+    last_c = remote(gmix_h.at[last, mine], gm_last.at[mine], ring.pair(3, last), at.mate_c)
+    last_over = remote(gm_last.at[over], gm_last.at[over], ring.pair(4, last), at.mate_c)
+
+    def step_last(s):
+        last_y.wait()
+        last_over.start()
 
     def norm_load(s):
         return pltpu.make_async_copy(n1_h.at[s], n1s, load_sems.at[2, 0])
@@ -1139,7 +1160,9 @@
     def mid_load(s):
         return pltpu.make_async_copy(gmid_h.at[s], gmid, load_sems.at[2, 1])
 
-    for copy in load_copies(0):
+    mix_load(0).start()
+    kv_load(0).start()
+    for copy in (last_own, last_y, last_c):
         copy.start()
     for i in range(4):
         first_copy(i).start()
@@ -1152,14 +1175,23 @@
     a_qkv[...] = jnp.zeros_like(a_qkv)
     a_out[...] = jnp.zeros_like(a_out)
     def m1_copy(s):
-        return remote(dfar.at[s], m1.at[s], (m1_sems.at[0, s], m1_sems.at[1, s]), at.down)
+        return remote(dfar.at[lax.rem(s, 2)], m1.at[s], (m1_sems.at[0, s], m1_sems.at[1, s]), at.down)
 
     def m2_copy(s):
         return remote(dnear.at[s], m2.at[s], (m2_sems.at[0, s], m2_sems.at[1, s]), at.down)
 
     def step_e(s):
-        for copy in load_copies(s):
-            copy.wait()
+        kv_load(s).wait()
+
+        @pl.when(s < last)
+        def _():
+            mix_load(s).wait()
+
+        @pl.when(s == last)
+        def _():
+            for copy in (last_own, last_c, last_over):
+                copy.wait()
+            gm[...] = gm_last[...]
 
         ga[...] = matmul(gm[...], wout[...], 1, 1).astype(BF)
         lane = lax.broadcasted_iota(jnp.int32, (1, LOCAL), 1) // HD
@@ -1208,7 +1240,12 @@
 
         pairs(0, 0, GROUP, True)
         pairs(1, HALF, HALF, True)
-        dfar[s] = turned(0)
+
+        @pl.when((at.z > 1) & (s > 1))
+        def _():
+            m1_copy(s - 2).wait_send()
+
+        dfar[lax.rem(s, 2)] = turned(0)
 
         @pl.when(at.z > 1)
         def _():
@@ -1220,10 +1257,13 @@
         down[s] = turned(2)
         a_out[...] += matmul(att[s], gm[...], 0, 0)
 
-        @pl.when(s < 3)
-        def _():
-            for copy in load_copies(s + 1):
-                copy.start()
+        @pl.when(s < last)
+        def _():
+            kv_load(s + 1).start()
+
+        @pl.when(s < last - 1)
+        def _():
+            mix_load(s + 1).start()
 
         norm_early(s).wait()
         a_qkv[0] += matmul(n1e[...], gq[s], 0, 0)
@@ -1349,6 +1389,7 @@
     chains = (red_fc2, red_fc1)
     actions = {
         "E": step_e,
+        "L": step_last,
         "I": step_i,
         "F": step_f,
         "Q": ring.step_q,
@@ -1391,9 +1432,11 @@
         ring.step_u(*ends(s), s)
         ig_copy(s).wait()
 
-        @pl.when(at.z > 1)
-        def _():
-            m1_copy(s).wait_send()
+        if s > 1:
+
+            @pl.when(at.z > 1)
+            def _():
+                m1_copy(s).wait_send()
 
         @pl.when(at.z > 0)
         def _():
@@ -1422,6 +1465,7 @@
         out_specs=(anys, vmem, vmem, vmem, vmem, vmem),
         scratch_shapes=[
             low(GROUP, 1024),
+            low(GROUP, 1024),
             low(3, GROUP, 2 * LOCAL),
             low(GROUP, 1024),
             low(GROUP, LOCAL),
@@ -1430,7 +1474,7 @@
             pltpu.VMEM((HALF, SPAN), F32),
             pltpu.VMEM((8, 3072), F32),
             pltpu.VMEM((2 * LOCAL, 3 * GROUP), F32),
-            low(SEQS, GROUP, 2 * LOCAL),
+            low(2, GROUP, 2 * LOCAL),
             low(SEQS, GROUP, 2 * LOCAL),
             low(SEQS, GROUP, 2 * LOCAL),
             low(SEQS, GROUP, 2 * LOCAL),
@@ -1457,6 +1501,7 @@
             low(LOCAL // 4, fs),
             dma((5, 2, SEQS)),
             dma((3, 2)),
+            dma,
             dma((4,)),
             dma((2, SEQS)),
             dma((2, SEQS)),

time: 421 us -> 415 us (0.986)
  Pallas kernels: 420 us -> 414 us
    pallas_call x1, Pallas kernels: 212 us -> 207 us  [front_call(): pl.pallas_call(functools.partial(front_kernel, nf), out_shape=(shape((SEQ...]
where the time goes in v6:
time: 415 us
  Pallas kernels  414 us (100%)
    pallas_call x1, Pallas kernels, front_call(): pl.pallas_call(functools.partial(front_kernel, nf), out_shape=(shape((SEQ...  207 us
    pallas_call x1, Pallas kernels, back_call(): pl.pallas_call(functools.partial(back_kernel, nf), out_shape=(shape((SEQS...  196 us
    pallas_call x1, Pallas kernels, finish_call(): pl.pallas_call(functools.partial(finish_kernel, nf), out_shape=(block, sh...  11.3 us

profile of v6, /device:TPU:0, one launch (start us, length us, event | category | flops | bytes accessed | tf_op | source)
XLA Modules:
  0.0 414.5 jit_solution(14224524325708105769)
XLA Ops:
  0.7 206.6 %front.1 = (bf16[4,512,1024]{2,1,0:T(8,128)(2,1)}, bf16[4,512,1024]{2,1,0:T(8,128)(2,1)}, f32[4,128,1024]{2,1,0:T(8,128)}, bf16[1024,1024]{1,0:T(8,128)(2,1)}, b...) custom-call(bf16[3,512,256]{2,1,0:T(8,128)(2,1)} %wqkv_s.1, ...), custom_call_target="tpu_custom_call" | custom-call | flops 38654705664 | bytes 31457280 | tf_op jit(solution)/shard_map/front/pallas_call | solution.py:728
  207.2 195.8 %back.1 = (bf16[4,512,1024]{2,1,0:T(8,128)(2,1)}, f32[16,1024]{1,0:T(8,128)}, bf16[3,512,256]{2,1,0:T(8,128)(2,1)}, bf16[256,512]{1,0:T(8,128)(2,1)}, bf16[512,1...) custom-call(bf16[4,512,1024]{2,1,0:T(8,128)(2,1)} %get-tuple-element.50.gmix_h, f32[4,128,1024]{2,1,0:T(8,128)} %get-tuple-element.51.gmid_h, ...), custom_call_target="tpu_custom_call" | custom-call | flops 25769803776 | bytes 31457280 | tf_op jit(solution)/shard_map/back/pallas_call | solution.py:1454
  403.0 11.3 %finish.1 = (bf16[4,512,1024]{2,1,0:T(8,128)(2,1)}, f32[1,1]{1,0:T(1,128)}, bf16[4,512,1024]{2,1,0:T(8,128)(2,1)}, f32[512]{0:T(512)}, f32[512]{0:T(512)}, /*ind...) custom-call(bf16[4,512,1024]{2,1,0:T(8,128)(2,1)} %get-tuple-element, ...), custom_call_target="tpu_custom_call" | custom-call | tf_op jit(solution)/shard_map/finish/pallas_call | solution.py:1624

commit v7 on v6

--- a/solution.py
+++ b/solution.py
@@ -259,10 +259,10 @@
     gfc1,
     gfc2,
     small,
-    att,
-    q,
+    att_h,
+    q_h,
     kv_h,
-    lse,
+    lse_h,
     n1_h,
     wqkv_h,
     wout_h,
@@ -307,6 +307,11 @@
     vec_own,
     vec_got,
     v_sems,
+    att,
+    q,
+    lse,
+    head_sems,
+    mid_sems,
 ):
     at = Place(nf)
     at.barrier()
@@ -501,6 +506,16 @@
 
     def kv_out(s):
         return pltpu.make_async_copy(kv.at[s], kv_h.at[s], res_sem.at[s])
+
+    def head_copies(s):
+        pairs = ((att, att_h), (q, q_h), (lse, lse_h))
+        return [
+            pltpu.make_async_copy(source.at[s], target.at[s], head_sems.at[i, s])
+            for i, (source, target) in enumerate(pairs)
+        ]
+
+    def mid_copy(s):
+        return pltpu.make_async_copy(gblk.at[s], gmid_h.at[s], mid_sems.at[s])
 
     def mix_copy(s):
         return pltpu.make_async_copy(tok_q.at[s], gmix_h.at[s, mine], mix_sem.at[s])
@@ -533,6 +548,7 @@
             small[2:3, :] += column_sum(summed)
             grad = gblk[s] + norm_back(summed, xhat, inverse, vec[1:2, :])
             gblk[s] = grad
+            mid_copy(s).start()
             small[3:4, :] += column_sum(grad)
             tok_q[s] = grad.astype(BF)
             mix_copy(s).start()
@@ -611,6 +627,8 @@
             return carry
 
         lax.fori_loop(0, 2, block, 0)
+        for copy in head_copies(s):
+            copy.start()
         send[s] = matmul(att[s], wout[...], 1, 0).astype(BF)
         ring.rs_core(s).start()
 
@@ -696,23 +714,28 @@
     for k in range(3):
         actions[f"R{k}"] = functools.partial(step_r, k)
         actions[f"T{k}"] = lambda s, k=k: ring.step_t(*ends(k, s), s)
-    actions["W"] = lambda s: None
-    actions["V"] = lambda s: [weight_wait(i) for i in (4, 1)]
-    run_order(actions, FRONT_ORDER)
-    last = pltpu.make_async_copy(gblk, gmid_h, out_sem)
-    last.start()
     kept = (
         pltpu.make_async_copy(wqkv, wqkv_h, keep_sem.at[0]),
         pltpu.make_async_copy(wout, wout_h, keep_sem.at[1]),
     )
-    for copy in kept:
-        copy.start()
+
+    def step_weights(s):
+        for i in (4, 1):
+            weight_wait(i)
+        for copy in kept:
+            copy.start()
+
+    actions["W"] = lambda s: None
+    actions["V"] = step_weights
+    run_order(actions, FRONT_ORDER)
     for s in range(SEQS):
         if s < SEQS - 1:
             ring.step_u(*ends(2, s), s)
         mix_copy(s).wait()
         kv_out(s).wait()
-    last.wait()
+        mid_copy(s).wait()
+        for copy in head_copies(s):
+            copy.wait()
     down_out().wait()
     up_out().wait()
     for copy in kept:
@@ -743,7 +766,7 @@
             shape((LOCAL, 1024), BF),
         ),
         in_specs=[anys] * 7 + [vmem] * 10,
-        out_specs=(anys, anys, anys, anys, anys, vmem, vmem, vmem, anys, vmem, anys, anys, anys),
+        out_specs=(anys, anys, anys, anys, anys, vmem, anys, anys, anys, anys, anys, anys, anys),
         scratch_shapes=[
             pltpu.VMEM((3, 1024, LOCAL), BF),
             pltpu.VMEM((LOCAL, 1024), BF),
@@ -786,6 +809,11 @@
             pltpu.VMEM((8, 1024), F32),
             pltpu.VMEM((nf - 1, 8, 1024), F32),
             dma((2, nf - 1)),
+            pltpu.VMEM((SEQS, GROUP, LOCAL), BF),
+            pltpu.VMEM((SEQS, GROUP, LOCAL), BF),
+            pltpu.VMEM((SEQS, GROUP, 128), F32),
+            dma((3, SEQS)),
+            dma((SEQS,)),
         ],
         compiler_params=pltpu.CompilerParams(
             collective_id=1, has_side_effects=True, vmem_limit_bytes=63 * 2**20
@@ -1027,13 +1055,13 @@
     gmid_h,
     gfc1_h,
     gfc2_h,
-    att,
-    q,
+    att_h,
+    q_h,
     kv_h,
-    lse,
+    lse_h,
     n1_h,
     tokens,
-    wqkv,
+    wqkv_h,
     wout,
     segs,
     sums_one,
@@ -1095,9 +1123,14 @@
     sum_sems,
     sum_f_sems,
     n1e,
+    att,
+    q,
+    lse,
+    wqkv,
+    head_sems,
+    w_sem,
 ):
     at = Place(nf)
-    at.barrier()
     ring = Ring(at, send, recv_c, send_y, recv_y, ring_sems)
     mine = aligned(at.mine, QUARTER)
     rows_cut = lambda ref, where: ref.at[where, :]
@@ -1160,10 +1193,25 @@
     def mid_load(s):
         return pltpu.make_async_copy(gmid_h.at[s], gmid, load_sems.at[2, 1])
 
+    def head_loads(s):
+        pairs = ((att_h, att), (q_h, q), (lse_h, lse))
+        return [
+            pltpu.make_async_copy(source.at[s], target.at[s], head_sems.at[i, s])
+            for i, (source, target) in enumerate(pairs)
+        ]
+
+    w_load = pltpu.make_async_copy(wqkv_h, wqkv, w_sem)
     mix_load(0).start()
     kv_load(0).start()
+    for copy in head_loads(0):
+        copy.start()
+    at.barrier()
     for copy in (last_own, last_y, last_c):
         copy.start()
+    for s in range(1, SEQS):
+        for copy in head_loads(s):
+            copy.start()
+    w_load.start()
     for i in range(4):
         first_copy(i).start()
     norm_load(0).start()
@@ -1172,8 +1220,6 @@
     segk[...] = jnp.full(segk.shape, -1.0, F32)
     segk[0:4, 1024:3072] = segs[...].astype(F32)
     small[...] = jnp.zeros_like(small)
-    a_qkv[...] = jnp.zeros_like(a_qkv)
-    a_out[...] = jnp.zeros_like(a_out)
     def m1_copy(s):
         return remote(dfar.at[lax.rem(s, 2)], m1.at[s], (m1_sems.at[0, s], m1_sems.at[1, s]), at.down)
 
@@ -1182,6 +1228,8 @@
 
     def step_e(s):
         kv_load(s).wait()
+        for copy in head_loads(s):
+            copy.wait()
 
         @pl.when(s < last)
         def _():
@@ -1251,6 +1299,11 @@
         def _():
             m1_copy(s).start()
 
+        @pl.when(s == 0)
+        def _():
+            a_qkv[...] = jnp.zeros_like(a_qkv)
+            a_out[...] = jnp.zeros_like(a_out)
+
         pairs(0, GROUP, SPAN - GROUP, False)
         pairs(1, GROUP, SPAN - HALF, False)
         dnear[s] = turned(1)
@@ -1289,6 +1342,10 @@
             down[s] = (down[s].astype(F32) + m2[s].astype(F32)).astype(BF)
 
         norm_load(s).wait()
+        @pl.when(s == 0)
+        def _():
+            w_load.wait()
+
         grads = (gq[s], down[s, :, 0:LOCAL], down[s, :, LOCAL:])
         send[s] = (
             matmul(grads[0], wqkv[0], 1, 1)
@@ -1461,7 +1518,7 @@
             shape((fs, 1024), BF),
             shape((1024, fs), BF),
         ),
-        in_specs=[anys] * 4 + [vmem, vmem, anys, vmem, anys, anys, vmem, vmem, vmem, vmem],
+        in_specs=[anys] * 11 + [vmem, vmem, vmem],
         out_specs=(anys, vmem, vmem, vmem, vmem, vmem),
         scratch_shapes=[
             low(GROUP, 1024),
@@ -1516,6 +1573,12 @@
             dma((2, 5)),
             dma((2, nf - 1)),
             low(GROUP, 1024),
+            low(SEQS, GROUP, LOCAL),
+            low(SEQS, GROUP, LOCAL),
+            pltpu.VMEM((SEQS, GROUP, 128), F32),
+            low(3, 1024, LOCAL),
+            dma((3, SEQS)),
+            dma,
         ],
         compiler_params=pltpu.CompilerParams(
             collective_id=2, has_side_effects=True, vmem_limit_bytes=63 * 2**20

time: 415 us -> 414 us (level)
  no operation moved by 1% of the time
where the time goes in v7:
time: 414 us
  Pallas kernels  413 us (100%)
    pallas_call x1, Pallas kernels, front_call(): pl.pallas_call(functools.partial(front_kernel, nf), out_shape=(shape((SEQ...  205 us
    pallas_call x1, Pallas kernels, back_call(): pl.pallas_call(functools.partial(back_kernel, nf), out_shape=(shape((SEQS...  196 us
    pallas_call x1, Pallas kernels, finish_call(): pl.pallas_call(functools.partial(finish_kernel, nf), out_shape=(block, sh...  11.3 us

profile of v7, /device:TPU:0, one launch (start us, length us, event | category | flops | bytes accessed | tf_op | source)
XLA Modules:
  0.0 413.5 jit_solution(6492246356205114339)
XLA Ops:
  0.7 205.2 %front.1 = (bf16[4,512,1024]{2,1,0:T(8,128)(2,1)}, bf16[4,512,1024]{2,1,0:T(8,128)(2,1)}, f32[4,128,1024]{2,1,0:T(8,128)}, bf16[1024,1024]{1,0:T(8,128)(2,1)}, b...) custom-call(bf16[3,512,256]{2,1,0:T(8,128)(2,1)} %wqkv_s.1, ...), custom_call_target="tpu_custom_call" | custom-call | flops 38654705664 | bytes 31457280 | tf_op jit(solution)/shard_map/front/pallas_call | solution.py:751
  205.9 196.2 %back.1 = (bf16[4,512,1024]{2,1,0:T(8,128)(2,1)}, f32[16,1024]{1,0:T(8,128)}, bf16[3,512,256]{2,1,0:T(8,128)(2,1)}, bf16[256,512]{1,0:T(8,128)(2,1)}, bf16[512,1...) custom-call(bf16[4,512,1024]{2,1,0:T(8,128)(2,1)} %get-tuple-element.50.gmix_h, f32[4,128,1024]{2,1,0:T(8,128)} %get-tuple-element.51.gmid_h, ...), custom_call_target="tpu_custom_call" | custom-call | flops 25769803776 | bytes 31457280 | tf_op jit(solution)/shard_map/back/pallas_call | solution.py:1511
  402.1 11.3 %finish.1 = (bf16[4,512,1024]{2,1,0:T(8,128)(2,1)}, f32[1,1]{1,0:T(1,128)}, bf16[4,512,1024]{2,1,0:T(8,128)(2,1)}, f32[512]{0:T(512)}, f32[512]{0:T(512)}, /*ind...) custom-call(bf16[4,512,1024]{2,1,0:T(8,128)(2,1)} %get-tuple-element, ...), custom_call_target="tpu_custom_call" | custom-call | tf_op jit(solution)/shard_map/finish/pallas_call | solution.py:1687

commit v8 on v7

--- a/solution.py
+++ b/solution.py
@@ -893,93 +893,93 @@
 
 
 BACK_ORDER = (
+    ("E", 0),
     ("K0", 0),
-    ("E", 0),
+    ("K0", 1),
+    ("K0", 2),
     ("E", 1),
     ("L", 0),
+    ("E", 2),
+    ("I", 0),
     ("K1", 0),
-    ("K0", 1),
-    ("K0", 2),
-    ("I", 0),
-    ("E", 2),
+    ("K1", 1),
+    ("I", 1),
+    ("K0", 3),
     ("K2", 0),
-    ("K1", 1),
     ("E", 3),
-    ("K0", 3),
     ("K3", 0),
     ("K1", 2),
     ("K2", 1),
-    ("I", 1),
-    ("B0", 0),
-    ("K2", 2),
-    ("K3", 1),
+    ("I", 2),
     ("K4", 0),
     ("F", 0),
-    ("I", 2),
+    ("K1", 3),
+    ("I", 3),
+    ("K3", 1),
+    ("K2", 2),
+    ("Q", 0),
+    ("F", 1),
+    ("B0", 0),
     ("K4", 1),
+    ("K2", 3),
+    ("Q", 1),
     ("D1", 0),
-    ("I", 3),
-    ("F", 1),
-    ("D2", 0),
-    ("Q", 1),
-    ("K1", 3),
-    ("Q", 0),
+    ("R", 0),
+    ("F", 2),
+    ("D1", 1),
     ("K3", 2),
-    ("D1", 1),
     ("B1", 0),
-    ("F", 2),
-    ("D1", 3),
-    ("D1", 2),
-    ("K2", 3),
-    ("K3", 3),
     ("F", 3),
     ("Q", 2),
+    ("K3", 3),
+    ("D1", 2),
+    ("C0", 0),
     ("D2", 1),
-    ("C0", 0),
+    ("D1", 3),
     ("B2", 0),
-    ("R", 0),
-    ("D2", 3),
+    ("D2", 0),
+    ("Q", 3),
+    ("K4", 2),
+    ("C1", 0),
     ("R", 1),
+    ("D1", 4),
+    ("R", 2),
     ("D2", 2),
     ("B3", 0),
-    ("Q", 3),
-    ("K4", 2),
-    ("D1", 4),
+    ("D3", 1),
+    ("D2", 3),
+    ("R", 3),
+    ("S0", 0),
+    ("D3", 0),
+    ("C2", 0),
     ("K4", 3),
     ("D1", 5),
-    ("D3", 0),
+    ("T", 2),
+    ("D2", 4),
+    ("S1", 0),
+    ("S2", 0),
+    ("D3", 3),
+    ("C3", 0),
+    ("B4", 0),
+    ("D3", 4),
+    ("S3", 0),
+    ("D1", 7),
+    ("D3", 2),
+    ("D2", 5),
     ("D1", 6),
-    ("C1", 0),
-    ("B4", 0),
-    ("D2", 4),
-    ("R", 2),
-    ("D1", 7),
+    ("C4", 0),
+    ("D2", 7),
+    ("T", 3),
+    ("D2", 6),
+    ("S4", 0),
+    ("B5", 0),
+    ("D3", 7),
     ("T", 0),
+    ("D3", 5),
+    ("C5", 0),
     ("T", 1),
-    ("D3", 3),
-    ("D2", 5),
-    ("R", 3),
-    ("S0", 0),
-    ("S1", 0),
-    ("D2", 6),
-    ("S2", 0),
-    ("D3", 2),
-    ("C2", 0),
-    ("C3", 0),
+    ("S5", 0),
     ("D3", 6),
-    ("T", 3),
-    ("D2", 7),
-    ("S3", 0),
-    ("D3", 5),
-    ("C4", 0),
-    ("D3", 7),
-    ("T", 2),
-    ("S4", 0),
-    ("D3", 1),
-    ("B5", 0),
-    ("D3", 4),
-    ("S5", 0),
-    ("C5", 0),
 )
 
 

time: 414 us -> 413 us (level)
  no operation moved by 1% of the time
where the time goes in v8:
time: 413 us; the launch traced here: 412 us
  Pallas kernels  412 us (100%)
    pallas_call x1, Pallas kernels, front_call(): pl.pallas_call(functools.partial(front_kernel, nf), out_shape=(shape((SEQ...  205 us
    pallas_call x1, Pallas kernels, back_call(): pl.pallas_call(functools.partial(back_kernel, nf), out_shape=(shape((SEQS...  195 us
    pallas_call x1, Pallas kernels, finish_call(): pl.pallas_call(functools.partial(finish_kernel, nf), out_shape=(block, sh...  11.3 us

profile of v8, /device:TPU:0, one launch (start us, length us, event | category | flops | bytes accessed | tf_op | source)
XLA Modules:
  0.0 412.5 jit_solution(9974029138050544062)
XLA Ops:
  0.7 205.2 %front.1 = (bf16[4,512,1024]{2,1,0:T(8,128)(2,1)}, bf16[4,512,1024]{2,1,0:T(8,128)(2,1)}, f32[4,128,1024]{2,1,0:T(8,128)}, bf16[1024,1024]{1,0:T(8,128)(2,1)}, b...) custom-call(bf16[3,512,256]{2,1,0:T(8,128)(2,1)} %wqkv_s.1, ...), custom_call_target="tpu_custom_call" | custom-call | flops 38654705664 | bytes 31457280 | tf_op jit(solution)/shard_map/front/pallas_call | solution.py:751
  205.9 195.1 %back.1 = (bf16[4,512,1024]{2,1,0:T(8,128)(2,1)}, f32[16,1024]{1,0:T(8,128)}, bf16[3,512,256]{2,1,0:T(8,128)(2,1)}, bf16[256,512]{1,0:T(8,128)(2,1)}, bf16[512,1...) custom-call(bf16[4,512,1024]{2,1,0:T(8,128)(2,1)} %get-tuple-element.50.gmix_h, f32[4,128,1024]{2,1,0:T(8,128)} %get-tuple-element.51.gmid_h, ...), custom_call_target="tpu_custom_call" | custom-call | flops 25769803776 | bytes 31457280 | tf_op jit(solution)/shard_map/back/pallas_call | solution.py:1511
  401.0 11.3 %finish.1 = (bf16[4,512,1024]{2,1,0:T(8,128)(2,1)}, f32[1,1]{1,0:T(1,128)}, bf16[4,512,1024]{2,1,0:T(8,128)(2,1)}, f32[512]{0:T(512)}, f32[512]{0:T(512)}, /*ind...) custom-call(bf16[4,512,1024]{2,1,0:T(8,128)(2,1)} %get-tuple-element, ...), custom_call_target="tpu_custom_call" | custom-call | tf_op jit(solution)/shard_map/finish/pallas_call | solution.py:1687

commit v9 on v8

--- a/solution.py
+++ b/solution.py
@@ -224,13 +224,13 @@
     ("P2", 3),
     ("R2", 0),
     ("Q", 3),
+    ("R2", 2),
     ("gdown", 0),
     ("T2", 0),
-    ("R2", 2),
     ("T2", 1),
     ("gup", 0),
+    ("T2", 2),
     ("R2", 3),
-    ("T2", 2),
 )
 
 

time: 413 us -> 413 us (level)
  no operation moved by 1% of the time
where the time goes in v9:
time: 413 us; the launch traced here: 412 us
  Pallas kernels  412 us (100%)
    pallas_call x1, Pallas kernels, front_call(): pl.pallas_call(functools.partial(front_kernel, nf), out_shape=(shape((SEQ...  205 us
    pallas_call x1, Pallas kernels, back_call(): pl.pallas_call(functools.partial(back_kernel, nf), out_shape=(shape((SEQS...  195 us
    pallas_call x1, Pallas kernels, finish_call(): pl.pallas_call(functools.partial(finish_kernel, nf), out_shape=(block, sh...  11.3 us

profile of v9, /device:TPU:0, one launch (start us, length us, event | category | flops | bytes accessed | tf_op | source)
XLA Modules:
  0.0 412.5 jit_solution(1837249634348362418)
XLA Ops:
  0.7 205.2 %front.1 = (bf16[4,512,1024]{2,1,0:T(8,128)(2,1)}, bf16[4,512,1024]{2,1,0:T(8,128)(2,1)}, f32[4,128,1024]{2,1,0:T(8,128)}, bf16[1024,1024]{1,0:T(8,128)(2,1)}, b...) custom-call(bf16[3,512,256]{2,1,0:T(8,128)(2,1)} %wqkv_s.1, ...), custom_call_target="tpu_custom_call" | custom-call | flops 38654705664 | bytes 31457280 | tf_op jit(solution)/shard_map/front/pallas_call | solution.py:751
  205.9 195.1 %back.1 = (bf16[4,512,1024]{2,1,0:T(8,128)(2,1)}, f32[16,1024]{1,0:T(8,128)}, bf16[3,512,256]{2,1,0:T(8,128)(2,1)}, bf16[256,512]{1,0:T(8,128)(2,1)}, bf16[512,1...) custom-call(bf16[4,512,1024]{2,1,0:T(8,128)(2,1)} %get-tuple-element.50.gmix_h, f32[4,128,1024]{2,1,0:T(8,128)} %get-tuple-element.51.gmid_h, ...), custom_call_target="tpu_custom_call" | custom-call | flops 25769803776 | bytes 31457280 | tf_op jit(solution)/shard_map/back/pallas_call | solution.py:1511
  401.0 11.3 %finish.1 = (bf16[4,512,1024]{2,1,0:T(8,128)(2,1)}, f32[1,1]{1,0:T(1,128)}, bf16[4,512,1024]{2,1,0:T(8,128)(2,1)}, f32[512]{0:T(512)}, f32[512]{0:T(512)}, /*ind...) custom-call(bf16[4,512,1024]{2,1,0:T(8,128)(2,1)} %get-tuple-element, ...), custom_call_target="tpu_custom_call" | custom-call | tf_op jit(solution)/shard_map/finish/pallas_call | solution.py:1687
